TPU v7x, 512 devices: a whole 4x4x16 slice. The times are simulated.
512 devices in a mesh: dp: 16 (over z), mem: 32 (over x, y, core).
Axes of the slice: x: 4, y: 4, z: 16, core: 2. Of those that a mesh axis runs over, the one named last changes fastest.
Arguments:
- owners: int32 [65536, 3], P(('dp', 'mem')), may hold values from 0 to 31, as said below
- pick_index: int32 [65536, 32], P(('dp', 'mem')), may hold values from 0 to 95, as said below
- key_scores: float32 [65536, 32], P(('dp', 'mem')), may hold values from -12 to 320
- output_cotangent: bfloat16 [65536, 4096], P(('dp', 'mem')), may hold values from -0.5 to 0.5
- value_table: bfloat16 [1024, 4096], P('mem'), may hold values from -14 to 14
- first_moment: float32 [1024, 4096], P('mem'), may hold values from -3 to 3
- second_moment: float32 [1024, 4096], P('mem'), may hold values from 0.5 to 8
- norm_gain: float32 [4096], replicated, may hold values from 0.5 to 1.5
Outputs:
- memory_out: bfloat16 [65536, 4096], P(('dp', 'mem'))
- score_gradient: float32 [65536, 32], P(('dp', 'mem'))
- gain_gradient: float32 [4096], replicated
- updated_table: bfloat16 [1024, 4096], P('mem')
- updated_first: float32 [1024, 4096], P('mem')
- updated_second: float32 [1024, 4096], P('mem')
Inputs may be any that keep to these rules, and one draw needn't show every extreme that they name: Each token names 3 different owners. Within the tokens of one device (aligned blocks of 128 rows) no owner is named by more than 24 tokens, and one owner, the same for every block of a draw, is named by exactly 24 tokens of every block. `pick_index`: the 32 entries of a token are different.
All inputs are finite; a program needn't handle non-finite values.
Results may differ from a plain program's by a relative error of at most 0.006.
Values may be sent and summed in bfloat16 or wider, within the bound.
No kernel may reach another device: no remote copies, remote signals or barrier semaphores. Data moves between devices by JAX's collectives and lax.ppermute only.
A program may use at most 64 MiB of HBM per device.

v0:
```python
import jax
import jax.numpy as jnp
from jax import lax
from jax.sharding import PartitionSpec as P

beta_first = 0.9
beta_second = 0.95
learning_rate = 0.01
adam_epsilon = 1e-08
first_bias = 1.0 - (0.9**50) ** 2
second_bias = 1.0 - (0.95**50) ** 2
norm_epsilon = 1e-05


def per_device(
    owners,
    pick_index,
    key_scores,
    output_cotangent,
    value_table,
    first_moment,
    second_moment,
    norm_gain,
):
    owner_count = lax.axis_size("mem")
    token_count, cand_count = owners.shape
    row_count, model_width = value_table.shape
    pair_count = token_count * cand_count
    slot_count = 6 * token_count // owner_count
    buffer_rows = owner_count * slot_count
    highest = lax.Precision.HIGHEST
    weights = jax.nn.softmax(key_scores, axis=-1)
    spread = (
        pick_index[:, :, None] == jnp.arange(cand_count * row_count, dtype=jnp.int32)[None, None, :]
    ).astype(jnp.float32)
    placed = jnp.einsum("tkm,tk->tm", spread, weights, precision=highest).astype(jnp.bfloat16)
    pair_weights = placed.reshape(pair_count, row_count)
    pair_owner = owners.reshape(pair_count)
    owner_hits = (pair_owner[:, None] == jnp.arange(owner_count, dtype=jnp.int32)[None, :]).astype(
        jnp.int32
    )
    earlier = jnp.cumsum(owner_hits, axis=0) - owner_hits
    slot_index = jnp.sum(earlier * owner_hits, axis=1)
    target = pair_owner * slot_count + slot_index
    buffer_slots = jnp.arange(buffer_rows, dtype=jnp.int32)
    dispatch = (buffer_slots[:, None] == target[None, :]).astype(jnp.bfloat16)
    combine = jnp.any(
        buffer_slots[None, None, :] == target.reshape(token_count, cand_count)[:, :, None], axis=1
    ).astype(jnp.bfloat16)
    send_weights = jnp.dot(dispatch, pair_weights, preferred_element_type=jnp.float32).astype(
        jnp.bfloat16
    )
    send_weights = send_weights.reshape(owner_count, slot_count, row_count)
    arrived = lax.all_to_all(send_weights, "mem", split_axis=0, concat_axis=0, tiled=True)
    partial_value = jnp.einsum(
        "scj,jd->scd", arrived, value_table, preferred_element_type=jnp.float32
    ).astype(jnp.bfloat16)
    returned = lax.all_to_all(partial_value, "mem", split_axis=0, concat_axis=0, tiled=True)
    arrived_weights = arrived
    memory = jnp.dot(
        combine, returned.reshape(buffer_rows, model_width), preferred_element_type=jnp.float32
    )
    inverse = lax.rsqrt(jnp.mean(memory * memory, axis=-1, keepdims=True) + norm_epsilon)
    memory_out = (memory * inverse * norm_gain).astype(jnp.bfloat16)
    cotangent = output_cotangent.astype(jnp.float32)
    scaled = cotangent * norm_gain
    memory_grad = inverse * scaled - memory * inverse**3 * jnp.mean(
        scaled * memory, axis=-1, keepdims=True
    )
    memory_grad = memory_grad.astype(jnp.bfloat16)
    gain_local = jnp.sum(cotangent * memory * inverse, axis=0)
    send_grads = lax.dot_general(
        combine, memory_grad, (((0,), (0,)), ((), ())), preferred_element_type=jnp.float32
    )
    send_grads = send_grads.astype(jnp.bfloat16).reshape(owner_count, slot_count, model_width)
    arrived = lax.all_to_all(send_grads, "mem", split_axis=0, concat_axis=0, tiled=True)
    pick_grad = jnp.einsum("scd,jd->scj", arrived, value_table, preferred_element_type=jnp.float32)
    back_grads = lax.all_to_all(
        pick_grad.astype(jnp.bfloat16), "mem", split_axis=0, concat_axis=0, tiled=True
    ).astype(pick_grad.dtype)
    table_local = jnp.einsum(
        "scj,scd->jd", arrived_weights, arrived, preferred_element_type=jnp.float32
    )
    pair_grad = lax.dot_general(
        dispatch.astype(jnp.float32),
        back_grads.reshape(buffer_rows, row_count),
        (((0,), (0,)), ((), ())),
        precision=highest,
    )
    placed_grad = pair_grad.reshape(token_count, cand_count * row_count)
    weight_grad = jnp.einsum("tkm,tm->tk", spread, placed_grad, precision=highest)
    score_gradient = weights * (
        weight_grad - jnp.sum(weights * weight_grad, axis=-1, keepdims=True)
    )
    table_grad = lax.psum(table_local.astype(jnp.bfloat16), "dp").astype(jnp.float32)
    gain_gradient = lax.psum(gain_local, ("dp", "mem"))
    updated_first = beta_first * first_moment + (1.0 - beta_first) * table_grad
    updated_second = beta_second * second_moment + (1.0 - beta_second) * table_grad * table_grad
    update = (
        learning_rate
        * (updated_first / first_bias)
        / (jnp.sqrt(updated_second / second_bias) + adam_epsilon)
    )
    updated_table = (value_table.astype(jnp.float32) - update).astype(jnp.bfloat16)
    return (memory_out, score_gradient, gain_gradient, updated_table, updated_first, updated_second)


def solution(mesh):
    return jax.shard_map(
        per_device,
        mesh=mesh,
        in_specs=(
            P(("dp", "mem"), None),
            P(("dp", "mem"), None),
            P(("dp", "mem"), None),
            P(("dp", "mem"), None),
            P("mem", None),
            P("mem", None),
            P("mem", None),
            P(),
        ),
        out_specs=(
            P(("dp", "mem"), None),
            P(("dp", "mem"), None),
            P(),
            P("mem", None),
            P("mem", None),
            P("mem", None),
        ),
        check_vma=False,
    )
```

profile of v0, /device:TPU:6, one launch (start us, length us, event | category | flops | bytes accessed | tf_op | source)
XLA Modules:
  0.0 483.5 jit_solution(8843205107341875663)
XLA Ops:
  7.2 0.0 copy-start.1
  7.2 0.8 copy.38
  8.0 0.2 eq.65
  8.2 0.2 eq.69
  8.4 0.7 reduce_max.9
  9.2 0.7 fusion.34
  9.9 0.7 fusion.35
  10.6 0.1 copy.45
  10.7 0.8 copy.42
  11.6 1.5 fusion.9
  13.1 0.9 reduce-window.6
  14.0 0.2 slice_reduce_fusion
  14.2 0.1 fusion.29
  14.3 0.1 reshape.86
  14.5 0.3 fusion.13
  14.8 0.2 copy.50
  15.0 0.2 reshape.100
  15.2 14.2 %all_to_all.20 = bf16[32,2,384]{2,1,0:T(2,128)(2,1)S(1)} all-to-all(bf16[32,2,384]{2,1,0:T(2,128)(2,1)S(1)} %reshape.100), channel_id=1, replica_groups=mesh['dp'=16,'mem'=32] {'mem'}, dimensions={0} | all-to-all | bytes 98304 | tf_op jit(solution)/shard_map/all_to_all | solution.py:54
  29.3 0.1 reshape.101
  29.5 0.0 copy-done.1
  29.5 4.9 %convolution_convert_fusion.1 = bf16[32,24,4096]{2,1,0:T(8,128)(2,1)} fusion(bf16[32,24,32]{2,1,0:T(8,128)(2,1)S(1)} %reshape.101, bf16[32,4096]{1,0:T(8,128)(2,1)S(1)} %copy-done.1), kind=kOutput, calls=%fused_computation.1 | convolution fusion | flops 204472320 | bytes 6602752 | tf_op jit(solution)/shard_map/scj,jd->scd/dot_general | solution.py:55
  34.4 6.9 %all-to-all-start.1 = ((bf16[32,24,4096]{2,1,0:T(8,128)(2,1)}), bf16[32,24,4096]{2,1,0:T(8,128)(2,1)}, u32[]{:S(2)}, u32[]{:S(2)}) async-start(bf16[32,24,4096]{2,1,0:T(8,128)(2,1)} %convolution_convert_fusion.1), calls=%async_computation.1 | async-start | bytes 12582912 | tf_op jit(solution)/shard_map/all_to_all | solution.py:58
  41.3 0.2 reduce_sum.57
  41.5 0.1 copy.41
  41.5 0.0 copy-done.6
  41.5 0.2 fusion.12
  41.8 76.7 %all-to-all-done.1 = bf16[32,24,4096]{2,1,0:T(8,128)(2,1)} async-done(((bf16[32,24,4096]{2,1,0:T(8,128)(2,1)}), bf16[32,24,4096]{2,1,0:T(8,128)(2,1)}, u32[]{:S(2)}, u32[]{:S(2)}) %all-to-all-start.1) | async-done | bytes 6291488 | tf_op jit(solution)/shard_map/all_to_all | solution.py:58
  118.5 4.0 multiply_reduce_fusion
  122.5 1.8 fusion.7
  124.3 4.6 convolution_convert_fusion
  129.0 13.2 %all-to-all-start.2 = ((bf16[32,24,4096]{2,1,0:T(8,128)(2,1)}), bf16[32,24,4096]{2,1,0:T(8,128)(2,1)}, u32[]{:S(2)}, u32[]{:S(2)}) async-start(bf16[32,24,4096]{2,1,0:T(8,128)(2,1)} %bitcast.56), calls=%async_computation.2 | async-start | bytes 12582912 | tf_op jit(solution)/shard_map/all_to_all | solution.py:76
  142.2 182.4 %psum.14 = f32[4096]{0:T(1024)} all-reduce(f32[4096]{0:T(1024)S(1)} %get-tuple-element.6), channel_id=1, replica_groups=mesh['dp'=16,'mem'=32] {'dp','mem'}, use_global_device_ids=true, to_apply=%region_10.11 | all-reduce | flops 4096 | bytes 32768 | tf_op jit(solution)/shard_map/psum | solution.py:96
  324.6 0.0 all-to-all-done.2
  324.6 4.6 convolution_convert_fusion.2
  329.1 0.8 reshape.102
  329.9 7.3 %all-to-all-start.3 = ((bf16[32,2,384]{2,1,0:T(2,128)(2,1)}), bf16[32,2,384]{2,1,0:T(2,128)(2,1)S(1)}, u32[]{:S(2)}, u32[]{:S(2)}) async-start(bf16[32,2,384]{2,1,0:T(2,128)(2,1)} %reshape.102), calls=%async_computation.3 | async-start | bytes 98304 | tf_op jit(solution)/shard_map/all_to_all | solution.py:78
  337.3 0.0 all-reduce.2.cloned.1.call-start
  337.3 4.7 fusion
  342.0 0.0 all-reduce.2.cloned.1.call-update
  342.1 0.8 all-to-all-done.3
  342.9 0.1 reshape.103
  343.0 0.5 fusion.10
  343.5 0.1 reshape.95
  343.6 2.0 fusion.8
  345.6 0.1 copy.49
  345.7 0.6 fusion.32
  346.4 128.1 %all-reduce.2.cloned.1.call-done = bf16[32,4096]{1,0:T(8,128)(2,1)} async-done(((bf16[32,4096]{1,0:T(8,128)(2,1)}), bf16[32,4096]{1,0:T(8,128)(2,1)}) %all-reduce.2.cloned.1.call-update) | async-done | bytes 262160 | tf_op jit(solution)/shard_map/psum | solution.py:95
  474.5 2.2 subtract_convert_fusion
  (19 shorter events, 0.1 us)
Async XLA Ops:
  7.2 22.3 %copy-start.1 = (bf16[32,4096]{1,0:T(8,128)(2,1)S(1)}, bf16[32,4096]{1,0:T(8,128)(2,1)}, u32[]{:S(2)}) copy-start(bf16[32,4096]{1,0:T(8,128)(2,1)} %param.12) | copy-start | bytes 786436
  34.4 7.2 %copy-start.6 = (s32[128,3]{0,1:T(4,128)S(1)}, s32[128,3]{0,1:T(4,128)}, u32[]{:S(2)}) copy-start(s32[128,3]{0,1:T(4,128)} %param.8) | copy-start | bytes 4612
  34.4 84.2 %all-to-all-start.1 = ((bf16[32,24,4096]{2,1,0:T(8,128)(2,1)}), bf16[32,24,4096]{2,1,0:T(8,128)(2,1)}, u32[]{:S(2)}, u32[]{:S(2)}) async-start(bf16[32,24,4096]{2,1,0:T(8,128)(2,1)} %convolution_convert_fusion.1), calls=%async_computation.1 | async-start | bytes 12582912 | tf_op jit(solution)/shard_map/all_to_all | solution.py:58
  118.5 4.0 copy-start
  118.5 4.0 copy-start.5
  129.0 195.6 %all-to-all-start.2 = ((bf16[32,24,4096]{2,1,0:T(8,128)(2,1)}), bf16[32,24,4096]{2,1,0:T(8,128)(2,1)}, u32[]{:S(2)}, u32[]{:S(2)}) async-start(bf16[32,24,4096]{2,1,0:T(8,128)(2,1)} %bitcast.56), calls=%async_computation.2 | async-start | bytes 12582912 | tf_op jit(solution)/shard_map/all_to_all | solution.py:76
  329.9 12.9 %all-to-all-start.3 = ((bf16[32,2,384]{2,1,0:T(2,128)(2,1)}), bf16[32,2,384]{2,1,0:T(2,128)(2,1)S(1)}, u32[]{:S(2)}, u32[]{:S(2)}) async-start(bf16[32,2,384]{2,1,0:T(2,128)(2,1)} %reshape.102), calls=%async_computation.3 | async-start | bytes 98304 | tf_op jit(solution)/shard_map/all_to_all | solution.py:78
  337.3 137.2 %all-reduce.2.cloned.1.call-start = ((), (), s32[]{:S(2)}) async-start(), calls=%async_computation.4 | async-start | bytes 524288 | tf_op jit(solution)/shard_map/psum | solution.py:95
  342.0 3.6 copy-start.4
  342.0 132.4 %copy-start.2 = (f32[32,4096]{1,0:T(8,128)S(1)}, f32[32,4096]{1,0:T(8,128)}, u32[]{:S(2)}) copy-start(f32[32,4096]{1,0:T(8,128)} %param.13) | copy-start | bytes 1572868
  342.0 132.4 %copy-start.3 = (f32[32,4096]{1,0:T(8,128)S(1)}, f32[32,4096]{1,0:T(8,128)}, u32[]{:S(2)}) copy-start(f32[32,4096]{1,0:T(8,128)} %param.14) | copy-start | bytes 1572868
Sparse Core Ops, SparseCore 0:
  342.2 132.2 all-reduce.1
where the time goes:
time: 484 us
  waiting for transfers between devices  206 us (43%)
  blocking collectives  197 us (41%)
  starting transfers between devices  27.5 us (6%)
  matrix products  27.1 us (6%)
  between operations  14.2 us (3%)
  other arithmetic  8.21 us (2%)
    psum x1, blocking collectives, per_device(): gain_gradient = lax.psum(gain_local, ('dp', 'mem'))  182 us
    psum x1, waiting for transfers between devices, per_device(): lax.psum(table_local.astype(jnp.bfloat16), 'dp').astype(jnp.float32)  128 us
    all_to_all x1, waiting for transfers between devices, per_device(): lax.all_to_all(partial_value, 'mem', split_axis=0, concat_axis=0, tiled=T...  76.7 us
    all_to_all x1, blocking collectives, per_device(): lax.all_to_all(send_weights, 'mem', split_axis=0, concat_axis=0, tiled=True)  14.2 us
    all_to_all x1, starting transfers between devices, per_device(): lax.all_to_all(send_grads, 'mem', split_axis=0, concat_axis=0, tiled=True)  13.2 us
  transfers between devices with their start and end apart: 4, of which 3 were waited for; matrix products, arithmetic and copies ran while one was open for 2% of the time, Pallas kernels for 0%

commit v1 on v0

v1 whole, which is shorter than its diff:
```python
import functools

import jax
import jax.numpy as jnp
from jax import lax
from jax.experimental import pallas as pl
from jax.experimental.pallas import tpu as pltpu
from jax.sharding import Mesh
from jax.sharding import PartitionSpec as P

beta_first = 0.9
beta_second = 0.95
learning_rate = 0.01
adam_epsilon = 1e-08
first_bias = 1.0 - (0.9**50) ** 2
second_bias = 1.0 - (0.95**50) ** 2
norm_epsilon = 1e-05

L = 128
PAIR = 2
RING = 8
GROUP = PAIR * RING
CANDS = 3
ROWS = 32
PICKS = 32
D = 4096
WIDE = D // GROUP
TILES = WIDE // L
TOK = 128
SLOTS = CANDS * ROWS
TABLE = 1024
OWNERS = TABLE // ROWS
INFO = SLOTS + 8
GAIN_AT = TILES * ROWS
GRAD = GAIN_AT + 8
BACK = WIDE + SLOTS
STEP = 2
VMEM_LIMIT = 32 * 1024 * 1024
F32 = jnp.float32
BF16 = jnp.bfloat16
PARAMS = pltpu.CompilerParams(vmem_limit_bytes=VMEM_LIMIT)


def dot(a, b, dims):
    return lax.dot_general(a, b, (dims, ((), ())), preferred_element_type=F32)


def shape(*dims_and_type):
    return jax.ShapeDtypeStruct(dims_and_type[:-1], dims_and_type[-1])


def in_hbm(*dims_and_type):
    return pltpu.HBM(dims_and_type[:-1], dims_and_type[-1])


def table_kernel(place_ref, table_ref, out_ref):
    del place_ref
    for j in range(TILES):
        tile = table_ref[:, j * L : (j + 1) * L]
        for x in range(out_ref.shape[0]):
            out_ref[x, 0, j * ROWS : (j + 1) * ROWS, :] = tile


def pack_kernel(owners_ref, pick_ref, scores_ref, cotangent_ref, send_ref, weights_ref, info_ref):
    @pl.when(pl.program_id(0) == 0)
    def _():
        scores = scores_ref[...]
        shifted = jnp.exp(scores - jnp.max(scores, axis=0, keepdims=True))
        weights = shifted / jnp.sum(shifted, axis=0, keepdims=True)
        weights_ref[...] = weights
        pick = pick_ref[...]
        entry = lax.broadcasted_iota(jnp.int32, (SLOTS, TOK), 0)
        placed = jnp.zeros((SLOTS, TOK), F32)
        for k in range(PICKS):
            placed = jnp.where(pick[k : k + 1] == entry, weights[k : k + 1], placed)
        owners = owners_ref[...].astype(F32)
        line = lax.broadcasted_iota(jnp.int32, (8, TOK), 0)
        named = jnp.zeros((8, TOK), F32)
        for c in range(CANDS):
            named = jnp.where(line == c, owners[c : c + 1], named)
        info_ref[...] = jnp.concatenate([placed, named], axis=0).astype(BF16)

    for j in range(TILES):
        send_ref[0, j * L : (j + 1) * L, :] = jnp.transpose(cotangent_ref[:, j * L : (j + 1) * L])
    send_ref[0, WIDE:, :] = info_ref[...]


def load_info(batch_ref):
    info = jnp.concatenate([batch_ref[i, WIDE:, :] for i in range(STEP)], axis=1).astype(F32)
    placed = [info[c * ROWS : (c + 1) * ROWS] for c in range(CANDS)]
    named = [
        jnp.broadcast_to(info[SLOTS + c : SLOTS + c + 1], (ROWS, STEP * TOK)) for c in range(CANDS)
    ]
    return placed, named


def place(placed, named):
    blocks = []
    for o in range(OWNERS):
        block = jnp.zeros((ROWS, STEP * TOK), F32)
        for c in range(CANDS):
            block = jnp.where(named[c] == float(o), placed[c], block)
        blocks.append(block.astype(BF16))
    return jnp.concatenate(blocks, axis=0)


def load_table(table_ref):
    return jnp.concatenate(
        [table_ref[:, j * ROWS : (j + 1) * ROWS, :].reshape(TABLE, L) for j in range(TILES)], axis=1
    )


def load_cotangent(batch_ref):
    return jnp.concatenate([batch_ref[i, :WIDE, :] for i in range(STEP)], axis=1).astype(F32)


def forward_kernel(batch_ref, table_ref, gain_ref, memory_ref, sums_ref, turned_ref):
    @pl.when(pl.program_id(0) == 0)
    def _():
        turned_ref[...] = jnp.transpose(load_table(table_ref))

    memory = dot(turned_ref[...], place(*load_info(batch_ref)), ((1,), (0,)))
    memory_ref[...] = memory
    scaled = load_cotangent(batch_ref) * gain_ref[...]
    square = jnp.sum(memory * memory, axis=0, keepdims=True)
    cross = jnp.sum(scaled * memory, axis=0, keepdims=True)
    both = jnp.concatenate([square, cross], axis=0)
    for g in range(sums_ref.shape[0]):
        sums_ref[g] = both


def split(value):
    high = value.astype(BF16).astype(F32)
    return high, value - high


def gain_rows(rows):
    high, low = split(rows)
    return jnp.concatenate([high, low, jnp.zeros((8 - 2 * TILES, L), F32)], axis=0).astype(BF16)


def backward_kernel(batch_ref, gain_ref, memory_ref, sums_ref, out_ref, grad_ref, send_ref, total_ref, gain_sum_ref):
    step = pl.program_id(0)
    sums = jnp.sum(sums_ref[...], axis=0)
    inverse = lax.rsqrt(sums[0:1] / D + norm_epsilon)
    factor = inverse * inverse * inverse * (sums[1:2] / D)
    memory = memory_ref[...]
    cotangent = load_cotangent(batch_ref)
    gain = gain_ref[...]
    normed = memory * inverse
    out_ref[...] = (normed * gain).astype(BF16)
    grad = (inverse * (cotangent * gain) - memory * factor).astype(BF16)
    grad_ref[...] = grad
    gain_part = cotangent * normed
    folded = sum(gain_part[:, i * L : (i + 1) * L] for i in range(STEP))
    table_part = dot(place(*load_info(batch_ref)), grad, ((1,), (1,)))

    @pl.when(step == 0)
    def _():
        total_ref[...] = table_part
        gain_sum_ref[...] = folded

    @pl.when(step > 0)
    def _():
        total_ref[...] += table_part
        gain_sum_ref[...] += folded

    @pl.when(step == pl.num_programs(0) - 1)
    def _():
        for j in range(TILES):
            send_ref[:, j * ROWS : (j + 1) * ROWS, :] = (
                total_ref[:, j * L : (j + 1) * L].astype(BF16).reshape(OWNERS, ROWS, L)
            )
        turned = jnp.transpose(gain_sum_ref[...])
        rows = [jnp.sum(turned[:, j * L : (j + 1) * L], axis=0, keepdims=True) for j in range(TILES)]
        tail = gain_rows(jnp.concatenate(rows, axis=0))
        for o in range(OWNERS):
            send_ref[o, GAIN_AT:, :] = tail


def placed_grad_kernel(batch_ref, table_ref, out_ref, grad_ref, send_ref):
    _, named = load_info(batch_ref)
    full = dot(load_table(table_ref), grad_ref[...], ((1,), (0,)))
    found = [jnp.zeros((ROWS, STEP * TOK), F32) for _ in range(CANDS)]
    for o in range(OWNERS):
        block = full[o * ROWS : (o + 1) * ROWS]
        for c in range(CANDS):
            found[c] = jnp.where(named[c] == float(o), block, found[c])
    for i in range(STEP):
        send_ref[i, :WIDE, :] = out_ref[:, i * TOK : (i + 1) * TOK]
        for c in range(CANDS):
            send_ref[i, WIDE + c * ROWS : WIDE + (c + 1) * ROWS, :] = found[c][
                :, i * TOK : (i + 1) * TOK
            ].astype(BF16)


def merge(parts):
    total = jnp.sum(parts, axis=0)
    gain = total[GAIN_AT : GAIN_AT + TILES] + total[GAIN_AT + TILES : GAIN_AT + 2 * TILES]
    return total[:GAIN_AT], gain


def plane_kernel(parts_ref, send_ref):
    for b in range(parts_ref.shape[1]):
        rows, gain = merge(parts_ref[:, b].astype(F32))
        send_ref[b, :GAIN_AT, :] = rows.astype(BF16)
        send_ref[b, GAIN_AT:, :] = gain_rows(gain)


def share_kernel(parts_ref, send_ref):
    rows, gain = merge(parts_ref[...].astype(F32))
    rows = rows.astype(BF16)
    tail = gain_rows(gain)
    for b in range(send_ref.shape[0]):
        send_ref[b, :GAIN_AT, :] = rows
        send_ref[b, GAIN_AT:, :] = tail


def adam_kernel(grad_ref, table_ref, first_ref, second_ref, new_table_ref, new_first_ref, new_second_ref, gain_ref):
    for b in range(grad_ref.shape[0]):
        for j in range(TILES):
            at = b * WIDE + j * L
            grad = grad_ref[b, j * ROWS : (j + 1) * ROWS, :].astype(F32)
            first = beta_first * first_ref[:, at : at + L] + (1.0 - beta_first) * grad
            second = beta_second * second_ref[:, at : at + L] + (1.0 - beta_second) * grad * grad
            update = learning_rate * (first / first_bias) / (jnp.sqrt(second / second_bias) + adam_epsilon)
            new_first_ref[:, at : at + L] = first
            new_second_ref[:, at : at + L] = second
            new_table_ref[:, at : at + L] = (table_ref[:, at : at + L].astype(F32) - update).astype(BF16)
            tail = grad_ref[b, GAIN_AT:, :].astype(F32)
            gain_ref[:, at : at + L] = tail[j : j + 1] + tail[TILES + j : TILES + j + 1]


def out_kernel(parts_ref, pick_ref, weights_ref, out_ref, score_ref, placed_grad_ref):
    step = pl.program_id(0)
    for j in range(TILES):
        out_ref[:, j * L : (j + 1) * L] = jnp.transpose(parts_ref[0, j * L : (j + 1) * L, :])
    part = parts_ref[0, WIDE:, :].astype(F32)

    @pl.when(step == 0)
    def _():
        placed_grad_ref[...] = part

    @pl.when(step > 0)
    def _():
        placed_grad_ref[...] += part

    @pl.when(step == pl.num_programs(0) - 1)
    def _():
        pick = pick_ref[...]
        weights = weights_ref[...]
        weight_grad = jnp.zeros((PICKS, TOK), F32)
        for m in range(SLOTS):
            weight_grad = jnp.where(pick == m, placed_grad_ref[m : m + 1, :], weight_grad)
        mean = jnp.sum(weights * weight_grad, axis=0, keepdims=True)
        score_ref[...] = weights * (weight_grad - mean)


def exchange(array, axes):
    return lax.all_to_all(array, axes, split_axis=0, concat_axis=0, tiled=True)


def per_device(
    owners,
    pick_index,
    key_scores,
    output_cotangent,
    value_table,
    first_moment,
    second_moment,
    norm_gain,
):
    rows_x = lax.axis_size("x")
    steps = GROUP // STEP
    half = lax.axis_index("dl")
    block_index = half * RING + lax.axis_index("yc")

    whole = lambda *dims: pl.BlockSpec(dims, lambda i: (0,) * len(dims))

    table_send = pl.pallas_call(
        table_kernel,
        grid_spec=pltpu.PrefetchScalarGridSpec(
            num_scalar_prefetch=1,
            grid=(RING,),
            in_specs=[pl.BlockSpec((ROWS, WIDE), lambda i, place_ref: (0, place_ref[0] * RING + i))],
            out_specs=pl.BlockSpec((rows_x, 1, TILES * ROWS, L), lambda i, place_ref: (0, i, 0, 0)),
        ),
        out_shape=in_hbm(rows_x, RING, TILES * ROWS, L, BF16),
        compiler_params=PARAMS,
        name="table_send",
    )(half.reshape(1).astype(jnp.int32), value_table)
    table = exchange(table_send.reshape(OWNERS, TILES * ROWS, L), ("x", "yc"))

    batch_send, weights = pl.pallas_call(
        pack_kernel,
        grid=(GROUP,),
        in_specs=[
            whole(CANDS, TOK),
            whole(PICKS, TOK),
            whole(PICKS, TOK),
            pl.BlockSpec((TOK, WIDE), lambda i: (0, i)),
        ],
        out_specs=[pl.BlockSpec((1, WIDE + INFO, L), lambda i: (i, 0, 0)), whole(PICKS, TOK)],
        out_shape=(in_hbm(GROUP, WIDE + INFO, L, BF16), shape(PICKS, TOK, F32)),
        scratch_shapes=[pltpu.VMEM((INFO, TOK), BF16)],
        compiler_params=PARAMS,
        name="pack",
    )(owners.T, pick_index.T, key_scores.T, output_cotangent)
    batch = exchange(batch_send, ("dl", "yc"))
    gain = lax.dynamic_slice(norm_gain, (block_index * WIDE,), (WIDE,)).reshape(WIDE, 1)

    batch_spec = pl.BlockSpec((STEP, WIDE + INFO, L), lambda i: (i, 0, 0))
    table_spec = whole(OWNERS, TILES * ROWS, L)
    wide_spec = pl.BlockSpec((WIDE, STEP * TOK), lambda i: (0, i))
    sums_spec = pl.BlockSpec((GROUP, 2, STEP * TOK), lambda i: (0, 0, i))
    tokens = GROUP * TOK

    memory, sums_send = pl.pallas_call(
        forward_kernel,
        grid=(steps,),
        in_specs=[batch_spec, table_spec, whole(WIDE, 1)],
        out_specs=[wide_spec, sums_spec],
        out_shape=(shape(WIDE, tokens, F32), shape(GROUP, 2, tokens, F32)),
        scratch_shapes=[pltpu.VMEM((WIDE, TABLE), BF16)],
        compiler_params=PARAMS,
        name="forward",
    )(batch, table, gain)
    sums = exchange(sums_send, ("dl", "yc"))

    out_turned, memory_grad, grad_send = pl.pallas_call(
        backward_kernel,
        grid=(steps,),
        in_specs=[batch_spec, whole(WIDE, 1), wide_spec, sums_spec],
        out_specs=[wide_spec, wide_spec, whole(OWNERS, GRAD, L)],
        out_shape=(
            shape(WIDE, tokens, BF16),
            shape(WIDE, tokens, BF16),
            in_hbm(OWNERS, GRAD, L, BF16),
        ),
        scratch_shapes=[pltpu.VMEM((TABLE, WIDE), F32), pltpu.VMEM((WIDE, L), F32)],
        compiler_params=PARAMS,
        name="backward",
    )(batch, gain, memory, sums)
    plane_parts = exchange(grad_send, ("x", "yc"))

    back_send = pl.pallas_call(
        placed_grad_kernel,
        grid=(steps,),
        in_specs=[batch_spec, table_spec, wide_spec, wide_spec],
        out_specs=pl.BlockSpec((STEP, BACK, L), lambda i: (i, 0, 0)),
        out_shape=in_hbm(GROUP, BACK, L, BF16),
        compiler_params=PARAMS,
        name="placed_grad",
    )(batch, table, out_turned, memory_grad)

    shares_send = pl.pallas_call(
        plane_kernel,
        out_shape=in_hbm(RING, GRAD, L, BF16),
        compiler_params=PARAMS,
        name="plane_sum",
    )(plane_parts.reshape(rows_x, RING, GRAD, L))
    shares = exchange(shares_send, "dh")
    total_send = pl.pallas_call(
        share_kernel,
        out_shape=in_hbm(GROUP, GRAD, L, BF16),
        compiler_params=PARAMS,
        name="share_sum",
    )(shares)
    total = exchange(total_send, ("dl", "dh"))

    back = exchange(back_send, ("dl", "yc"))
    memory_out, score_turned = pl.pallas_call(
        out_kernel,
        grid=(GROUP,),
        in_specs=[pl.BlockSpec((1, BACK, L), lambda i: (i, 0, 0)), whole(PICKS, TOK), whole(PICKS, TOK)],
        out_specs=[pl.BlockSpec((TOK, WIDE), lambda i: (0, i)), whole(PICKS, TOK)],
        out_shape=(shape(TOK, D, BF16), shape(PICKS, TOK, F32)),
        scratch_shapes=[pltpu.VMEM((SLOTS, TOK), F32)],
        compiler_params=PARAMS,
        name="unpack",
    )(back, pick_index.T, weights)

    new_table, new_first, new_second, gain_gradient = pl.pallas_call(
        adam_kernel,
        out_shape=(
            shape(ROWS, D, BF16),
            shape(ROWS, D, F32),
            shape(ROWS, D, F32),
            shape(1, D, F32),
        ),
        compiler_params=PARAMS,
        name="adam",
    )(total, value_table, first_moment, second_moment)
    return (memory_out, score_turned.T, gain_gradient.reshape(D), new_table, new_first, new_second)


def solution(mesh):
    planes, mem_count = mesh.shape["dp"], mesh.shape["mem"]
    split_mesh = Mesh(
        mesh.devices.reshape(planes // PAIR, PAIR, mem_count // RING, RING), ("dh", "dl", "x", "yc")
    )
    tokens = P(("dh", "dl", "x", "yc"), None)
    rows = P(("x", "yc"), None)
    return jax.shard_map(
        per_device,
        mesh=split_mesh,
        in_specs=(tokens, tokens, tokens, tokens, rows, rows, rows, P()),
        out_specs=(tokens, tokens, P(), rows, rows, rows),
        check_vma=False,
    )
```

time: 484 us -> 174 us (0.36)
  the two profiles are of different devices: /device:TPU:6 before, /device:TPU:64 now
where the time goes in v1:
time: 174 us; the launch traced here: 173 us
  waiting for transfers between devices  60.4 us (35%)
  blocking collectives  56.9 us (33%)
  Pallas kernels  31.7 us (18%)
  starting transfers between devices  20.5 us (12%)
  local copies, waits for them, and re-layouts  3.18 us (2%)
    all_to_all x4, waiting for transfers between devices, exchange(): return lax.all_to_all(array, axes, split_axis=0, concat_axis=0, tiled=True)  60.4 us
    all_to_all x3, blocking collectives, exchange(): return lax.all_to_all(array, axes, split_axis=0, concat_axis=0, tiled=True)  56.9 us
    all_to_all x4, starting transfers between devices, exchange(): return lax.all_to_all(array, axes, split_axis=0, concat_axis=0, tiled=True)  20.5 us
    pallas_call x1, Pallas kernels, per_device(): pl.pallas_call(pack_kernel, grid=(GROUP,), in_specs=[whole(CANDS, TOK), w...  6.08 us
    pallas_call x1, Pallas kernels, per_device(): pl.pallas_call(backward_kernel, grid=(steps,), in_specs=[batch_spec, whol...  5.99 us
    pallas_call x1, Pallas kernels, per_device(): pl.pallas_call(out_kernel, grid=(GROUP,), in_specs=[pl.BlockSpec((1, BACK...  5.87 us
    pallas_call x1, Pallas kernels, per_device(): pl.pallas_call(placed_grad_kernel, grid=(steps,), in_specs=[batch_spec, t...  4.9 us
  transfers between devices with their start and end apart: 4, of which 4 were waited for; matrix products, arithmetic and copies ran while one was open for 1% of the time, Pallas kernels for 7%

profile of v1, /device:TPU:64, one launch (start us, length us, event | category | flops | bytes accessed | tf_op | source)
XLA Modules:
  0.0 173.4 jit_solution(2219139875622282138)
XLA Ops:
  0.6 0.0 copy-start
  0.6 0.0 copy-start.1
  0.7 1.0 copy-done.1
  1.7 0.0 copy-start.7
  1.7 0.0 copy-start.8
  1.7 0.0 copy-start.9
  1.7 2.6 %table_send.1 = bf16[4,8,64,128]{3,2,1,0:T(8,128)(2,1)} custom-call(s32[1]{0:T(128)} %bitcast.3.place_ref, bf16[32,4096]{1,0:T(8,128)(2,1)S(1)} %copy-done.1), custom_call_target="tpu_custom_call" | custom-call | tf_op jit(solution)/shard_map/table_send/pallas_call | solution.py:280
  4.3 7.3 %all-to-all-start.1 = ((bf16[32,64,128]{2,1,0:T(8,128)(2,1)}), bf16[32,64,128]{2,1,0:T(8,128)(2,1)S(1)}, u32[]{:S(2)}, u32[]{:S(2)}) async-start(bf16[32,64,128]{2,1,0:T(8,128)(2,1)} %bitcast.14), calls=%async_computation.1 | async-start | bytes 1048576 | tf_op jit(solution)/shard_map/all_to_all | solution.py:260
  11.6 0.0 copy-done
  11.7 0.0 copy-done.7
  11.7 0.0 copy-done.8
  11.7 0.0 copy-done.9
  11.7 6.1 %pack.1 = (bf16[16,360,128]{2,1,0:T(8,128)(2,1)}, f32[32,128]{1,0:T(8,128)S(1)}) custom-call(s32[3,128]{1,0:T(4,128)S(1)} %bitcast.13, s32[32,128]{1,0:T(8,128)S(1)} %bitcast.10, f32[32,128]{1,0:T(8,128)S(1)} %bitcast.12, bf16[128,4096]{1,0:T(8,128)(2,1)S(1)} %copy-done), custom_call_target="tpu_custom_call" | custom-call | tf_op jit(solution)/shard_map/pack/pallas_call | solution.py:294
  17.8 5.1 %all-to-all-done.1.table_ref = bf16[32,64,128]{2,1,0:T(8,128)(2,1)S(1)} async-done(((bf16[32,64,128]{2,1,0:T(8,128)(2,1)}), bf16[32,64,128]{2,1,0:T(8,128)(2,1)S(1)}, u32[]{:S(2)}, u32[]{:S(2)}) %all-to-all-start.1) | async-done | bytes 524320 | tf_op jit(solution)/shard_map/all_to_all | solution.py:260
  22.8 4.5 %all-to-all-start = ((bf16[16,360,128]{2,1,0:T(8,128)(2,1)}), bf16[16,360,128]{2,1,0:T(8,128)(2,1)S(1)}, u32[]{:S(2)}, u32[]{:S(2)}) async-start(bf16[16,360,128]{2,1,0:T(8,128)(2,1)} %get-tuple-element.19), calls=%async_computation | async-start | bytes 2949120 | tf_op jit(solution)/shard_map/all_to_all | solution.py:260
  27.4 0.8 dynamic_slice.3
  28.2 0.1 copy.15.gain_ref
  28.3 20.4 %all-to-all-done.batch_ref = bf16[16,360,128]{2,1,0:T(8,128)(2,1)S(1)} async-done(((bf16[16,360,128]{2,1,0:T(8,128)(2,1)}), bf16[16,360,128]{2,1,0:T(8,128)(2,1)S(1)}, u32[]{:S(2)}, u32[]{:S(2)}) %all-to-all-start) | async-done | bytes 1474592 | tf_op jit(solution)/shard_map/all_to_all | solution.py:260
  48.7 3.4 %forward.1 = (f32[256,2048]{1,0:T(8,128)S(1)}, f32[16,2,2048]{2,1,0:T(2,128)S(1)}) custom-call(bf16[16,360,128]{2,1,0:T(8,128)(2,1)S(1)} %all-to-all-done.batch_ref, bf16[32,64,128]{2,1,0:T(8,128)(2,1)S(1)} %all-to-all-done.1.table_ref, f32[256,1]{1,0:T(8,128)S(1)} %copy.15.gain_ref), custom_call_target="tpu_custom_call" | custom-call | tf_op jit(solution)/shard_map/forward/pallas_call | solution.py:318
  52.1 11.6 %all_to_all.35.sums_ref = f32[16,2,2048]{2,1,0:T(2,128)S(1)} all-to-all(f32[16,2,2048]{2,1,0:T(2,128)S(1)} %get-tuple-element.21), channel_id=1, replica_groups=mesh['dh'=8,'dl'=2,'x'=4,'yc'=8] {'dl','yc'}, dimensions={0} | all-to-all | bytes 524288 | tf_op jit(solution)/shard_map/all_to_all | solution.py:260
  63.7 6.0 %backward.1 = (bf16[256,2048]{1,0:T(8,128)(2,1)S(1)}, bf16[256,2048]{1,0:T(8,128)(2,1)S(1)}, bf16[32,72,128]{2,1,0:T(8,128)(2,1)}) custom-call(bf16[16,360,128]{2,1,0:T(8,128)(2,1)S(1)} %all-to-all-done.batch_ref, f32[256,1]{1,0:T(8,128)S(1)} %copy.15.gain_ref, f32[256,2048]{1,0:T(8,128)S(1)} %get-tuple-element.20.memory_ref, ...), custom_call_target="tpu_custom_call" | custom-call | tf_op jit(solution)/shard_map/backward/pallas_call | solution.py:330
  69.7 0.0 copy-start.3
  69.7 15.7 %all_to_all.36 = bf16[32,72,128]{2,1,0:T(8,128)(2,1)S(1)} all-to-all(bf16[32,72,128]{2,1,0:T(8,128)(2,1)} %get-tuple-element.27), channel_id=1, replica_groups=mesh['dh'=8,'dl'=2,'x'=4,'yc'=8] {'x','yc'}, dimensions={0} | all-to-all | bytes 1179648 | tf_op jit(solution)/shard_map/all_to_all | solution.py:260
  85.4 0.8 plane_sum.1
  86.1 0.0 copy-done.3
  86.1 29.6 %all_to_all.37.parts_ref = bf16[8,72,128]{2,1,0:T(8,128)(2,1)S(1)} all-to-all(bf16[8,72,128]{2,1,0:T(8,128)(2,1)} %plane_sum.1), channel_id=1, replica_groups=mesh['dh'=8,'dl'=2,'x'=4,'yc'=8] {'dh'}, dimensions={0} | all-to-all | bytes 294912 | tf_op jit(solution)/shard_map/all_to_all | solution.py:260
  115.7 0.7 share_sum.1
  116.4 5.0 %all-to-all-start.6 = ((bf16[16,72,128]{2,1,0:T(8,128)(2,1)}), bf16[16,72,128]{2,1,0:T(8,128)(2,1)S(1)}, u32[]{:S(2)}, u32[]{:S(2)}) async-start(bf16[16,72,128]{2,1,0:T(8,128)(2,1)} %share_sum.1), calls=%async_computation.6 | async-start | bytes 589824 | tf_op jit(solution)/shard_map/all_to_all | solution.py:260
  121.4 0.0 copy-start.4
  121.4 1.2 copy-done.4
  122.6 4.9 %placed_grad.1 = bf16[16,352,128]{2,1,0:T(8,128)(2,1)} custom-call(bf16[16,360,128]{2,1,0:T(8,128)(2,1)S(1)} %all-to-all-done.batch_ref, bf16[32,64,128]{2,1,0:T(8,128)(2,1)S(1)} %all-to-all-done.1.table_ref, bf16[256,2048]{1,0:T(8,128)(2,1)S(1)} %get-tuple-element.22.out_ref, bf16[256,2048]{1,0:T(8,128)(2,1)S(1)} %copy-done.4), custom_call_target="tpu_custom_call" | custom-call | tf_op jit(solution)/shard_map/placed_grad/pallas_call | solution.py:346
  127.5 0.0 copy-start.2
  127.5 0.0 copy-start.5
  127.5 0.0 copy-start.6
  127.5 15.4 %all-to-all-done.6.grad_ref = bf16[16,72,128]{2,1,0:T(8,128)(2,1)S(1)} async-done(((bf16[16,72,128]{2,1,0:T(8,128)(2,1)}), bf16[16,72,128]{2,1,0:T(8,128)(2,1)S(1)}, u32[]{:S(2)}, u32[]{:S(2)}) %all-to-all-start.6) | async-done | bytes 294944 | tf_op jit(solution)/shard_map/all_to_all | solution.py:260
  142.9 3.7 %all-to-all-start.3 = ((bf16[16,352,128]{2,1,0:T(8,128)(2,1)}), bf16[16,352,128]{2,1,0:T(8,128)(2,1)S(1)}, u32[]{:S(2)}, u32[]{:S(2)}) async-start(bf16[16,352,128]{2,1,0:T(8,128)(2,1)} %placed_grad.1), calls=%async_computation.3 | async-start | bytes 2883584 | tf_op jit(solution)/shard_map/all_to_all | solution.py:260
  146.6 0.0 copy-done.2
  146.6 0.0 copy-done.5
  146.6 0.0 copy-done.6
  146.7 1.3 adam.1
  148.0 19.6 %all-to-all-done.3.parts_ref = bf16[16,352,128]{2,1,0:T(8,128)(2,1)S(1)} async-done(((bf16[16,352,128]{2,1,0:T(8,128)(2,1)}), bf16[16,352,128]{2,1,0:T(8,128)(2,1)S(1)}, u32[]{:S(2)}, u32[]{:S(2)}) %all-to-all-start.3) | async-done | bytes 1441824 | tf_op jit(solution)/shard_map/all_to_all | solution.py:260
  167.6 5.9 %unpack.1 = (bf16[128,4096]{1,0:T(8,128)(2,1)}, f32[32,128]{1,0:T(8,128)}) custom-call(bf16[16,352,128]{2,1,0:T(8,128)(2,1)S(1)} %all-to-all-done.3.parts_ref, s32[32,128]{1,0:T(8,128)S(1)} %bitcast.11, f32[32,128]{1,0:T(8,128)S(1)} %get-tuple-element.24.weights_ref), custom_call_target="tpu_custom_call" | custom-call | tf_op jit(solution)/shard_map/unpack/pallas_call | solution.py:372
Async XLA Ops:
  0.6 11.0 %copy-start = (bf16[128,4096]{1,0:T(8,128)(2,1)S(1)}, bf16[128,4096]{1,0:T(8,128)(2,1)}, u32[]{:S(2)}) copy-start(bf16[128,4096]{1,0:T(8,128)(2,1)} %cotangent_ref.1) | copy-start | bytes 3145732
  0.6 1.0 copy-start.1
  1.7 10.0 %copy-start.7 = (s32[128,32]{0,1:T(8,128)S(1)}, s32[128,32]{0,1:T(8,128)}, u32[]{:S(2)}) copy-start(s32[128,32]{0,1:T(8,128)} %param.9) | copy-start | bytes 49156
  1.7 10.0 %copy-start.8 = (f32[128,32]{0,1:T(8,128)S(1)}, f32[128,32]{0,1:T(8,128)}, u32[]{:S(2)}) copy-start(f32[128,32]{0,1:T(8,128)} %param.10) | copy-start | bytes 49156
  1.7 10.0 %copy-start.9 = (s32[128,3]{0,1:T(4,128)S(1)}, s32[128,3]{0,1:T(4,128)}, u32[]{:S(2)}) copy-start(s32[128,3]{0,1:T(4,128)} %param.8) | copy-start | bytes 4612
  4.3 18.5 %all-to-all-start.1 = ((bf16[32,64,128]{2,1,0:T(8,128)(2,1)}), bf16[32,64,128]{2,1,0:T(8,128)(2,1)S(1)}, u32[]{:S(2)}, u32[]{:S(2)}) async-start(bf16[32,64,128]{2,1,0:T(8,128)(2,1)} %bitcast.14), calls=%async_computation.1 | async-start | bytes 1048576 | tf_op jit(solution)/shard_map/all_to_all | solution.py:260
  22.8 25.9 %all-to-all-start = ((bf16[16,360,128]{2,1,0:T(8,128)(2,1)}), bf16[16,360,128]{2,1,0:T(8,128)(2,1)S(1)}, u32[]{:S(2)}, u32[]{:S(2)}) async-start(bf16[16,360,128]{2,1,0:T(8,128)(2,1)} %get-tuple-element.19), calls=%async_computation | async-start | bytes 2949120 | tf_op jit(solution)/shard_map/all_to_all | solution.py:260
  69.7 16.4 %copy-start.3 = (bf16[256,2048]{1,0:T(8,128)(2,1)}, bf16[256,2048]{1,0:T(8,128)(2,1)S(1)}, u32[]{:S(2)}) copy-start(bf16[256,2048]{1,0:T(8,128)(2,1)S(1)} %get-tuple-element.23.grad_ref) | copy-start | bytes 3145732
  116.4 26.5 %all-to-all-start.6 = ((bf16[16,72,128]{2,1,0:T(8,128)(2,1)}), bf16[16,72,128]{2,1,0:T(8,128)(2,1)S(1)}, u32[]{:S(2)}, u32[]{:S(2)}) async-start(bf16[16,72,128]{2,1,0:T(8,128)(2,1)} %share_sum.1), calls=%async_computation.6 | async-start | bytes 589824 | tf_op jit(solution)/shard_map/all_to_all | solution.py:260
  121.4 1.2 copy-start.4
  127.5 19.1 %copy-start.2 = (bf16[32,4096]{1,0:T(8,128)(2,1)S(1)}, bf16[32,4096]{1,0:T(8,128)(2,1)}, u32[]{:S(2)}) copy-start(bf16[32,4096]{1,0:T(8,128)(2,1)} %table_ref.3) | copy-start | bytes 786436
  127.5 19.1 %copy-start.5 = (f32[32,4096]{1,0:T(8,128)S(1)}, f32[32,4096]{1,0:T(8,128)}, u32[]{:S(2)}) copy-start(f32[32,4096]{1,0:T(8,128)} %first_ref.1) | copy-start | bytes 1572868
  127.5 19.1 %copy-start.6 = (f32[32,4096]{1,0:T(8,128)S(1)}, f32[32,4096]{1,0:T(8,128)}, u32[]{:S(2)}) copy-start(f32[32,4096]{1,0:T(8,128)} %second_ref.1) | copy-start | bytes 1572868
  142.9 24.7 %all-to-all-start.3 = ((bf16[16,352,128]{2,1,0:T(8,128)(2,1)}), bf16[16,352,128]{2,1,0:T(8,128)(2,1)S(1)}, u32[]{:S(2)}, u32[]{:S(2)}) async-start(bf16[16,352,128]{2,1,0:T(8,128)(2,1)} %placed_grad.1), calls=%async_computation.3 | async-start | bytes 2883584 | tf_op jit(solution)/shard_map/all_to_all | solution.py:260

commit v2 on v1

--- a/solution.py
+++ b/solution.py
@@ -34,7 +34,8 @@
 GAIN_AT = TILES * ROWS
 GRAD = GAIN_AT + 8
 BACK = WIDE + SLOTS
-STEP = 2
+STEP = 4
+MANY = 4
 VMEM_LIMIT = 32 * 1024 * 1024
 F32 = jnp.float32
 BF16 = jnp.bfloat16
@@ -55,10 +56,12 @@
 
 def table_kernel(place_ref, table_ref, out_ref):
     del place_ref
-    for j in range(TILES):
-        tile = table_ref[:, j * L : (j + 1) * L]
-        for x in range(out_ref.shape[0]):
-            out_ref[x, 0, j * ROWS : (j + 1) * ROWS, :] = tile
+    for b in range(RING):
+        for j in range(TILES):
+            at = b * WIDE + j * L
+            tile = table_ref[:, at : at + L]
+            for x in range(out_ref.shape[0]):
+                out_ref[x, b, j * ROWS : (j + 1) * ROWS, :] = tile
 
 
 def pack_kernel(owners_ref, pick_ref, scores_ref, cotangent_ref, send_ref, weights_ref, info_ref):
@@ -80,9 +83,11 @@
             named = jnp.where(line == c, owners[c : c + 1], named)
         info_ref[...] = jnp.concatenate([placed, named], axis=0).astype(BF16)
 
-    for j in range(TILES):
-        send_ref[0, j * L : (j + 1) * L, :] = jnp.transpose(cotangent_ref[:, j * L : (j + 1) * L])
-    send_ref[0, WIDE:, :] = info_ref[...]
+    for b in range(MANY):
+        for j in range(TILES):
+            at = b * WIDE + j * L
+            send_ref[b, j * L : (j + 1) * L, :] = jnp.transpose(cotangent_ref[:, at : at + L])
+        send_ref[b, WIDE:, :] = info_ref[...]
 
 
 def load_info(batch_ref):
@@ -209,33 +214,33 @@
 
 def share_kernel(parts_ref, send_ref):
     rows, gain = merge(parts_ref[...].astype(F32))
-    rows = rows.astype(BF16)
-    tail = gain_rows(gain)
-    for b in range(send_ref.shape[0]):
-        send_ref[b, :GAIN_AT, :] = rows
-        send_ref[b, GAIN_AT:, :] = tail
+    send_ref[:GAIN_AT, :] = rows.astype(BF16)
+    send_ref[GAIN_AT:, :] = gain_rows(gain)
 
 
 def adam_kernel(grad_ref, table_ref, first_ref, second_ref, new_table_ref, new_first_ref, new_second_ref, gain_ref):
-    for b in range(grad_ref.shape[0]):
+    for z in range(grad_ref.shape[0]):
+        b = (z % PAIR) * RING + z // PAIR
+        tail = grad_ref[z, GAIN_AT:, :].astype(F32)
         for j in range(TILES):
             at = b * WIDE + j * L
-            grad = grad_ref[b, j * ROWS : (j + 1) * ROWS, :].astype(F32)
+            grad = grad_ref[z, j * ROWS : (j + 1) * ROWS, :].astype(F32)
             first = beta_first * first_ref[:, at : at + L] + (1.0 - beta_first) * grad
             second = beta_second * second_ref[:, at : at + L] + (1.0 - beta_second) * grad * grad
             update = learning_rate * (first / first_bias) / (jnp.sqrt(second / second_bias) + adam_epsilon)
             new_first_ref[:, at : at + L] = first
             new_second_ref[:, at : at + L] = second
             new_table_ref[:, at : at + L] = (table_ref[:, at : at + L].astype(F32) - update).astype(BF16)
-            tail = grad_ref[b, GAIN_AT:, :].astype(F32)
             gain_ref[:, at : at + L] = tail[j : j + 1] + tail[TILES + j : TILES + j + 1]
 
 
 def out_kernel(parts_ref, pick_ref, weights_ref, out_ref, score_ref, placed_grad_ref):
     step = pl.program_id(0)
-    for j in range(TILES):
-        out_ref[:, j * L : (j + 1) * L] = jnp.transpose(parts_ref[0, j * L : (j + 1) * L, :])
-    part = parts_ref[0, WIDE:, :].astype(F32)
+    for b in range(MANY):
+        for j in range(TILES):
+            at = b * WIDE + j * L
+            out_ref[:, at : at + L] = jnp.transpose(parts_ref[b, j * L : (j + 1) * L, :])
+    part = sum(parts_ref[b, WIDE:, :].astype(F32) for b in range(MANY))
 
     @pl.when(step == 0)
     def _():
@@ -281,9 +286,9 @@
         table_kernel,
         grid_spec=pltpu.PrefetchScalarGridSpec(
             num_scalar_prefetch=1,
-            grid=(RING,),
-            in_specs=[pl.BlockSpec((ROWS, WIDE), lambda i, place_ref: (0, place_ref[0] * RING + i))],
-            out_specs=pl.BlockSpec((rows_x, 1, TILES * ROWS, L), lambda i, place_ref: (0, i, 0, 0)),
+            grid=(1,),
+            in_specs=[pl.BlockSpec((ROWS, RING * WIDE), lambda i, place_ref: (0, place_ref[0]))],
+            out_specs=pl.BlockSpec((rows_x, RING, TILES * ROWS, L), lambda i, place_ref: (0, 0, 0, 0)),
         ),
         out_shape=in_hbm(rows_x, RING, TILES * ROWS, L, BF16),
         compiler_params=PARAMS,
@@ -293,14 +298,14 @@
 
     batch_send, weights = pl.pallas_call(
         pack_kernel,
-        grid=(GROUP,),
+        grid=(GROUP // MANY,),
         in_specs=[
             whole(CANDS, TOK),
             whole(PICKS, TOK),
             whole(PICKS, TOK),
-            pl.BlockSpec((TOK, WIDE), lambda i: (0, i)),
+            pl.BlockSpec((TOK, MANY * WIDE), lambda i: (0, i)),
         ],
-        out_specs=[pl.BlockSpec((1, WIDE + INFO, L), lambda i: (i, 0, 0)), whole(PICKS, TOK)],
+        out_specs=[pl.BlockSpec((MANY, WIDE + INFO, L), lambda i: (i, 0, 0)), whole(PICKS, TOK)],
         out_shape=(in_hbm(GROUP, WIDE + INFO, L, BF16), shape(PICKS, TOK, F32)),
         scratch_shapes=[pltpu.VMEM((INFO, TOK), BF16)],
         compiler_params=PARAMS,
@@ -333,8 +338,8 @@
         in_specs=[batch_spec, whole(WIDE, 1), wide_spec, sums_spec],
         out_specs=[wide_spec, wide_spec, whole(OWNERS, GRAD, L)],
         out_shape=(
-            shape(WIDE, tokens, BF16),
-            shape(WIDE, tokens, BF16),
+            in_hbm(WIDE, tokens, BF16),
+            in_hbm(WIDE, tokens, BF16),
             in_hbm(OWNERS, GRAD, L, BF16),
         ),
         scratch_shapes=[pltpu.VMEM((TABLE, WIDE), F32), pltpu.VMEM((WIDE, L), F32)],
@@ -353,27 +358,29 @@
         name="placed_grad",
     )(batch, table, out_turned, memory_grad)
 
+    plane_parts, back_send = lax.optimization_barrier((plane_parts, back_send))
     shares_send = pl.pallas_call(
         plane_kernel,
-        out_shape=in_hbm(RING, GRAD, L, BF16),
+        out_shape=shape(RING, GRAD, L, BF16),
         compiler_params=PARAMS,
         name="plane_sum",
     )(plane_parts.reshape(rows_x, RING, GRAD, L))
     shares = exchange(shares_send, "dh")
-    total_send = pl.pallas_call(
+    total = pl.pallas_call(
         share_kernel,
-        out_shape=in_hbm(GROUP, GRAD, L, BF16),
+        out_shape=shape(GRAD, L, BF16),
         compiler_params=PARAMS,
         name="share_sum",
     )(shares)
-    total = exchange(total_send, ("dl", "dh"))
+    total, back_send = lax.optimization_barrier((total, back_send))
+    totals = lax.all_gather(total, ("dh", "dl"), axis=0, tiled=False)
 
     back = exchange(back_send, ("dl", "yc"))
     memory_out, score_turned = pl.pallas_call(
         out_kernel,
-        grid=(GROUP,),
-        in_specs=[pl.BlockSpec((1, BACK, L), lambda i: (i, 0, 0)), whole(PICKS, TOK), whole(PICKS, TOK)],
-        out_specs=[pl.BlockSpec((TOK, WIDE), lambda i: (0, i)), whole(PICKS, TOK)],
+        grid=(GROUP // MANY,),
+        in_specs=[pl.BlockSpec((MANY, BACK, L), lambda i: (i, 0, 0)), whole(PICKS, TOK), whole(PICKS, TOK)],
+        out_specs=[pl.BlockSpec((TOK, MANY * WIDE), lambda i: (0, i)), whole(PICKS, TOK)],
         out_shape=(shape(TOK, D, BF16), shape(PICKS, TOK, F32)),
         scratch_shapes=[pltpu.VMEM((SLOTS, TOK), F32)],
         compiler_params=PARAMS,
@@ -390,7 +397,7 @@
         ),
         compiler_params=PARAMS,
         name="adam",
-    )(total, value_table, first_moment, second_moment)
+    )(totals, value_table, first_moment, second_moment)
     return (memory_out, score_turned.T, gain_gradient.reshape(D), new_table, new_first, new_second)
 
 

time: 174 us -> 163 us (0.937)
  the two profiles are of different devices: /device:TPU:64 before, /device:TPU:8 now
where the time goes in v2:
time: 163 us
  blocking collectives  84.4 us (52%)
  waiting for transfers between devices  30.7 us (19%)
  starting transfers between devices  25.9 us (16%)
  Pallas kernels  16.6 us (10%)
  local copies, waits for them, and re-layouts  4.4 us (3%)
    all_gather x1, blocking collectives, per_device(): totals = lax.all_gather(total, ('dh', 'dl'), axis=0, tiled=False)  42.5 us
    all_to_all x2, blocking collectives, exchange(): return lax.all_to_all(array, axes, split_axis=0, concat_axis=0, tiled=True)  41.9 us
    all_to_all x4, waiting for transfers between devices, exchange(): return lax.all_to_all(array, axes, split_axis=0, concat_axis=0, tiled=True)  30.7 us
    all_to_all x4, starting transfers between devices, exchange(): return lax.all_to_all(array, axes, split_axis=0, concat_axis=0, tiled=True)  25.9 us
    pallas_call x1, Pallas kernels, per_device(): pl.pallas_call(backward_kernel, grid=(steps,), in_specs=[batch_spec, whol...  4.59 us
    unnamed x20, local copies, waits for them, and re-layouts  3.51 us
  transfers between devices with their start and end apart: 4, of which 3 were waited for; matrix products, arithmetic and copies ran while one was open for 1% of the time, Pallas kernels for 4%

profile of v2, /device:TPU:8, one launch (start us, length us, event | category | flops | bytes accessed | tf_op | source)
XLA Modules:
  0.0 162.8 jit_solution(12462424844683899884)
XLA Ops:
  0.6 0.0 copy-start
  0.6 0.0 copy-start.1
  0.7 1.0 copy-done.1
  1.7 0.0 copy-start.7
  1.7 0.0 copy-start.8
  1.7 0.0 copy-start.9
  1.7 0.9 table_send.1
  2.6 9.4 %all-to-all-start.1 = ((bf16[32,64,128]{2,1,0:T(8,128)(2,1)}), bf16[32,64,128]{2,1,0:T(8,128)(2,1)S(1)}, u32[]{:S(2)}, u32[]{:S(2)}) async-start(bf16[32,64,128]{2,1,0:T(8,128)(2,1)} %bitcast.16), calls=%async_computation.1 | async-start | bytes 1048576 | tf_op jit(solution)/shard_map/all_to_all | solution.py:265
  11.9 0.0 copy-done
  12.0 0.0 copy-done.7
  12.0 0.0 copy-done.8
  12.0 0.0 copy-done.9
  12.0 2.2 %pack.1 = (bf16[16,360,128]{2,1,0:T(8,128)(2,1)}, f32[32,128]{1,0:T(8,128)S(1)}) custom-call(s32[3,128]{1,0:T(4,128)S(1)} %bitcast.15, s32[32,128]{1,0:T(8,128)S(1)} %bitcast.12, f32[32,128]{1,0:T(8,128)S(1)} %bitcast.14, bf16[128,4096]{1,0:T(8,128)(2,1)S(1)} %copy-done), custom_call_target="tpu_custom_call" | custom-call | tf_op jit(solution)/shard_map/pack/pallas_call | solution.py:299
  14.2 8.0 %all-to-all-done.1.table_ref = bf16[32,64,128]{2,1,0:T(8,128)(2,1)S(1)} async-done(((bf16[32,64,128]{2,1,0:T(8,128)(2,1)}), bf16[32,64,128]{2,1,0:T(8,128)(2,1)S(1)}, u32[]{:S(2)}, u32[]{:S(2)}) %all-to-all-start.1) | async-done | bytes 524320 | tf_op jit(solution)/shard_map/all_to_all | solution.py:265
  22.2 4.8 %all-to-all-start = ((bf16[16,360,128]{2,1,0:T(8,128)(2,1)}), bf16[16,360,128]{2,1,0:T(8,128)(2,1)S(1)}, u32[]{:S(2)}, u32[]{:S(2)}) async-start(bf16[16,360,128]{2,1,0:T(8,128)(2,1)} %get-tuple-element.23), calls=%async_computation | async-start | bytes 2949120 | tf_op jit(solution)/shard_map/all_to_all | solution.py:265
  27.0 0.8 dynamic_slice.3
  27.7 0.1 copy.15.gain_ref
  27.9 17.4 %all-to-all-done.batch_ref = bf16[16,360,128]{2,1,0:T(8,128)(2,1)S(1)} async-done(((bf16[16,360,128]{2,1,0:T(8,128)(2,1)}), bf16[16,360,128]{2,1,0:T(8,128)(2,1)S(1)}, u32[]{:S(2)}, u32[]{:S(2)}) %all-to-all-start) | async-done | bytes 1474592 | tf_op jit(solution)/shard_map/all_to_all | solution.py:265
  45.2 2.5 %forward.1 = (f32[256,2048]{1,0:T(8,128)S(1)}, f32[16,2,2048]{2,1,0:T(2,128)S(1)}) custom-call(bf16[16,360,128]{2,1,0:T(8,128)(2,1)S(1)} %all-to-all-done.batch_ref, bf16[32,64,128]{2,1,0:T(8,128)(2,1)S(1)} %all-to-all-done.1.table_ref, f32[256,1]{1,0:T(8,128)S(1)} %copy.15.gain_ref), custom_call_target="tpu_custom_call" | custom-call | tf_op jit(solution)/shard_map/forward/pallas_call | solution.py:323
  47.8 12.2 %all_to_all.30.sums_ref = f32[16,2,2048]{2,1,0:T(2,128)S(1)} all-to-all(f32[16,2,2048]{2,1,0:T(2,128)S(1)} %get-tuple-element.25), channel_id=1, replica_groups=mesh['dh'=8,'dl'=2,'x'=4,'yc'=8] {'dl','yc'}, dimensions={0} | all-to-all | bytes 524288 | tf_op jit(solution)/shard_map/all_to_all | solution.py:265
  59.9 4.6 %backward.1 = (bf16[256,2048]{1,0:T(8,128)(2,1)}, bf16[256,2048]{1,0:T(8,128)(2,1)}, bf16[32,72,128]{2,1,0:T(8,128)(2,1)}) custom-call(bf16[16,360,128]{2,1,0:T(8,128)(2,1)S(1)} %all-to-all-done.batch_ref, f32[256,1]{1,0:T(8,128)S(1)} %copy.15.gain_ref, f32[256,2048]{1,0:T(8,128)S(1)} %get-tuple-element.24.memory_ref, f32[16,2,2048]{2,1,0:T(2,128)S(1)} %all_to_all.30.sums_ref), custom_call_target="tpu_custom_call" | custom-call | tf_op jit(solution)/shard_map/backward/pallas_call | solution.py:335
  64.5 6.3 %all-to-all-start.3 = ((bf16[32,72,128]{2,1,0:T(8,128)(2,1)}), bf16[32,72,128]{2,1,0:T(8,128)(2,1)S(1)}, u32[]{:S(2)}, u32[]{:S(2)}) async-start(bf16[32,72,128]{2,1,0:T(8,128)(2,1)} %get-tuple-element.26), calls=%async_computation.3 | async-start | bytes 1179648 | tf_op jit(solution)/shard_map/all_to_all | solution.py:265
  70.8 0.0 copy-start.3
  70.8 1.2 copy-done.3
  72.0 0.0 copy-start.4
  72.0 1.2 copy-done.4
  73.2 3.0 %placed_grad.1 = bf16[16,352,128]{2,1,0:T(8,128)(2,1)} custom-call(bf16[16,360,128]{2,1,0:T(8,128)(2,1)S(1)} %all-to-all-done.batch_ref, bf16[32,64,128]{2,1,0:T(8,128)(2,1)S(1)} %all-to-all-done.1.table_ref, bf16[256,2048]{1,0:T(8,128)(2,1)S(1)} %copy-done.3, bf16[256,2048]{1,0:T(8,128)(2,1)S(1)} %copy-done.4), custom_call_target="tpu_custom_call" | custom-call | tf_op jit(solution)/shard_map/placed_grad/pallas_call | solution.py:351
  76.3 5.4 %all-to-all-done.3 = bf16[32,72,128]{2,1,0:T(8,128)(2,1)S(1)} async-done(((bf16[32,72,128]{2,1,0:T(8,128)(2,1)}), bf16[32,72,128]{2,1,0:T(8,128)(2,1)S(1)}, u32[]{:S(2)}, u32[]{:S(2)}) %all-to-all-start.3) | async-done | bytes 589856 | tf_op jit(solution)/shard_map/all_to_all | solution.py:265
  81.6 0.1 plane_sum.1
  81.7 29.7 %all_to_all.31.parts_ref = bf16[8,72,128]{2,1,0:T(8,128)(2,1)S(1)} all-to-all(bf16[8,72,128]{2,1,0:T(8,128)(2,1)S(1)} %plane_sum.1), channel_id=1, replica_groups=mesh['dh'=8,'dl'=2,'x'=4,'yc'=8] {'dh'}, dimensions={0} | all-to-all | bytes 294912 | tf_op jit(solution)/shard_map/all_to_all | solution.py:265
  111.5 0.0 copy-start.2
  111.5 0.0 copy-start.5
  111.5 0.0 copy-start.6
  111.5 5.5 %all-to-all-start.5 = ((bf16[16,352,128]{2,1,0:T(8,128)(2,1)}), bf16[16,352,128]{2,1,0:T(8,128)(2,1)S(1)}, u32[]{:S(2)}, u32[]{:S(2)}) async-start(bf16[16,352,128]{2,1,0:T(8,128)(2,1)} %placed_grad.1), calls=%async_computation.5 | async-start | bytes 2883584 | tf_op jit(solution)/shard_map/all_to_all | solution.py:265
  117.0 42.5 %all-gather = bf16[1152,128]{1,0:T(8,128)(2,1)S(1)} all-gather(bf16[72,128]{1,0:T(8,128)(2,1)S(1)} %share_sum.1), channel_id=2, replica_groups=mesh['dh'=8,'dl'=2,'x'=4,'yc'=8] {'dh','dl'}, dimensions={0}, use_global_device_ids=true | all-gather | bytes 313344 | tf_op jit(solution)/shard_map/all_gather | solution.py:376
  159.5 0.0 copy-done.2
  159.5 0.0 copy-done.5
  159.5 0.0 copy-done.6
  159.5 1.3 adam.1
  160.8 0.0 all-to-all-done.5.parts_ref
  160.8 2.0 %unpack.1 = (bf16[128,4096]{1,0:T(8,128)(2,1)}, f32[32,128]{1,0:T(8,128)}) custom-call(bf16[16,352,128]{2,1,0:T(8,128)(2,1)S(1)} %all-to-all-done.5.parts_ref, s32[32,128]{1,0:T(8,128)S(1)} %bitcast.13, f32[32,128]{1,0:T(8,128)S(1)} %get-tuple-element.32.weights_ref), custom_call_target="tpu_custom_call" | custom-call | tf_op jit(solution)/shard_map/unpack/pallas_call | solution.py:379
  (1 shorter events, 0.0 us)
Async XLA Ops:
  0.6 11.3 %copy-start = (bf16[128,4096]{1,0:T(8,128)(2,1)S(1)}, bf16[128,4096]{1,0:T(8,128)(2,1)}, u32[]{:S(2)}) copy-start(bf16[128,4096]{1,0:T(8,128)(2,1)} %cotangent_ref.1) | copy-start | bytes 3145732
  0.6 1.0 copy-start.1
  1.7 10.3 %copy-start.7 = (s32[128,32]{0,1:T(8,128)S(1)}, s32[128,32]{0,1:T(8,128)}, u32[]{:S(2)}) copy-start(s32[128,32]{0,1:T(8,128)} %param.9) | copy-start | bytes 49156
  1.7 10.3 %copy-start.8 = (f32[128,32]{0,1:T(8,128)S(1)}, f32[128,32]{0,1:T(8,128)}, u32[]{:S(2)}) copy-start(f32[128,32]{0,1:T(8,128)} %param.10) | copy-start | bytes 49156
  1.7 10.3 %copy-start.9 = (s32[128,3]{0,1:T(4,128)S(1)}, s32[128,3]{0,1:T(4,128)}, u32[]{:S(2)}) copy-start(s32[128,3]{0,1:T(4,128)} %param.8) | copy-start | bytes 4612
  2.6 19.6 %all-to-all-start.1 = ((bf16[32,64,128]{2,1,0:T(8,128)(2,1)}), bf16[32,64,128]{2,1,0:T(8,128)(2,1)S(1)}, u32[]{:S(2)}, u32[]{:S(2)}) async-start(bf16[32,64,128]{2,1,0:T(8,128)(2,1)} %bitcast.16), calls=%async_computation.1 | async-start | bytes 1048576 | tf_op jit(solution)/shard_map/all_to_all | solution.py:265
  22.2 23.0 %all-to-all-start = ((bf16[16,360,128]{2,1,0:T(8,128)(2,1)}), bf16[16,360,128]{2,1,0:T(8,128)(2,1)S(1)}, u32[]{:S(2)}, u32[]{:S(2)}) async-start(bf16[16,360,128]{2,1,0:T(8,128)(2,1)} %get-tuple-element.23), calls=%async_computation | async-start | bytes 2949120 | tf_op jit(solution)/shard_map/all_to_all | solution.py:265
  64.5 17.1 %all-to-all-start.3 = ((bf16[32,72,128]{2,1,0:T(8,128)(2,1)}), bf16[32,72,128]{2,1,0:T(8,128)(2,1)S(1)}, u32[]{:S(2)}, u32[]{:S(2)}) async-start(bf16[32,72,128]{2,1,0:T(8,128)(2,1)} %get-tuple-element.26), calls=%async_computation.3 | async-start | bytes 1179648 | tf_op jit(solution)/shard_map/all_to_all | solution.py:265
  70.8 1.2 copy-start.3
  72.0 1.2 copy-start.4
  111.5 48.0 %copy-start.2 = (bf16[32,4096]{1,0:T(8,128)(2,1)S(1)}, bf16[32,4096]{1,0:T(8,128)(2,1)}, u32[]{:S(2)}) copy-start(bf16[32,4096]{1,0:T(8,128)(2,1)} %table_ref.3) | copy-start | bytes 786436
  111.5 48.0 %copy-start.5 = (f32[32,4096]{1,0:T(8,128)S(1)}, f32[32,4096]{1,0:T(8,128)}, u32[]{:S(2)}) copy-start(f32[32,4096]{1,0:T(8,128)} %first_ref.1) | copy-start | bytes 1572868
  111.5 48.0 %copy-start.6 = (f32[32,4096]{1,0:T(8,128)S(1)}, f32[32,4096]{1,0:T(8,128)}, u32[]{:S(2)}) copy-start(f32[32,4096]{1,0:T(8,128)} %second_ref.1) | copy-start | bytes 1572868
  111.5 49.3 %all-to-all-start.5 = ((bf16[16,352,128]{2,1,0:T(8,128)(2,1)}), bf16[16,352,128]{2,1,0:T(8,128)(2,1)S(1)}, u32[]{:S(2)}, u32[]{:S(2)}) async-start(bf16[16,352,128]{2,1,0:T(8,128)(2,1)} %placed_grad.1), calls=%async_computation.5 | async-start | bytes 2883584 | tf_op jit(solution)/shard_map/all_to_all | solution.py:265

commit v3 on v2

--- a/solution.py
+++ b/solution.py
@@ -20,6 +20,7 @@
 PAIR = 2
 RING = 8
 GROUP = PAIR * RING
+CHIPS = GROUP // 2
 CANDS = 3
 ROWS = 32
 PICKS = 32
@@ -183,7 +184,7 @@
             send_ref[o, GAIN_AT:, :] = tail
 
 
-def placed_grad_kernel(batch_ref, table_ref, out_ref, grad_ref, send_ref):
+def placed_grad_kernel(place_ref, batch_ref, table_ref, out_ref, grad_ref, same_ref, other_ref, stage_ref):
     _, named = load_info(batch_ref)
     full = dot(load_table(table_ref), grad_ref[...], ((1,), (0,)))
     found = [jnp.zeros((ROWS, STEP * TOK), F32) for _ in range(CANDS)]
@@ -191,12 +192,26 @@
         block = full[o * ROWS : (o + 1) * ROWS]
         for c in range(CANDS):
             found[c] = jnp.where(named[c] == float(o), block, found[c])
-    for i in range(STEP):
-        send_ref[i, :WIDE, :] = out_ref[:, i * TOK : (i + 1) * TOK]
-        for c in range(CANDS):
-            send_ref[i, WIDE + c * ROWS : WIDE + (c + 1) * ROWS, :] = found[c][
-                :, i * TOK : (i + 1) * TOK
-            ].astype(BF16)
+    stage_ref[:WIDE, :] = out_ref[...]
+    for c in range(CANDS):
+        stage_ref[WIDE + c * ROWS : WIDE + (c + 1) * ROWS, :] = found[c].astype(BF16)
+    low = lax.rem(place_ref[0], STEP)
+    for s in range(GROUP // STEP):
+
+        @pl.when(pl.program_id(0) == s)
+        def _():
+            for u in range(STEP):
+                at = pl.multiple_of(lax.bitwise_xor(low, u) * TOK, TOK)
+                send_ref = other_ref if u % 2 else same_ref
+                send_ref[(s * STEP + u) // 2] = stage_ref[:, pl.ds(at, TOK)]
+
+
+def merge_kernel(same_ref, other_ref, *send_refs):
+    for k, send_ref in enumerate(send_refs):
+        send_ref[:WIDE, :] = same_ref[k, :WIDE, :]
+        send_ref[WIDE : 2 * WIDE, :] = other_ref[k, :WIDE, :]
+        both = same_ref[k, WIDE:, :].astype(F32) + other_ref[k, WIDE:, :].astype(F32)
+        send_ref[2 * WIDE :, :] = both.astype(BF16)
 
 
 def merge(parts):
@@ -214,17 +229,19 @@
 
 def share_kernel(parts_ref, send_ref):
     rows, gain = merge(parts_ref[...].astype(F32))
-    send_ref[:GAIN_AT, :] = rows.astype(BF16)
-    send_ref[GAIN_AT:, :] = gain_rows(gain)
+    rows = rows.astype(BF16)
+    tail = gain_rows(gain)
+    for b in range(send_ref.shape[0]):
+        send_ref[b, :GAIN_AT, :] = rows
+        send_ref[b, GAIN_AT:, :] = tail
 
 
 def adam_kernel(grad_ref, table_ref, first_ref, second_ref, new_table_ref, new_first_ref, new_second_ref, gain_ref):
-    for z in range(grad_ref.shape[0]):
-        b = (z % PAIR) * RING + z // PAIR
-        tail = grad_ref[z, GAIN_AT:, :].astype(F32)
+    for b in range(grad_ref.shape[0]):
+        tail = grad_ref[b, GAIN_AT:, :].astype(F32)
         for j in range(TILES):
             at = b * WIDE + j * L
-            grad = grad_ref[z, j * ROWS : (j + 1) * ROWS, :].astype(F32)
+            grad = grad_ref[b, j * ROWS : (j + 1) * ROWS, :].astype(F32)
             first = beta_first * first_ref[:, at : at + L] + (1.0 - beta_first) * grad
             second = beta_second * second_ref[:, at : at + L] + (1.0 - beta_second) * grad * grad
             update = learning_rate * (first / first_bias) / (jnp.sqrt(second / second_bias) + adam_epsilon)
@@ -234,35 +251,31 @@
             gain_ref[:, at : at + L] = tail[j : j + 1] + tail[TILES + j : TILES + j + 1]
 
 
-def out_kernel(parts_ref, pick_ref, weights_ref, out_ref, score_ref, placed_grad_ref):
-    step = pl.program_id(0)
-    for b in range(MANY):
-        for j in range(TILES):
-            at = b * WIDE + j * L
-            out_ref[:, at : at + L] = jnp.transpose(parts_ref[b, j * L : (j + 1) * L, :])
-    part = sum(parts_ref[b, WIDE:, :].astype(F32) for b in range(MANY))
-
-    @pl.when(step == 0)
-    def _():
-        placed_grad_ref[...] = part
-
-    @pl.when(step > 0)
-    def _():
-        placed_grad_ref[...] += part
-
-    @pl.when(step == pl.num_programs(0) - 1)
-    def _():
-        pick = pick_ref[...]
-        weights = weights_ref[...]
-        weight_grad = jnp.zeros((PICKS, TOK), F32)
-        for m in range(SLOTS):
-            weight_grad = jnp.where(pick == m, placed_grad_ref[m : m + 1, :], weight_grad)
-        mean = jnp.sum(weights * weight_grad, axis=0, keepdims=True)
-        score_ref[...] = weights * (weight_grad - mean)
+def out_kernel(place_ref, pick_ref, weights_ref, *refs):
+    parts, (out_ref, score_ref, placed_grad_ref) = refs[:-3], refs[-3:]
+    for k, part_ref in enumerate(parts):
+        for core in range(2):
+            start = lax.bitwise_xor(place_ref[0], 2 * k + core) * WIDE
+            for j in range(TILES):
+                at = pl.multiple_of(start + j * L, L)
+                row = core * WIDE + j * L
+                out_ref[:, pl.ds(at, L)] = jnp.transpose(part_ref[row : row + L, :])
+    placed_grad_ref[...] = sum(part_ref[2 * WIDE :, :].astype(F32) for part_ref in parts)
+    pick = pick_ref[...]
+    weights = weights_ref[...]
+    weight_grad = jnp.zeros((PICKS, TOK), F32)
+    for m in range(SLOTS):
+        weight_grad = jnp.where(pick == m, placed_grad_ref[m : m + 1, :], weight_grad)
+    mean = jnp.sum(weights * weight_grad, axis=0, keepdims=True)
+    score_ref[...] = weights * (weight_grad - mean)
 
 
 def exchange(array, axes):
     return lax.all_to_all(array, axes, split_axis=0, concat_axis=0, tiled=True)
+
+
+def swap(array, k):
+    return lax.ppermute(array, ("dl", "yc"), [(i, i ^ k) for i in range(GROUP)])
 
 
 def per_device(
@@ -348,15 +361,33 @@
     )(batch, gain, memory, sums)
     plane_parts = exchange(grad_send, ("x", "yc"))
 
+    place_in_group = block_index.reshape(1).astype(jnp.int32)
+    turn = lambda i, place_ref: lax.bitwise_xor(i, lax.div(place_ref[0], STEP))
+    same, other = pl.pallas_call(
+        placed_grad_kernel,
+        grid_spec=pltpu.PrefetchScalarGridSpec(
+            num_scalar_prefetch=1,
+            grid=(steps,),
+            in_specs=[
+                pl.BlockSpec((STEP, WIDE + INFO, L), lambda i, place_ref: (turn(i, place_ref), 0, 0)),
+                pl.BlockSpec((OWNERS, TILES * ROWS, L), lambda i, place_ref: (0, 0, 0)),
+                pl.BlockSpec((WIDE, STEP * TOK), lambda i, place_ref: (0, turn(i, place_ref))),
+                pl.BlockSpec((WIDE, STEP * TOK), lambda i, place_ref: (0, turn(i, place_ref))),
+            ],
+            out_specs=[pl.BlockSpec((CHIPS, BACK, L), lambda i, place_ref: (0, 0, 0))] * 2,
+            scratch_shapes=[pltpu.VMEM((BACK, STEP * TOK), BF16)],
+        ),
+        out_shape=[shape(CHIPS, BACK, L, BF16)] * 2,
+        compiler_params=PARAMS,
+        name="placed_grad",
+    )(place_in_group, batch, table, out_turned, memory_grad)
+    other = swap(other, 1)
     back_send = pl.pallas_call(
-        placed_grad_kernel,
-        grid=(steps,),
-        in_specs=[batch_spec, table_spec, wide_spec, wide_spec],
-        out_specs=pl.BlockSpec((STEP, BACK, L), lambda i: (i, 0, 0)),
-        out_shape=in_hbm(GROUP, BACK, L, BF16),
-        compiler_params=PARAMS,
-        name="placed_grad",
-    )(batch, table, out_turned, memory_grad)
+        merge_kernel,
+        out_shape=[shape(2 * WIDE + SLOTS, L, BF16)] * CHIPS,
+        compiler_params=PARAMS,
+        name="merge",
+    )(same, other)
 
     plane_parts, back_send = lax.optimization_barrier((plane_parts, back_send))
     shares_send = pl.pallas_call(
@@ -365,27 +396,33 @@
         compiler_params=PARAMS,
         name="plane_sum",
     )(plane_parts.reshape(rows_x, RING, GRAD, L))
+    shares_send, back_send = lax.optimization_barrier((shares_send, back_send))
     shares = exchange(shares_send, "dh")
-    total = pl.pallas_call(
+    half_way = CHIPS // 2
+    back = [swap(back_send[k], 2 * k) for k in range(1, half_way)]
+    shares, back = lax.optimization_barrier((shares, back))
+    total_send = pl.pallas_call(
         share_kernel,
-        out_shape=shape(GRAD, L, BF16),
+        out_shape=shape(GROUP, GRAD, L, BF16),
         compiler_params=PARAMS,
         name="share_sum",
     )(shares)
-    total, back_send = lax.optimization_barrier((total, back_send))
-    totals = lax.all_gather(total, ("dh", "dl"), axis=0, tiled=False)
-
-    back = exchange(back_send, ("dl", "yc"))
+    total_send, late_send = lax.optimization_barrier((total_send, back_send[half_way:]))
+    total = exchange(total_send, ("dl", "dh"))
+    late = [swap(late_send[k - half_way], 2 * k) for k in range(half_way, CHIPS)]
+    total, late = lax.optimization_barrier((total, late))
+
+    vmem = pl.BlockSpec(memory_space=pltpu.VMEM)
+    smem = pl.BlockSpec(memory_space=pltpu.SMEM)
     memory_out, score_turned = pl.pallas_call(
         out_kernel,
-        grid=(GROUP // MANY,),
-        in_specs=[pl.BlockSpec((MANY, BACK, L), lambda i: (i, 0, 0)), whole(PICKS, TOK), whole(PICKS, TOK)],
-        out_specs=[pl.BlockSpec((TOK, MANY * WIDE), lambda i: (0, i)), whole(PICKS, TOK)],
+        in_specs=[smem] + [vmem] * (2 + CHIPS),
+        out_specs=[vmem, vmem],
         out_shape=(shape(TOK, D, BF16), shape(PICKS, TOK, F32)),
         scratch_shapes=[pltpu.VMEM((SLOTS, TOK), F32)],
         compiler_params=PARAMS,
         name="unpack",
-    )(back, pick_index.T, weights)
+    )(place_in_group, pick_index.T, weights, back_send[0], *back, *late)
 
     new_table, new_first, new_second, gain_gradient = pl.pallas_call(
         adam_kernel,
@@ -397,7 +434,7 @@
         ),
         compiler_params=PARAMS,
         name="adam",
-    )(totals, value_table, first_moment, second_moment)
+    )(total, value_table, first_moment, second_moment)
     return (memory_out, score_turned.T, gain_gradient.reshape(D), new_table, new_first, new_second)
 
 

time: 163 us -> 166 us (1.018)
  the two profiles are of different devices: /device:TPU:8 before, /device:TPU:6 now
where the time goes in v3:
time: 166 us; the launch traced here: 163 us
  starting transfers between devices  70.2 us (42%)
  waiting for transfers between devices  55.1 us (33%)
  Pallas kernels  18.3 us (11%)
  blocking collectives  11.6 us (7%)
  local copies, waits for them, and re-layouts  7.06 us (4%)
    all_to_all x5, starting transfers between devices, exchange(): return lax.all_to_all(array, axes, split_axis=0, concat_axis=0, tiled=True)  43.2 us
    all_to_all x5, waiting for transfers between devices, exchange(): return lax.all_to_all(array, axes, split_axis=0, concat_axis=0, tiled=True)  34.9 us
    ppermute x8, starting transfers between devices, swap(): return lax.ppermute(array, ('dl', 'yc'), [(i, i ^ k) for i in range(GROUP)])  27 us
    ppermute x8, waiting for transfers between devices, swap(): return lax.ppermute(array, ('dl', 'yc'), [(i, i ^ k) for i in range(GROUP)])  20.2 us
    all_to_all x1, blocking collectives, exchange(): return lax.all_to_all(array, axes, split_axis=0, concat_axis=0, tiled=True)  11.6 us
    unnamed x32, local copies, waits for them, and re-layouts  6.16 us
    pallas_call x1, Pallas kernels, per_device(): pl.pallas_call(backward_kernel, grid=(steps,), in_specs=[batch_spec, whol...  4.58 us
  transfers between devices with their start and end apart: 13, of which 10 were waited for; matrix products, arithmetic and copies ran while one was open for 1% of the time, Pallas kernels for 2%

profile of v3, /device:TPU:6, one launch (start us, length us, event | category | flops | bytes accessed | tf_op | source)
XLA Modules:
  0.0 163.2 jit_solution(8538419581246933216)
XLA Ops:
  0.6 0.0 copy-start.1
  0.7 1.0 copy-done.1
  1.7 0.9 table_send.1
  2.6 9.6 %all-to-all-start.1 = ((bf16[32,64,128]{2,1,0:T(8,128)(2,1)}), bf16[32,64,128]{2,1,0:T(8,128)(2,1)S(1)}, u32[]{:S(2)}, u32[]{:S(2)}) async-start(bf16[32,64,128]{2,1,0:T(8,128)(2,1)} %bitcast.15), calls=%async_computation.1 | async-start | bytes 1048576 | tf_op jit(solution)/shard_map/all_to_all | solution.py:274
  12.2 2.2 %pack.1 = (bf16[16,360,128]{2,1,0:T(8,128)(2,1)}, f32[32,128]{1,0:T(8,128)S(1)}) custom-call(s32[3,128]{1,0:T(4,128)S(1)} %bitcast.14, s32[32,128]{1,0:T(8,128)S(1)} %bitcast.11, f32[32,128]{1,0:T(8,128)S(1)} %bitcast.13, bf16[128,4096]{1,0:T(8,128)(2,1)S(1)} %copy-done), custom_call_target="tpu_custom_call" | custom-call | tf_op jit(solution)/shard_map/pack/pallas_call | solution.py:312
  14.4 7.1 %all-to-all-done.1.table_ref = bf16[32,64,128]{2,1,0:T(8,128)(2,1)S(1)} async-done(((bf16[32,64,128]{2,1,0:T(8,128)(2,1)}), bf16[32,64,128]{2,1,0:T(8,128)(2,1)S(1)}, u32[]{:S(2)}, u32[]{:S(2)}) %all-to-all-start.1) | async-done | bytes 524320 | tf_op jit(solution)/shard_map/all_to_all | solution.py:274
  21.4 3.7 %all-to-all-start = ((bf16[16,360,128]{2,1,0:T(8,128)(2,1)}), bf16[16,360,128]{2,1,0:T(8,128)(2,1)S(1)}, u32[]{:S(2)}, u32[]{:S(2)}) async-start(bf16[16,360,128]{2,1,0:T(8,128)(2,1)} %get-tuple-element.62), calls=%async_computation | async-start | bytes 2949120 | tf_op jit(solution)/shard_map/all_to_all | solution.py:274
  25.2 0.8 dynamic_slice.3
  25.9 0.1 copy.15.gain_ref
  26.1 20.4 %all-to-all-done.batch_ref = bf16[16,360,128]{2,1,0:T(8,128)(2,1)S(1)} async-done(((bf16[16,360,128]{2,1,0:T(8,128)(2,1)}), bf16[16,360,128]{2,1,0:T(8,128)(2,1)S(1)}, u32[]{:S(2)}, u32[]{:S(2)}) %all-to-all-start) | async-done | bytes 1474592 | tf_op jit(solution)/shard_map/all_to_all | solution.py:274
  46.5 2.5 %forward.1 = (f32[256,2048]{1,0:T(8,128)S(1)}, f32[16,2,2048]{2,1,0:T(2,128)S(1)}) custom-call(bf16[16,360,128]{2,1,0:T(8,128)(2,1)S(1)} %all-to-all-done.batch_ref, bf16[32,64,128]{2,1,0:T(8,128)(2,1)S(1)} %all-to-all-done.1.table_ref, f32[256,1]{1,0:T(8,128)S(1)} %copy.15.gain_ref), custom_call_target="tpu_custom_call" | custom-call | tf_op jit(solution)/shard_map/forward/pallas_call | solution.py:336
  49.0 11.6 %all_to_all.30.sums_ref = f32[16,2,2048]{2,1,0:T(2,128)S(1)} all-to-all(f32[16,2,2048]{2,1,0:T(2,128)S(1)} %get-tuple-element.64), channel_id=1, replica_groups=mesh['dh'=8,'dl'=2,'x'=4,'yc'=8] {'dl','yc'}, dimensions={0} | all-to-all | bytes 524288 | tf_op jit(solution)/shard_map/all_to_all | solution.py:274
  60.6 4.6 %backward.1 = (bf16[256,2048]{1,0:T(8,128)(2,1)}, bf16[256,2048]{1,0:T(8,128)(2,1)}, bf16[32,72,128]{2,1,0:T(8,128)(2,1)}) custom-call(bf16[16,360,128]{2,1,0:T(8,128)(2,1)S(1)} %all-to-all-done.batch_ref, f32[256,1]{1,0:T(8,128)S(1)} %copy.15.gain_ref, f32[256,2048]{1,0:T(8,128)S(1)} %get-tuple-element.63.memory_ref, f32[16,2,2048]{2,1,0:T(2,128)S(1)} %all_to_all.30.sums_ref), custom_call_target="tpu_custom_call" | custom-call | tf_op jit(solution)/shard_map/backward/pallas_call | solution.py:348
  65.2 1.2 copy-done.3
  66.4 1.2 copy-done.4
  67.6 3.2 %placed_grad.1 = (bf16[8,352,128]{2,1,0:T(8,128)(2,1)S(1)}, bf16[8,352,128]{2,1,0:T(8,128)(2,1)}) custom-call(s32[1]{0:T(128)} %bitcast.place_ref, bf16[16,360,128]{2,1,0:T(8,128)(2,1)S(1)} %all-to-all-done.batch_ref, bf16[32,64,128]{2,1,0:T(8,128)(2,1)S(1)} %all-to-all-done.1.table_ref, bf16[256,2048]{1,0:T(8,128)(2,1)S(1)} %copy-done.3, ...), custom_call_target="tpu_custom_call" | custom-call | tf_op jit(solution)/shard_map/placed_grad/pallas_call | solution.py:366
  70.9 1.9 %collective-permute-start = (bf16[8,352,128]{2,1,0:T(8,128)(2,1)}, bf16[8,352,128]{2,1,0:T(8,128)(2,1)S(1)}, u32[]{:S(2)}, u32[]{:S(2)}) collective-permute-start(bf16[8,352,128]{2,1,0:T(8,128)(2,1)} %get-tuple-element.69), channel_id=1, source_target_pairs={{0,1},{1,0},{2,3},{3,2},{4,5},{5,4},{6,7},{7,6},{32,33},{33,32},{3... | collective-permute-start | bytes 2162696 | tf_op jit(solution)/shard_map/ppermute | solution.py:278
  72.8 5.9 %all-to-all-start.3 = ((bf16[32,72,128]{2,1,0:T(8,128)(2,1)}), bf16[32,72,128]{2,1,0:T(8,128)(2,1)S(1)}, u32[]{:S(2)}, u32[]{:S(2)}) async-start(bf16[32,72,128]{2,1,0:T(8,128)(2,1)} %get-tuple-element.65), calls=%async_computation.3 | async-start | bytes 1179648 | tf_op jit(solution)/shard_map/all_to_all | solution.py:274
  78.7 0.0 collective-permute-done.other_ref
  78.7 0.0 copy-start.2
  78.7 0.0 copy-start.5
  78.7 0.8 merge.1
  79.5 0.7 copy-done.11
  80.1 0.7 copy-done.13
  80.8 0.7 copy-done.14
  81.4 0.7 copy-done.15
  82.1 6.5 %all-to-all-done.3 = bf16[32,72,128]{2,1,0:T(8,128)(2,1)S(1)} async-done(((bf16[32,72,128]{2,1,0:T(8,128)(2,1)}), bf16[32,72,128]{2,1,0:T(8,128)(2,1)S(1)}, u32[]{:S(2)}, u32[]{:S(2)}) %all-to-all-start.3) | async-done | bytes 589856 | tf_op jit(solution)/shard_map/all_to_all | solution.py:274
  88.6 0.7 plane_sum.1
  89.3 13.2 %all-to-all-start.4 = ((bf16[8,72,128]{2,1,0:T(8,128)(2,1)}), bf16[8,72,128]{2,1,0:T(8,128)(2,1)S(1)}, u32[]{:S(2)}, u32[]{:S(2)}) async-start(bf16[8,72,128]{2,1,0:T(8,128)(2,1)} %plane_sum.1), calls=%async_computation.4 | async-start | bytes 294912 | tf_op jit(solution)/shard_map/all_to_all | solution.py:274
  102.5 2.6 %collective-permute-start.1 = (bf16[608,128]{1,0:T(8,128)(2,1)}, bf16[608,128]{1,0:T(8,128)(2,1)S(1)}, u32[]{:S(2)}, u32[]{:S(2)}) collective-permute-start(bf16[608,128]{1,0:T(8,128)(2,1)} %copy-done.15), channel_id=1, source_target_pairs={{0,2},{1,3},{2,0},{3,1},{4,6},{5,7},{6,4},{7,5},{32,34},{33,35},{3... | collective-permute-start | bytes 466952 | tf_op jit(solution)/shard_map/ppermute | solution.py:278
  105.1 4.3 %collective-permute-start.2 = (bf16[608,128]{1,0:T(8,128)(2,1)}, bf16[608,128]{1,0:T(8,128)(2,1)S(1)}, u32[]{:S(2)}, u32[]{:S(2)}) collective-permute-start(bf16[608,128]{1,0:T(8,128)(2,1)} %copy-done.14), channel_id=1, source_target_pairs={{0,4},{1,5},{2,6},{3,7},{4,0},{5,1},{6,2},{7,3},{32,36},{33,37},{3... | collective-permute-start | bytes 466952 | tf_op jit(solution)/shard_map/ppermute | solution.py:278
  109.4 3.5 %collective-permute-start.3 = (bf16[608,128]{1,0:T(8,128)(2,1)}, bf16[608,128]{1,0:T(8,128)(2,1)S(1)}, u32[]{:S(2)}, u32[]{:S(2)}) collective-permute-start(bf16[608,128]{1,0:T(8,128)(2,1)} %copy-done.13), channel_id=1, source_target_pairs={{0,6},{1,7},{2,4},{3,5},{4,2},{5,3},{6,0},{7,1},{32,38},{33,39},{3... | collective-permute-start | bytes 466952 | tf_op jit(solution)/shard_map/ppermute | solution.py:278
  113.0 2.2 %collective-permute-done.2.refs_2_ = bf16[608,128]{1,0:T(8,128)(2,1)S(1)} collective-permute-done((bf16[608,128]{1,0:T(8,128)(2,1)}, bf16[608,128]{1,0:T(8,128)(2,1)S(1)}, u32[]{:S(2)}, u32[]{:S(2)}) %collective-permute-start.2) | collective-permute-done | bytes 155680 | tf_op jit(solution)/shard_map/ppermute | solution.py:278
  115.2 3.3 %collective-permute-done.3.refs_3_ = bf16[608,128]{1,0:T(8,128)(2,1)S(1)} collective-permute-done((bf16[608,128]{1,0:T(8,128)(2,1)}, bf16[608,128]{1,0:T(8,128)(2,1)S(1)}, u32[]{:S(2)}, u32[]{:S(2)}) %collective-permute-start.3) | collective-permute-done | bytes 155680 | tf_op jit(solution)/shard_map/ppermute | solution.py:278
  118.5 1.0 all-to-all-done.4.parts_ref
  119.5 0.7 share_sum.1
  120.3 10.8 %all-to-all-start.5 = ((bf16[16,72,128]{2,1,0:T(8,128)(2,1)}), bf16[16,72,128]{2,1,0:T(8,128)(2,1)S(1)}, u32[]{:S(2)}, u32[]{:S(2)}) async-start(bf16[16,72,128]{2,1,0:T(8,128)(2,1)} %share_sum.1), calls=%async_computation.5 | async-start | bytes 589824 | tf_op jit(solution)/shard_map/all_to_all | solution.py:274
  131.1 3.8 %collective-permute-start.4 = (bf16[608,128]{1,0:T(8,128)(2,1)}, bf16[608,128]{1,0:T(8,128)(2,1)S(1)}, u32[]{:S(2)}, u32[]{:S(2)}) collective-permute-start(bf16[608,128]{1,0:T(8,128)(2,1)} %get-tuple-element.101), channel_id=1, source_target_pairs={{0,32},{1,33},{2,34},{3,35},{4,36},{5,37},{6,38},{7,39},{32,0},{33... | collective-permute-start | bytes 466952 | tf_op jit(solution)/shard_map/ppermute | solution.py:278
  134.9 2.2 %collective-permute-start.5 = (bf16[608,128]{1,0:T(8,128)(2,1)S(1)}, bf16[608,128]{1,0:T(8,128)(2,1)S(1)}, u32[]{:S(2)}, u32[]{:S(2)}) collective-permute-start(bf16[608,128]{1,0:T(8,128)(2,1)S(1)} %copy-done.12), channel_id=1, source_target_pairs={{0,34},{1,35},{2,32},{3,33},{4,38},{5,39},{6,36},{7,37},{32,2},{33... | collective-permute-start | bytes 466952 | tf_op jit(solution)/shard_map/ppermute | solution.py:278
  137.1 5.6 %collective-permute-start.6 = (bf16[608,128]{1,0:T(8,128)(2,1)}, bf16[608,128]{1,0:T(8,128)(2,1)S(1)}, u32[]{:S(2)}, u32[]{:S(2)}) collective-permute-start(bf16[608,128]{1,0:T(8,128)(2,1)} %copy-done.10), channel_id=1, source_target_pairs={{0,36},{1,37},{2,38},{3,39},{4,32},{5,33},{6,34},{7,35},{32,4},{33... | collective-permute-start | bytes 466952 | tf_op jit(solution)/shard_map/ppermute | solution.py:278
  142.7 3.1 %collective-permute-start.7 = (bf16[608,128]{1,0:T(8,128)(2,1)S(1)}, bf16[608,128]{1,0:T(8,128)(2,1)S(1)}, u32[]{:S(2)}, u32[]{:S(2)}) collective-permute-start(bf16[608,128]{1,0:T(8,128)(2,1)S(1)} %get-tuple-element.104), channel_id=1, source_target_pairs={{0,38},{1,39},{2,36},{3,37},{4,34},{5,35},{6,32},{7,33},{32,6},{33... | collective-permute-start | bytes 466952 | tf_op jit(solution)/shard_map/ppermute | solution.py:278
  145.8 3.3 %collective-permute-done.4.refs_4_ = bf16[608,128]{1,0:T(8,128)(2,1)S(1)} collective-permute-done((bf16[608,128]{1,0:T(8,128)(2,1)}, bf16[608,128]{1,0:T(8,128)(2,1)S(1)}, u32[]{:S(2)}, u32[]{:S(2)}) %collective-permute-start.4) | collective-permute-done | bytes 155680 | tf_op jit(solution)/shard_map/ppermute | solution.py:278
  149.2 4.9 %collective-permute-done.5.refs_5_ = bf16[608,128]{1,0:T(8,128)(2,1)S(1)} collective-permute-done((bf16[608,128]{1,0:T(8,128)(2,1)S(1)}, bf16[608,128]{1,0:T(8,128)(2,1)S(1)}, u32[]{:S(2)}, u32[]{:S(2)}) %collective-permute-start.5) | collective-permute-done | bytes 155680 | tf_op jit(solution)/shard_map/ppermute | solution.py:278
  154.0 5.3 %collective-permute-done.6.refs_6_ = bf16[608,128]{1,0:T(8,128)(2,1)S(1)} collective-permute-done((bf16[608,128]{1,0:T(8,128)(2,1)}, bf16[608,128]{1,0:T(8,128)(2,1)S(1)}, u32[]{:S(2)}, u32[]{:S(2)}) %collective-permute-start.6) | collective-permute-done | bytes 155680 | tf_op jit(solution)/shard_map/ppermute | solution.py:278
  159.3 1.2 collective-permute-done.7.refs_7_
  160.5 0.0 all-to-all-done.5.grad_ref
  160.5 1.3 adam.1
  161.9 1.3 unpack.1
  (23 shorter events, 0.0 us)
Async XLA Ops:
  0.6 11.5 %copy-start = (bf16[128,4096]{1,0:T(8,128)(2,1)S(1)}, bf16[128,4096]{1,0:T(8,128)(2,1)}, u32[]{:S(2)}) copy-start(bf16[128,4096]{1,0:T(8,128)(2,1)} %cotangent_ref.1) | copy-start | bytes 3145732
  0.6 1.0 copy-start.1
  1.7 10.4 %copy-start.7 = (s32[128,32]{0,1:T(8,128)S(1)}, s32[128,32]{0,1:T(8,128)}, u32[]{:S(2)}) copy-start(s32[128,32]{0,1:T(8,128)} %param.9) | copy-start | bytes 49156
  1.7 10.5 %copy-start.8 = (f32[128,32]{0,1:T(8,128)S(1)}, f32[128,32]{0,1:T(8,128)}, u32[]{:S(2)}) copy-start(f32[128,32]{0,1:T(8,128)} %param.10) | copy-start | bytes 49156
  1.7 10.5 %copy-start.9 = (s32[128,3]{0,1:T(4,128)S(1)}, s32[128,3]{0,1:T(4,128)}, u32[]{:S(2)}) copy-start(s32[128,3]{0,1:T(4,128)} %param.8) | copy-start | bytes 4612
  2.6 18.9 %all-to-all-start.1 = ((bf16[32,64,128]{2,1,0:T(8,128)(2,1)}), bf16[32,64,128]{2,1,0:T(8,128)(2,1)S(1)}, u32[]{:S(2)}, u32[]{:S(2)}) async-start(bf16[32,64,128]{2,1,0:T(8,128)(2,1)} %bitcast.15), calls=%async_computation.1 | async-start | bytes 1048576 | tf_op jit(solution)/shard_map/all_to_all | solution.py:274
  21.4 25.0 %all-to-all-start = ((bf16[16,360,128]{2,1,0:T(8,128)(2,1)}), bf16[16,360,128]{2,1,0:T(8,128)(2,1)S(1)}, u32[]{:S(2)}, u32[]{:S(2)}) async-start(bf16[16,360,128]{2,1,0:T(8,128)(2,1)} %get-tuple-element.62), calls=%async_computation | async-start | bytes 2949120 | tf_op jit(solution)/shard_map/all_to_all | solution.py:274
  65.2 1.2 copy-start.3
  66.4 1.2 copy-start.4
  70.9 7.8 %collective-permute-start = (bf16[8,352,128]{2,1,0:T(8,128)(2,1)}, bf16[8,352,128]{2,1,0:T(8,128)(2,1)S(1)}, u32[]{:S(2)}, u32[]{:S(2)}) collective-permute-start(bf16[8,352,128]{2,1,0:T(8,128)(2,1)} %get-tuple-element.69), channel_id=1, source_target_pairs={{0,1},{1,0},{2,3},{3,2},{4,5},{5,4},{6,7},{7,6},{32,33},{33,32},{3... | collective-permute-start | bytes 2162696 | tf_op jit(solution)/shard_map/ppermute | solution.py:278
  72.8 15.8 %all-to-all-start.3 = ((bf16[32,72,128]{2,1,0:T(8,128)(2,1)}), bf16[32,72,128]{2,1,0:T(8,128)(2,1)S(1)}, u32[]{:S(2)}, u32[]{:S(2)}) async-start(bf16[32,72,128]{2,1,0:T(8,128)(2,1)} %get-tuple-element.65), calls=%async_computation.3 | async-start | bytes 1179648 | tf_op jit(solution)/shard_map/all_to_all | solution.py:274
  78.7 81.8 %copy-start.2 = (bf16[32,4096]{1,0:T(8,128)(2,1)S(1)}, bf16[32,4096]{1,0:T(8,128)(2,1)}, u32[]{:S(2)}) copy-start(bf16[32,4096]{1,0:T(8,128)(2,1)} %table_ref.3) | copy-start | bytes 786436
  78.7 81.8 %copy-start.5 = (f32[32,4096]{1,0:T(8,128)S(1)}, f32[32,4096]{1,0:T(8,128)}, u32[]{:S(2)}) copy-start(f32[32,4096]{1,0:T(8,128)} %first_ref.1) | copy-start | bytes 1572868
  79.5 0.7 copy-start.11
  80.1 0.7 copy-start.13
  80.8 0.7 copy-start.14
  81.4 0.7 copy-start.15
  82.1 23.0 %copy-start.10 = (bf16[608,128]{1,0:T(8,128)(2,1)}, bf16[608,128]{1,0:T(8,128)(2,1)S(1)}, u32[]{:S(2)}) copy-start(bf16[608,128]{1,0:T(8,128)(2,1)S(1)} %get-tuple-element.103) | copy-start | bytes 466948
  82.1 78.4 %copy-start.6 = (f32[32,4096]{1,0:T(8,128)S(1)}, f32[32,4096]{1,0:T(8,128)}, u32[]{:S(2)}) copy-start(f32[32,4096]{1,0:T(8,128)} %second_ref.1) | copy-start | bytes 1572868
  88.6 46.4 %copy-start.12 = (bf16[608,128]{1,0:T(8,128)(2,1)S(1)}, bf16[608,128]{1,0:T(8,128)(2,1)}, u32[]{:S(2)}) copy-start(bf16[608,128]{1,0:T(8,128)(2,1)} %copy-done.11) | copy-start | bytes 466948
  89.3 30.2 %all-to-all-start.4 = ((bf16[8,72,128]{2,1,0:T(8,128)(2,1)}), bf16[8,72,128]{2,1,0:T(8,128)(2,1)S(1)}, u32[]{:S(2)}, u32[]{:S(2)}) async-start(bf16[8,72,128]{2,1,0:T(8,128)(2,1)} %plane_sum.1), calls=%async_computation.4 | async-start | bytes 294912 | tf_op jit(solution)/shard_map/all_to_all | solution.py:274
  102.5 10.4 %collective-permute-start.1 = (bf16[608,128]{1,0:T(8,128)(2,1)}, bf16[608,128]{1,0:T(8,128)(2,1)S(1)}, u32[]{:S(2)}, u32[]{:S(2)}) collective-permute-start(bf16[608,128]{1,0:T(8,128)(2,1)} %copy-done.15), channel_id=1, source_target_pairs={{0,2},{1,3},{2,0},{3,1},{4,6},{5,7},{6,4},{7,5},{32,34},{33,35},{3... | collective-permute-start | bytes 466952 | tf_op jit(solution)/shard_map/ppermute | solution.py:278
  105.1 10.0 %collective-permute-start.2 = (bf16[608,128]{1,0:T(8,128)(2,1)}, bf16[608,128]{1,0:T(8,128)(2,1)S(1)}, u32[]{:S(2)}, u32[]{:S(2)}) collective-permute-start(bf16[608,128]{1,0:T(8,128)(2,1)} %copy-done.14), channel_id=1, source_target_pairs={{0,4},{1,5},{2,6},{3,7},{4,0},{5,1},{6,2},{7,3},{32,36},{33,37},{3... | collective-permute-start | bytes 466952 | tf_op jit(solution)/shard_map/ppermute | solution.py:278
  109.4 9.1 %collective-permute-start.3 = (bf16[608,128]{1,0:T(8,128)(2,1)}, bf16[608,128]{1,0:T(8,128)(2,1)S(1)}, u32[]{:S(2)}, u32[]{:S(2)}) collective-permute-start(bf16[608,128]{1,0:T(8,128)(2,1)} %copy-done.13), channel_id=1, source_target_pairs={{0,6},{1,7},{2,4},{3,5},{4,2},{5,3},{6,0},{7,1},{32,38},{33,39},{3... | collective-permute-start | bytes 466952 | tf_op jit(solution)/shard_map/ppermute | solution.py:278
  120.3 40.2 %all-to-all-start.5 = ((bf16[16,72,128]{2,1,0:T(8,128)(2,1)}), bf16[16,72,128]{2,1,0:T(8,128)(2,1)S(1)}, u32[]{:S(2)}, u32[]{:S(2)}) async-start(bf16[16,72,128]{2,1,0:T(8,128)(2,1)} %share_sum.1), calls=%async_computation.5 | async-start | bytes 589824 | tf_op jit(solution)/shard_map/all_to_all | solution.py:274
  131.1 18.1 %collective-permute-start.4 = (bf16[608,128]{1,0:T(8,128)(2,1)}, bf16[608,128]{1,0:T(8,128)(2,1)S(1)}, u32[]{:S(2)}, u32[]{:S(2)}) collective-permute-start(bf16[608,128]{1,0:T(8,128)(2,1)} %get-tuple-element.101), channel_id=1, source_target_pairs={{0,32},{1,33},{2,34},{3,35},{4,36},{5,37},{6,38},{7,39},{32,0},{33... | collective-permute-start | bytes 466952 | tf_op jit(solution)/shard_map/ppermute | solution.py:278
  134.9 19.1 %collective-permute-start.5 = (bf16[608,128]{1,0:T(8,128)(2,1)S(1)}, bf16[608,128]{1,0:T(8,128)(2,1)S(1)}, u32[]{:S(2)}, u32[]{:S(2)}) collective-permute-start(bf16[608,128]{1,0:T(8,128)(2,1)S(1)} %copy-done.12), channel_id=1, source_target_pairs={{0,34},{1,35},{2,32},{3,33},{4,38},{5,39},{6,36},{7,37},{32,2},{33... | collective-permute-start | bytes 466952 | tf_op jit(solution)/shard_map/ppermute | solution.py:278
  137.1 22.2 %collective-permute-start.6 = (bf16[608,128]{1,0:T(8,128)(2,1)}, bf16[608,128]{1,0:T(8,128)(2,1)S(1)}, u32[]{:S(2)}, u32[]{:S(2)}) collective-permute-start(bf16[608,128]{1,0:T(8,128)(2,1)} %copy-done.10), channel_id=1, source_target_pairs={{0,36},{1,37},{2,38},{3,39},{4,32},{5,33},{6,34},{7,35},{32,4},{33... | collective-permute-start | bytes 466952 | tf_op jit(solution)/shard_map/ppermute | solution.py:278
  142.7 17.8 %collective-permute-start.7 = (bf16[608,128]{1,0:T(8,128)(2,1)S(1)}, bf16[608,128]{1,0:T(8,128)(2,1)S(1)}, u32[]{:S(2)}, u32[]{:S(2)}) collective-permute-start(bf16[608,128]{1,0:T(8,128)(2,1)S(1)} %get-tuple-element.104), channel_id=1, source_target_pairs={{0,38},{1,39},{2,36},{3,37},{4,34},{5,35},{6,32},{7,33},{32,6},{33... | collective-permute-start | bytes 466952 | tf_op jit(solution)/shard_map/ppermute | solution.py:278

commit v4 on v2

--- a/solution.py
+++ b/solution.py
@@ -54,14 +54,25 @@
     return pltpu.HBM(dims_and_type[:-1], dims_and_type[-1])
 
 
-def table_kernel(place_ref, table_ref, out_ref):
-    del place_ref
-    for b in range(RING):
-        for j in range(TILES):
-            at = b * WIDE + j * L
-            tile = table_ref[:, at : at + L]
-            for x in range(out_ref.shape[0]):
-                out_ref[x, b, j * ROWS : (j + 1) * ROWS, :] = tile
+def table_core_kernel(place_ref, table_ref, same_ref, other_ref):
+    for k in range(RING // 2):
+        for core, out_ref in enumerate((same_ref, other_ref)):
+            block = lax.bitwise_xor(place_ref[2], k) * 2 + lax.bitwise_xor(place_ref[3], core)
+            for j in range(TILES):
+                at = pl.multiple_of(block * WIDE + j * L, L)
+                out_ref[k, j * ROWS : (j + 1) * ROWS, :] = table_ref[:, pl.ds(at, L)]
+
+
+def table_y_kernel(place_ref, same_ref, got_ref, *send_refs):
+    for k, send_ref in enumerate(send_refs):
+        send_ref[place_ref[3]] = same_ref[k]
+        send_ref[1 - place_ref[3]] = got_ref[k]
+
+
+def table_join_kernel(axis, place_ref, *refs):
+    out_ref = refs[-1]
+    for k, part_ref in enumerate(refs[:-1]):
+        out_ref[lax.bitwise_xor(place_ref[axis], k)] = part_ref[...]
 
 
 def pack_kernel(owners_ref, pick_ref, scores_ref, cotangent_ref, send_ref, weights_ref, info_ref):
@@ -144,7 +155,8 @@
     return jnp.concatenate([high, low, jnp.zeros((8 - 2 * TILES, L), F32)], axis=0).astype(BF16)
 
 
-def backward_kernel(batch_ref, gain_ref, memory_ref, sums_ref, out_ref, grad_ref, send_ref, total_ref, gain_sum_ref):
+def backward_kernel(place_ref, batch_ref, gain_ref, memory_ref, sums_ref, out_ref, grad_ref, *refs):
+    send_refs, (total_ref, gain_sum_ref) = refs[:-2], refs[-2:]
     step = pl.program_id(0)
     sums = jnp.sum(sums_ref[...], axis=0)
     inverse = lax.rsqrt(sums[0:1] / D + norm_epsilon)
@@ -172,15 +184,17 @@
 
     @pl.when(step == pl.num_programs(0) - 1)
     def _():
-        for j in range(TILES):
-            send_ref[:, j * ROWS : (j + 1) * ROWS, :] = (
-                total_ref[:, j * L : (j + 1) * L].astype(BF16).reshape(OWNERS, ROWS, L)
-            )
         turned = jnp.transpose(gain_sum_ref[...])
         rows = [jnp.sum(turned[:, j * L : (j + 1) * L], axis=0, keepdims=True) for j in range(TILES)]
         tail = gain_rows(jnp.concatenate(rows, axis=0))
-        for o in range(OWNERS):
-            send_ref[o, GAIN_AT:, :] = tail
+        for k, send_ref in enumerate(send_refs):
+            start = pl.multiple_of(lax.bitwise_xor(place_ref[1], k) * RING * ROWS, RING * ROWS)
+            part = total_ref[pl.ds(start, RING * ROWS), :].astype(BF16)
+            for o in range(RING):
+                for j in range(TILES):
+                    at = o * GAIN_AT + j * ROWS
+                    send_ref[at : at + ROWS, :] = part[o * ROWS : (o + 1) * ROWS, j * L : (j + 1) * L]
+            send_ref[RING * GAIN_AT :, :] = tail
 
 
 def placed_grad_kernel(batch_ref, table_ref, out_ref, grad_ref, send_ref):
@@ -205,26 +219,47 @@
     return total[:GAIN_AT], gain
 
 
-def plane_kernel(parts_ref, send_ref):
-    for b in range(parts_ref.shape[1]):
-        rows, gain = merge(parts_ref[:, b].astype(F32))
-        send_ref[b, :GAIN_AT, :] = rows.astype(BF16)
-        send_ref[b, GAIN_AT:, :] = gain_rows(gain)
+def x_sum_kernel(place_ref, *refs):
+    parts, send_refs = refs[: len(refs) // 2], refs[len(refs) // 2 :]
+    last = sum(part_ref[RING * GAIN_AT :, :].astype(F32) for part_ref in parts)
+    tail = gain_rows(last[:TILES] + last[TILES : 2 * TILES])
+    for k, send_ref in enumerate(send_refs):
+        at = pl.ds(pl.multiple_of(lax.bitwise_xor(place_ref[2], k) * 2 * GAIN_AT, 2 * GAIN_AT), 2 * GAIN_AT)
+        send_ref[: 2 * GAIN_AT, :] = sum(part_ref[at, :].astype(F32) for part_ref in parts).astype(BF16)
+        send_ref[2 * GAIN_AT :, :] = tail
+
+
+def y_join_kernel(place_ref, *refs):
+    parts, (same_ref, other_ref) = refs[:-2], refs[-2:]
+    for k, part_ref in enumerate(parts):
+        for core, out_ref in enumerate((same_ref, other_ref)):
+            start = pl.multiple_of(lax.bitwise_xor(place_ref[3], core) * GAIN_AT, GAIN_AT)
+            out_ref[k, :GAIN_AT, :] = part_ref[pl.ds(start, GAIN_AT), :]
+            out_ref[k, GAIN_AT:, :] = part_ref[2 * GAIN_AT :, :]
+
+
+def plane_kernel(place_ref, same_ref, got_ref, send_ref):
+    for k in range(RING // 2):
+        for core, part_ref in enumerate((same_ref, got_ref)):
+            block = lax.bitwise_xor(place_ref[2], k) * 2 + lax.bitwise_xor(place_ref[3], core)
+            send_ref[block] = part_ref[k]
 
 
 def share_kernel(parts_ref, send_ref):
     rows, gain = merge(parts_ref[...].astype(F32))
-    send_ref[:GAIN_AT, :] = rows.astype(BF16)
-    send_ref[GAIN_AT:, :] = gain_rows(gain)
+    rows = rows.astype(BF16)
+    tail = gain_rows(gain)
+    for b in range(send_ref.shape[0]):
+        send_ref[b, :GAIN_AT, :] = rows
+        send_ref[b, GAIN_AT:, :] = tail
 
 
 def adam_kernel(grad_ref, table_ref, first_ref, second_ref, new_table_ref, new_first_ref, new_second_ref, gain_ref):
-    for z in range(grad_ref.shape[0]):
-        b = (z % PAIR) * RING + z // PAIR
-        tail = grad_ref[z, GAIN_AT:, :].astype(F32)
+    for b in range(grad_ref.shape[0]):
+        tail = grad_ref[b, GAIN_AT:, :].astype(F32)
         for j in range(TILES):
             at = b * WIDE + j * L
-            grad = grad_ref[z, j * ROWS : (j + 1) * ROWS, :].astype(F32)
+            grad = grad_ref[b, j * ROWS : (j + 1) * ROWS, :].astype(F32)
             first = beta_first * first_ref[:, at : at + L] + (1.0 - beta_first) * grad
             second = beta_second * second_ref[:, at : at + L] + (1.0 - beta_second) * grad * grad
             update = learning_rate * (first / first_bias) / (jnp.sqrt(second / second_bias) + adam_epsilon)
@@ -263,6 +298,14 @@
 
 def exchange(array, axes):
     return lax.all_to_all(array, axes, split_axis=0, concat_axis=0, tiled=True)
+
+
+def swaps(array, axis, step):
+    arrays = array if isinstance(array, (list, tuple)) else [array] * 4
+    count = lax.axis_size(axis)
+    return [arrays[0]] + [
+        lax.ppermute(arrays[k], axis, [(i, i ^ (k * step)) for i in range(count)]) for k in range(1, 4)
+    ]
 
 
 def per_device(
@@ -280,21 +323,23 @@
     half = lax.axis_index("dl")
     block_index = half * RING + lax.axis_index("yc")
 
-    whole = lambda *dims: pl.BlockSpec(dims, lambda i: (0,) * len(dims))
-
-    table_send = pl.pallas_call(
-        table_kernel,
-        grid_spec=pltpu.PrefetchScalarGridSpec(
-            num_scalar_prefetch=1,
-            grid=(1,),
-            in_specs=[pl.BlockSpec((ROWS, RING * WIDE), lambda i, place_ref: (0, place_ref[0]))],
-            out_specs=pl.BlockSpec((rows_x, RING, TILES * ROWS, L), lambda i, place_ref: (0, 0, 0, 0)),
-        ),
-        out_shape=in_hbm(rows_x, RING, TILES * ROWS, L, BF16),
-        compiler_params=PARAMS,
-        name="table_send",
-    )(half.reshape(1).astype(jnp.int32), value_table)
-    table = exchange(table_send.reshape(OWNERS, TILES * ROWS, L), ("x", "yc"))
+    yc = lax.axis_index("yc")
+    place_here = jnp.stack([half, lax.axis_index("x"), yc // 2, yc % 2]).astype(jnp.int32)
+    rows_y = RING // 2
+    vmem = pl.BlockSpec(memory_space=pltpu.VMEM)
+    smem = pl.BlockSpec(memory_space=pltpu.SMEM)
+
+    def call(kernel, name, parts, outs):
+        return pl.pallas_call(
+            kernel,
+            in_specs=[smem] + [vmem] * len(parts),
+            out_specs=[vmem] * len(outs),
+            out_shape=outs,
+            compiler_params=PARAMS,
+            name=name,
+        )(place_here, *parts)
+
+    whole = lambda *dims: pl.BlockSpec(dims, lambda i, *refs: (0,) * len(dims))
 
     batch_send, weights = pl.pallas_call(
         pack_kernel,
@@ -303,21 +348,48 @@
             whole(CANDS, TOK),
             whole(PICKS, TOK),
             whole(PICKS, TOK),
-            pl.BlockSpec((TOK, MANY * WIDE), lambda i: (0, i)),
+            pl.BlockSpec((TOK, MANY * WIDE), lambda i, *refs: (0, i)),
         ],
-        out_specs=[pl.BlockSpec((MANY, WIDE + INFO, L), lambda i: (i, 0, 0)), whole(PICKS, TOK)],
+        out_specs=[pl.BlockSpec((MANY, WIDE + INFO, L), lambda i, *refs: (i, 0, 0)), whole(PICKS, TOK)],
         out_shape=(in_hbm(GROUP, WIDE + INFO, L, BF16), shape(PICKS, TOK, F32)),
         scratch_shapes=[pltpu.VMEM((INFO, TOK), BF16)],
         compiler_params=PARAMS,
         name="pack",
     )(owners.T, pick_index.T, key_scores.T, output_cotangent)
+    batch_send, own_rows = lax.optimization_barrier((batch_send, value_table))
     batch = exchange(batch_send, ("dl", "yc"))
+
+    same, other = pl.pallas_call(
+        table_core_kernel,
+        grid_spec=pltpu.PrefetchScalarGridSpec(
+            num_scalar_prefetch=1,
+            grid=(1,),
+            in_specs=[pl.BlockSpec((ROWS, RING * WIDE), lambda i, place_ref: (0, place_ref[0]))],
+            out_specs=[whole(rows_y, GAIN_AT, L)] * 2,
+        ),
+        out_shape=[shape(rows_y, GAIN_AT, L, BF16)] * 2,
+        compiler_params=PARAMS,
+        name="table_core",
+    )(place_here, own_rows)
+    got = lax.ppermute(other, "yc", [(i, i ^ 1) for i in range(RING)])
+    pieces = call(table_y_kernel, "table_y", [same, got], [shape(2, GAIN_AT, L, BF16)] * rows_y)
+    pieces = swaps(pieces, "yc", 2)
+    (table,) = call(
+        functools.partial(table_join_kernel, 2), "table_x", pieces, [shape(rows_y, 2, GAIN_AT, L, BF16)]
+    )
+    (table,) = call(
+        functools.partial(table_join_kernel, 1),
+        "table_all",
+        swaps(table, "x", 1),
+        [shape(rows_x, rows_y, 2, GAIN_AT, L, BF16)],
+    )
+    table = table.reshape(OWNERS, GAIN_AT, L)
     gain = lax.dynamic_slice(norm_gain, (block_index * WIDE,), (WIDE,)).reshape(WIDE, 1)
 
-    batch_spec = pl.BlockSpec((STEP, WIDE + INFO, L), lambda i: (i, 0, 0))
+    batch_spec = pl.BlockSpec((STEP, WIDE + INFO, L), lambda i, *refs: (i, 0, 0))
     table_spec = whole(OWNERS, TILES * ROWS, L)
-    wide_spec = pl.BlockSpec((WIDE, STEP * TOK), lambda i: (0, i))
-    sums_spec = pl.BlockSpec((GROUP, 2, STEP * TOK), lambda i: (0, 0, i))
+    wide_spec = pl.BlockSpec((WIDE, STEP * TOK), lambda i, *refs: (0, i))
+    sums_spec = pl.BlockSpec((GROUP, 2, STEP * TOK), lambda i, *refs: (0, 0, i))
     tokens = GROUP * TOK
 
     memory, sums_send = pl.pallas_call(
@@ -332,55 +404,52 @@
     )(batch, table, gain)
     sums = exchange(sums_send, ("dl", "yc"))
 
-    out_turned, memory_grad, grad_send = pl.pallas_call(
+    out_turned, memory_grad, *pieces = pl.pallas_call(
         backward_kernel,
-        grid=(steps,),
-        in_specs=[batch_spec, whole(WIDE, 1), wide_spec, sums_spec],
-        out_specs=[wide_spec, wide_spec, whole(OWNERS, GRAD, L)],
-        out_shape=(
-            in_hbm(WIDE, tokens, BF16),
-            in_hbm(WIDE, tokens, BF16),
-            in_hbm(OWNERS, GRAD, L, BF16),
+        grid_spec=pltpu.PrefetchScalarGridSpec(
+            num_scalar_prefetch=1,
+            grid=(steps,),
+            in_specs=[batch_spec, whole(WIDE, 1), wide_spec, sums_spec],
+            out_specs=[wide_spec, wide_spec] + [whole(RING * GAIN_AT + 8, L)] * rows_x,
+            scratch_shapes=[pltpu.VMEM((TABLE, WIDE), F32), pltpu.VMEM((WIDE, L), F32)],
         ),
-        scratch_shapes=[pltpu.VMEM((TABLE, WIDE), F32), pltpu.VMEM((WIDE, L), F32)],
+        out_shape=[shape(WIDE, tokens, BF16)] * 2 + [shape(RING * GAIN_AT + 8, L, BF16)] * rows_x,
         compiler_params=PARAMS,
         name="backward",
-    )(batch, gain, memory, sums)
-    plane_parts = exchange(grad_send, ("x", "yc"))
+    )(place_here, batch, gain, memory, sums)
 
     back_send = pl.pallas_call(
         placed_grad_kernel,
         grid=(steps,),
         in_specs=[batch_spec, table_spec, wide_spec, wide_spec],
-        out_specs=pl.BlockSpec((STEP, BACK, L), lambda i: (i, 0, 0)),
+        out_specs=pl.BlockSpec((STEP, BACK, L), lambda i, *refs: (i, 0, 0)),
         out_shape=in_hbm(GROUP, BACK, L, BF16),
         compiler_params=PARAMS,
         name="placed_grad",
     )(batch, table, out_turned, memory_grad)
 
-    plane_parts, back_send = lax.optimization_barrier((plane_parts, back_send))
-    shares_send = pl.pallas_call(
-        plane_kernel,
-        out_shape=shape(RING, GRAD, L, BF16),
-        compiler_params=PARAMS,
-        name="plane_sum",
-    )(plane_parts.reshape(rows_x, RING, GRAD, L))
+    back_send, pieces = lax.optimization_barrier((back_send, pieces))
+    back = exchange(back_send, ("dl", "yc"))
+
+    pieces = call(x_sum_kernel, "x_sum", swaps(pieces, "x", 1), [shape(2 * GAIN_AT + 8, L, BF16)] * rows_y)
+    same, other = call(y_join_kernel, "y_join", swaps(pieces, "yc", 2), [shape(rows_y, GRAD, L, BF16)] * 2)
+    got = lax.ppermute(other, "yc", [(i, i ^ 1) for i in range(RING)])
+    (shares_send,) = call(plane_kernel, "plane_join", [same, got], [shape(RING, GRAD, L, BF16)])
+    shares_send, back = lax.optimization_barrier((shares_send, back))
     shares = exchange(shares_send, "dh")
-    total = pl.pallas_call(
+    total_send = pl.pallas_call(
         share_kernel,
-        out_shape=shape(GRAD, L, BF16),
+        out_shape=shape(GROUP, GRAD, L, BF16),
         compiler_params=PARAMS,
         name="share_sum",
     )(shares)
-    total, back_send = lax.optimization_barrier((total, back_send))
-    totals = lax.all_gather(total, ("dh", "dl"), axis=0, tiled=False)
-
-    back = exchange(back_send, ("dl", "yc"))
+    total = exchange(total_send, ("dl", "dh"))
+
     memory_out, score_turned = pl.pallas_call(
         out_kernel,
         grid=(GROUP // MANY,),
-        in_specs=[pl.BlockSpec((MANY, BACK, L), lambda i: (i, 0, 0)), whole(PICKS, TOK), whole(PICKS, TOK)],
-        out_specs=[pl.BlockSpec((TOK, MANY * WIDE), lambda i: (0, i)), whole(PICKS, TOK)],
+        in_specs=[pl.BlockSpec((MANY, BACK, L), lambda i, *refs: (i, 0, 0)), whole(PICKS, TOK), whole(PICKS, TOK)],
+        out_specs=[pl.BlockSpec((TOK, MANY * WIDE), lambda i, *refs: (0, i)), whole(PICKS, TOK)],
         out_shape=(shape(TOK, D, BF16), shape(PICKS, TOK, F32)),
         scratch_shapes=[pltpu.VMEM((SLOTS, TOK), F32)],
         compiler_params=PARAMS,
@@ -397,7 +466,7 @@
         ),
         compiler_params=PARAMS,
         name="adam",
-    )(totals, value_table, first_moment, second_moment)
+    )(total, value_table, first_moment, second_moment)
     return (memory_out, score_turned.T, gain_gradient.reshape(D), new_table, new_first, new_second)
 
 

time: 163 us -> 168 us (1.031)
  the two profiles are of different devices: /device:TPU:8 before, /device:TPU:64 now
where the time goes in v4:
time: 168 us; the launch traced here: 167 us
  starting transfers between devices  61.1 us (36%)
  waiting for transfers between devices  40.5 us (24%)
  blocking collectives  40.4 us (24%)
  Pallas kernels  20.1 us (12%)
  local copies, waits for them, and re-layouts  4.25 us (3%)
    ppermute x12, starting transfers between devices, swaps(): lax.ppermute(arrays[k], axis, [(i, i ^ k * step) for i in range(count)])  41.1 us
    all_to_all x2, blocking collectives, exchange(): return lax.all_to_all(array, axes, split_axis=0, concat_axis=0, tiled=True)  40.4 us
    ppermute x12, waiting for transfers between devices, swaps(): lax.ppermute(arrays[k], axis, [(i, i ^ k * step) for i in range(count)])  20.7 us
    all_to_all x3, waiting for transfers between devices, exchange(): return lax.all_to_all(array, axes, split_axis=0, concat_axis=0, tiled=True)  17.7 us
    all_to_all x3, starting transfers between devices, exchange(): return lax.all_to_all(array, axes, split_axis=0, concat_axis=0, tiled=True)  15.8 us
    ppermute x2, starting transfers between devices, per_device(): got = lax.ppermute(other, 'yc', [(i, i ^ 1) for i in range(RING)])  4.22 us
    pallas_call x1, Pallas kernels, per_device(): pl.pallas_call(backward_kernel, grid_spec=pltpu.PrefetchScalarGridSpec(nu...  4.21 us
    pallas_call x6, Pallas kernels, call(): pl.pallas_call(kernel, in_specs=[smem] + [vmem] * len(parts), out_specs=[...  3.41 us
  transfers between devices with their start and end apart: 17, of which 12 were waited for; matrix products, arithmetic and copies ran while one was open for 1% of the time, Pallas kernels for 4%

profile of v4, /device:TPU:64, one launch (start us, length us, event | category | flops | bytes accessed | tf_op | source)
XLA Modules:
  0.0 167.4 jit_solution(7148210097527385807)
XLA Ops:
  0.6 1.2 copy-done.1
  1.9 0.7 copy-done.4
  2.6 0.7 copy-done.6
  3.3 0.7 copy-done.7
  4.0 2.2 %pack.1 = (bf16[16,360,128]{2,1,0:T(8,128)(2,1)}, f32[32,128]{1,0:T(8,128)S(1)}) custom-call(s32[3,128]{1,0:T(4,128)S(1)} %bitcast.16, s32[32,128]{1,0:T(8,128)S(1)} %bitcast.13, f32[32,128]{1,0:T(8,128)S(1)} %bitcast.15, bf16[128,4096]{1,0:T(8,128)(2,1)S(1)} %copy-done.1), custom_call_target="tpu_custom_call" | custom-call | tf_op jit(solution)/shard_map/pack/pallas_call | solution.py:344
  6.2 6.1 %all-to-all-start = ((bf16[16,360,128]{2,1,0:T(8,128)(2,1)}), bf16[16,360,128]{2,1,0:T(8,128)(2,1)S(1)}, u32[]{:S(2)}, u32[]{:S(2)}) async-start(bf16[16,360,128]{2,1,0:T(8,128)(2,1)} %get-tuple-element.44), calls=%async_computation | async-start | bytes 2949120 | tf_op jit(solution)/shard_map/all_to_all | solution.py:300
  12.4 0.6 table_core.1
  13.0 2.3 %collective-permute-start = (bf16[4,64,128]{2,1,0:T(8,128)(2,1)S(1)}, bf16[4,64,128]{2,1,0:T(8,128)(2,1)S(1)}, u32[]{:S(2)}, u32[]{:S(2)}) collective-permute-start(bf16[4,64,128]{2,1,0:T(8,128)(2,1)S(1)} %get-tuple-element.47), channel_id=1, source_target_pairs={{0,1},{1,0},{2,3},{3,2},{4,5},{5,4},{6,7},{7,6},{8,9},{9,8},{10,11... | collective-permute-start | bytes 196616 | tf_op jit(solution)/shard_map/ppermute | solution.py:374
  15.3 0.9 collective-permute-done.got_ref
  16.7 3.8 %collective-permute-start.1 = (bf16[2,64,128]{2,1,0:T(8,128)(2,1)S(1)}, bf16[2,64,128]{2,1,0:T(8,128)(2,1)S(1)}, u32[]{:S(2)}, u32[]{:S(2)}) collective-permute-start(bf16[2,64,128]{2,1,0:T(8,128)(2,1)S(1)} %get-tuple-element.49), channel_id=1, source_target_pairs={{0,2},{1,3},{2,0},{3,1},{4,6},{5,7},{6,4},{7,5},{8,10},{9,11},{10,... | collective-permute-start | bytes 98312 | tf_op jit(solution)/shard_map/ppermute | solution.py:307
  20.5 4.6 %collective-permute-start.2 = (bf16[2,64,128]{2,1,0:T(8,128)(2,1)S(1)}, bf16[2,64,128]{2,1,0:T(8,128)(2,1)S(1)}, u32[]{:S(2)}, u32[]{:S(2)}) collective-permute-start(bf16[2,64,128]{2,1,0:T(8,128)(2,1)S(1)} %get-tuple-element.50), channel_id=1, source_target_pairs={{0,4},{1,5},{2,6},{3,7},{4,0},{5,1},{6,2},{7,3},{8,12},{9,13},{10,... | collective-permute-start | bytes 98312 | tf_op jit(solution)/shard_map/ppermute | solution.py:307
  25.1 2.1 %collective-permute-start.3 = (bf16[2,64,128]{2,1,0:T(8,128)(2,1)S(1)}, bf16[2,64,128]{2,1,0:T(8,128)(2,1)S(1)}, u32[]{:S(2)}, u32[]{:S(2)}) collective-permute-start(bf16[2,64,128]{2,1,0:T(8,128)(2,1)S(1)} %get-tuple-element.51), channel_id=1, source_target_pairs={{0,6},{1,7},{2,4},{3,5},{4,2},{5,3},{6,0},{7,1},{8,14},{9,15},{10,... | collective-permute-start | bytes 98312 | tf_op jit(solution)/shard_map/ppermute | solution.py:307
  27.1 4.2 %collective-permute-done.1.refs_1_ = bf16[2,64,128]{2,1,0:T(8,128)(2,1)S(1)} collective-permute-done((bf16[2,64,128]{2,1,0:T(8,128)(2,1)S(1)}, bf16[2,64,128]{2,1,0:T(8,128)(2,1)S(1)}, u32[]{:S(2)}, u32[]{:S(2)}) %collective-permute-start.1) | collective-permute-done | bytes 32800 | tf_op jit(solution)/shard_map/ppermute | solution.py:307
  31.3 1.4 collective-permute-done.2.refs_2_
  32.7 1.4 collective-permute-done.3.refs_3_
  34.1 0.6 table_x.1.refs_0_
  34.7 4.7 %collective-permute-start.6 = (bf16[4,2,64,128]{3,2,1,0:T(8,128)(2,1)S(1)}, bf16[4,2,64,128]{3,2,1,0:T(8,128)(2,1)S(1)}, u32[]{:S(2)}, u32[]{:S(2)}) collective-permute-start(bf16[4,2,64,128]{3,2,1,0:T(8,128)(2,1)S(1)} %table_x.1.refs_0_), channel_id=1, source_target_pairs={{0,24},{8,16},{16,8},{24,0},{1,25},{9,17},{17,9},{25,1},{2,26},{10... | collective-permute-start | bytes 393224 | tf_op jit(solution)/shard_map/ppermute | solution.py:307
  39.4 2.7 %collective-permute-start.5 = (bf16[4,2,64,128]{3,2,1,0:T(8,128)(2,1)S(1)}, bf16[4,2,64,128]{3,2,1,0:T(8,128)(2,1)S(1)}, u32[]{:S(2)}, u32[]{:S(2)}) collective-permute-start(bf16[4,2,64,128]{3,2,1,0:T(8,128)(2,1)S(1)} %table_x.1.refs_0_), channel_id=1, source_target_pairs={{0,16},{8,24},{16,0},{24,8},{1,17},{9,25},{17,1},{25,9},{2,18},{10... | collective-permute-start | bytes 393224 | tf_op jit(solution)/shard_map/ppermute | solution.py:307
  42.1 2.4 %collective-permute-start.4 = (bf16[4,2,64,128]{3,2,1,0:T(8,128)(2,1)S(1)}, bf16[4,2,64,128]{3,2,1,0:T(8,128)(2,1)S(1)}, u32[]{:S(2)}, u32[]{:S(2)}) collective-permute-start(bf16[4,2,64,128]{3,2,1,0:T(8,128)(2,1)S(1)} %table_x.1.refs_0_), channel_id=1, source_target_pairs={{0,8},{8,0},{16,24},{24,16},{1,9},{9,1},{17,25},{25,17},{2,10},{10... | collective-permute-start | bytes 393224 | tf_op jit(solution)/shard_map/ppermute | solution.py:307
  44.5 0.8 dynamic_slice.3
  45.5 2.3 %collective-permute-done.5.refs_2_ = bf16[4,2,64,128]{3,2,1,0:T(8,128)(2,1)S(1)} collective-permute-done((bf16[4,2,64,128]{3,2,1,0:T(8,128)(2,1)S(1)}, bf16[4,2,64,128]{3,2,1,0:T(8,128)(2,1)S(1)}, u32[]{:S(2)}, u32[]{:S(2)}) %collective-permute-start.5) | collective-permute-done | bytes 131104 | tf_op jit(solution)/shard_map/ppermute | solution.py:307
  47.7 1.2 collective-permute-done.4.refs_1_
  48.9 0.6 table_all.1
  49.5 2.6 %forward.1 = (f32[256,2048]{1,0:T(8,128)S(1)}, f32[16,2,2048]{2,1,0:T(2,128)S(1)}) custom-call(bf16[16,360,128]{2,1,0:T(8,128)(2,1)S(1)} %all-to-all-done.batch_ref, bf16[32,64,128]{2,1,0:T(8,128)(2,1)S(1)} %bitcast.11, f32[256,1]{1,0:T(8,128)S(1)} %copy.15.gain_ref), custom_call_target="tpu_custom_call" | custom-call | tf_op jit(solution)/shard_map/forward/pallas_call | solution.py:395
  52.1 12.2 %all_to_all.25.sums_ref = f32[16,2,2048]{2,1,0:T(2,128)S(1)} all-to-all(f32[16,2,2048]{2,1,0:T(2,128)S(1)} %get-tuple-element.53), channel_id=1, replica_groups=mesh['dh'=8,'dl'=2,'x'=4,'yc'=8] {'dl','yc'}, dimensions={0} | all-to-all | bytes 524288 | tf_op jit(solution)/shard_map/all_to_all | solution.py:300
  64.3 4.2 %backward.1 = (bf16[256,2048]{1,0:T(8,128)(2,1)S(1)}, bf16[256,2048]{1,0:T(8,128)(2,1)S(1)}, bf16[520,128]{1,0:T(8,128)(2,1)S(1)}, bf16[520,128]{1,0:T(8,128)(2,...) custom-call(s32[4]{0:T(128)S(1)} %pad_add_fusion.place_ref, ...), custom_call_target="tpu_custom_call" | custom-call | tf_op jit(solution)/shard_map/backward/pallas_call | solution.py:407
  68.5 3.0 %placed_grad.1 = bf16[16,352,128]{2,1,0:T(8,128)(2,1)} custom-call(bf16[16,360,128]{2,1,0:T(8,128)(2,1)S(1)} %all-to-all-done.batch_ref, bf16[32,64,128]{2,1,0:T(8,128)(2,1)S(1)} %bitcast.12, bf16[256,2048]{1,0:T(8,128)(2,1)S(1)} %get-tuple-element.54.out_ref, bf16[256,2048]{1,0:T(8,128)(2,1)S(1)} %get-tuple-element.55.grad_ref), custom_call_target="tpu_custom_call" | custom-call | tf_op jit(solution)/shard_map/placed_grad/pallas_call | solution.py:421
  71.6 3.7 %all-to-all-start.2 = ((bf16[16,352,128]{2,1,0:T(8,128)(2,1)}), bf16[16,352,128]{2,1,0:T(8,128)(2,1)S(1)}, u32[]{:S(2)}, u32[]{:S(2)}) async-start(bf16[16,352,128]{2,1,0:T(8,128)(2,1)} %placed_grad.1), calls=%async_computation.2 | async-start | bytes 2883584 | tf_op jit(solution)/shard_map/all_to_all | solution.py:300
  75.3 3.0 %collective-permute-start.7 = (bf16[520,128]{1,0:T(8,128)(2,1)S(1)}, bf16[520,128]{1,0:T(8,128)(2,1)S(1)}, u32[]{:S(2)}, u32[]{:S(2)}) collective-permute-start(bf16[520,128]{1,0:T(8,128)(2,1)S(1)} %get-tuple-element.61), channel_id=1, source_target_pairs={{0,8},{8,0},{16,24},{24,16},{1,9},{9,1},{17,25},{25,17},{2,10},{10... | collective-permute-start | bytes 399368 | tf_op jit(solution)/shard_map/ppermute | solution.py:307
  78.2 4.6 %collective-permute-start.8 = (bf16[520,128]{1,0:T(8,128)(2,1)S(1)}, bf16[520,128]{1,0:T(8,128)(2,1)S(1)}, u32[]{:S(2)}, u32[]{:S(2)}) collective-permute-start(bf16[520,128]{1,0:T(8,128)(2,1)S(1)} %get-tuple-element.62), channel_id=1, source_target_pairs={{0,16},{8,24},{16,0},{24,8},{1,17},{9,25},{17,1},{25,9},{2,18},{10... | collective-permute-start | bytes 399368 | tf_op jit(solution)/shard_map/ppermute | solution.py:307
  82.9 2.8 %collective-permute-start.9 = (bf16[520,128]{1,0:T(8,128)(2,1)S(1)}, bf16[520,128]{1,0:T(8,128)(2,1)S(1)}, u32[]{:S(2)}, u32[]{:S(2)}) collective-permute-start(bf16[520,128]{1,0:T(8,128)(2,1)S(1)} %get-tuple-element.63), channel_id=1, source_target_pairs={{0,24},{8,16},{16,8},{24,0},{1,25},{9,17},{17,9},{25,1},{2,26},{10... | collective-permute-start | bytes 399368 | tf_op jit(solution)/shard_map/ppermute | solution.py:307
  85.7 1.8 %collective-permute-done.8.refs_2_ = bf16[520,128]{1,0:T(8,128)(2,1)S(1)} collective-permute-done((bf16[520,128]{1,0:T(8,128)(2,1)S(1)}, bf16[520,128]{1,0:T(8,128)(2,1)S(1)}, u32[]{:S(2)}, u32[]{:S(2)}) %collective-permute-start.8) | collective-permute-done | bytes 133152 | tf_op jit(solution)/shard_map/ppermute | solution.py:307
  87.5 3.7 %collective-permute-done.9.refs_3_ = bf16[520,128]{1,0:T(8,128)(2,1)S(1)} collective-permute-done((bf16[520,128]{1,0:T(8,128)(2,1)S(1)}, bf16[520,128]{1,0:T(8,128)(2,1)S(1)}, u32[]{:S(2)}, u32[]{:S(2)}) %collective-permute-start.9) | collective-permute-done | bytes 133152 | tf_op jit(solution)/shard_map/ppermute | solution.py:307
  91.2 0.6 x_sum.1
  91.8 3.6 %collective-permute-start.10 = (bf16[136,128]{1,0:T(8,128)(2,1)S(1)}, bf16[136,128]{1,0:T(8,128)(2,1)S(1)}, u32[]{:S(2)}, u32[]{:S(2)}) collective-permute-start(bf16[136,128]{1,0:T(8,128)(2,1)S(1)} %get-tuple-element.65), channel_id=1, source_target_pairs={{0,2},{1,3},{2,0},{3,1},{4,6},{5,7},{6,4},{7,5},{8,10},{9,11},{10,... | collective-permute-start | bytes 104456 | tf_op jit(solution)/shard_map/ppermute | solution.py:307
  95.4 4.6 %collective-permute-start.11 = (bf16[136,128]{1,0:T(8,128)(2,1)S(1)}, bf16[136,128]{1,0:T(8,128)(2,1)S(1)}, u32[]{:S(2)}, u32[]{:S(2)}) collective-permute-start(bf16[136,128]{1,0:T(8,128)(2,1)S(1)} %get-tuple-element.66), channel_id=1, source_target_pairs={{0,4},{1,5},{2,6},{3,7},{4,0},{5,1},{6,2},{7,3},{8,12},{9,13},{10,... | collective-permute-start | bytes 104456 | tf_op jit(solution)/shard_map/ppermute | solution.py:307
  100.0 2.2 %collective-permute-start.12 = (bf16[136,128]{1,0:T(8,128)(2,1)S(1)}, bf16[136,128]{1,0:T(8,128)(2,1)S(1)}, u32[]{:S(2)}, u32[]{:S(2)}) collective-permute-start(bf16[136,128]{1,0:T(8,128)(2,1)S(1)} %get-tuple-element.67), channel_id=1, source_target_pairs={{0,6},{1,7},{2,4},{3,5},{4,2},{5,3},{6,0},{7,1},{8,14},{9,15},{10,... | collective-permute-start | bytes 104456 | tf_op jit(solution)/shard_map/ppermute | solution.py:307
  102.7 4.3 %collective-permute-done.12.refs_3_ = bf16[136,128]{1,0:T(8,128)(2,1)S(1)} collective-permute-done((bf16[136,128]{1,0:T(8,128)(2,1)S(1)}, bf16[136,128]{1,0:T(8,128)(2,1)S(1)}, u32[]{:S(2)}, u32[]{:S(2)}) %collective-permute-start.12) | collective-permute-done | bytes 34848 | tf_op jit(solution)/shard_map/ppermute | solution.py:307
  107.0 0.6 y_join.1
  107.6 1.9 %collective-permute-start.13 = (bf16[4,72,128]{2,1,0:T(8,128)(2,1)S(1)}, bf16[4,72,128]{2,1,0:T(8,128)(2,1)S(1)}, u32[]{:S(2)}, u32[]{:S(2)}) collective-permute-start(bf16[4,72,128]{2,1,0:T(8,128)(2,1)S(1)} %get-tuple-element.69), channel_id=1, source_target_pairs={{0,1},{1,0},{2,3},{3,2},{4,5},{5,4},{6,7},{7,6},{8,9},{9,8},{10,11... | collective-permute-start | bytes 221192 | tf_op jit(solution)/shard_map/ppermute | solution.py:436
  109.5 1.2 collective-permute-done.13.got_ref
  110.7 0.6 plane_join.1
  111.3 28.2 %all_to_all.26.parts_ref = bf16[8,72,128]{2,1,0:T(8,128)(2,1)S(1)} all-to-all(bf16[8,72,128]{2,1,0:T(8,128)(2,1)S(1)} %plane_join.1), channel_id=1, replica_groups=mesh['dh'=8,'dl'=2,'x'=4,'yc'=8] {'dh'}, dimensions={0} | all-to-all | bytes 294912 | tf_op jit(solution)/shard_map/all_to_all | solution.py:300
  139.6 0.7 share_sum.1
  140.3 6.1 %all-to-all-start.4 = ((bf16[16,72,128]{2,1,0:T(8,128)(2,1)}), bf16[16,72,128]{2,1,0:T(8,128)(2,1)S(1)}, u32[]{:S(2)}, u32[]{:S(2)}) async-start(bf16[16,72,128]{2,1,0:T(8,128)(2,1)} %share_sum.1), calls=%async_computation.4 | async-start | bytes 589824 | tf_op jit(solution)/shard_map/all_to_all | solution.py:300
  146.4 2.0 %unpack.1 = (bf16[128,4096]{1,0:T(8,128)(2,1)}, f32[32,128]{1,0:T(8,128)}) custom-call(bf16[16,352,128]{2,1,0:T(8,128)(2,1)S(1)} %all-to-all-done.2.parts_ref, s32[32,128]{1,0:T(8,128)S(1)} %bitcast.14, f32[32,128]{1,0:T(8,128)S(1)} %get-tuple-element.72.weights_ref), custom_call_target="tpu_custom_call" | custom-call | tf_op jit(solution)/shard_map/unpack/pallas_call | solution.py:448
  148.3 17.7 %all-to-all-done.4.grad_ref = bf16[16,72,128]{2,1,0:T(8,128)(2,1)S(1)} async-done(((bf16[16,72,128]{2,1,0:T(8,128)(2,1)}), bf16[16,72,128]{2,1,0:T(8,128)(2,1)S(1)}, u32[]{:S(2)}, u32[]{:S(2)}) %all-to-all-start.4) | async-done | bytes 294944 | tf_op jit(solution)/shard_map/all_to_all | solution.py:300
  166.0 1.3 adam.1
  (21 shorter events, 1.3 us)
Async XLA Ops:
  0.6 1.2 copy-start.1
  1.9 0.7 copy-start.4
  2.6 0.7 copy-start.6
  3.3 0.7 copy-start.7
  6.2 6.2 %copy-start = (bf16[32,4096]{1,0:T(8,128)(2,1)S(1)}, bf16[32,4096]{1,0:T(8,128)(2,1)}, u32[]{:S(2)}) copy-start(bf16[32,4096]{1,0:T(8,128)(2,1)} %table_ref.2) | copy-start | bytes 786436
  6.2 43.3 %all-to-all-start = ((bf16[16,360,128]{2,1,0:T(8,128)(2,1)}), bf16[16,360,128]{2,1,0:T(8,128)(2,1)S(1)}, u32[]{:S(2)}, u32[]{:S(2)}) async-start(bf16[16,360,128]{2,1,0:T(8,128)(2,1)} %get-tuple-element.44), calls=%async_computation | async-start | bytes 2949120 | tf_op jit(solution)/shard_map/all_to_all | solution.py:300
  13.0 3.2 %collective-permute-start = (bf16[4,64,128]{2,1,0:T(8,128)(2,1)S(1)}, bf16[4,64,128]{2,1,0:T(8,128)(2,1)S(1)}, u32[]{:S(2)}, u32[]{:S(2)}) collective-permute-start(bf16[4,64,128]{2,1,0:T(8,128)(2,1)S(1)} %get-tuple-element.47), channel_id=1, source_target_pairs={{0,1},{1,0},{2,3},{3,2},{4,5},{5,4},{6,7},{7,6},{8,9},{9,8},{10,11... | collective-permute-start | bytes 196616 | tf_op jit(solution)/shard_map/ppermute | solution.py:374
  16.7 14.6 %collective-permute-start.1 = (bf16[2,64,128]{2,1,0:T(8,128)(2,1)S(1)}, bf16[2,64,128]{2,1,0:T(8,128)(2,1)S(1)}, u32[]{:S(2)}, u32[]{:S(2)}) collective-permute-start(bf16[2,64,128]{2,1,0:T(8,128)(2,1)S(1)} %get-tuple-element.49), channel_id=1, source_target_pairs={{0,2},{1,3},{2,0},{3,1},{4,6},{5,7},{6,4},{7,5},{8,10},{9,11},{10,... | collective-permute-start | bytes 98312 | tf_op jit(solution)/shard_map/ppermute | solution.py:307
  20.5 12.2 %collective-permute-start.2 = (bf16[2,64,128]{2,1,0:T(8,128)(2,1)S(1)}, bf16[2,64,128]{2,1,0:T(8,128)(2,1)S(1)}, u32[]{:S(2)}, u32[]{:S(2)}) collective-permute-start(bf16[2,64,128]{2,1,0:T(8,128)(2,1)S(1)} %get-tuple-element.50), channel_id=1, source_target_pairs={{0,4},{1,5},{2,6},{3,7},{4,0},{5,1},{6,2},{7,3},{8,12},{9,13},{10,... | collective-permute-start | bytes 98312 | tf_op jit(solution)/shard_map/ppermute | solution.py:307
  25.1 9.0 %collective-permute-start.3 = (bf16[2,64,128]{2,1,0:T(8,128)(2,1)S(1)}, bf16[2,64,128]{2,1,0:T(8,128)(2,1)S(1)}, u32[]{:S(2)}, u32[]{:S(2)}) collective-permute-start(bf16[2,64,128]{2,1,0:T(8,128)(2,1)S(1)} %get-tuple-element.51), channel_id=1, source_target_pairs={{0,6},{1,7},{2,4},{3,5},{4,2},{5,3},{6,0},{7,1},{8,14},{9,15},{10,... | collective-permute-start | bytes 98312 | tf_op jit(solution)/shard_map/ppermute | solution.py:307
  34.7 10.8 %collective-permute-start.6 = (bf16[4,2,64,128]{3,2,1,0:T(8,128)(2,1)S(1)}, bf16[4,2,64,128]{3,2,1,0:T(8,128)(2,1)S(1)}, u32[]{:S(2)}, u32[]{:S(2)}) collective-permute-start(bf16[4,2,64,128]{3,2,1,0:T(8,128)(2,1)S(1)} %table_x.1.refs_0_), channel_id=1, source_target_pairs={{0,24},{8,16},{16,8},{24,0},{1,25},{9,17},{17,9},{25,1},{2,26},{10... | collective-permute-start | bytes 393224 | tf_op jit(solution)/shard_map/ppermute | solution.py:307
  39.4 8.4 %collective-permute-start.5 = (bf16[4,2,64,128]{3,2,1,0:T(8,128)(2,1)S(1)}, bf16[4,2,64,128]{3,2,1,0:T(8,128)(2,1)S(1)}, u32[]{:S(2)}, u32[]{:S(2)}) collective-permute-start(bf16[4,2,64,128]{3,2,1,0:T(8,128)(2,1)S(1)} %table_x.1.refs_0_), channel_id=1, source_target_pairs={{0,16},{8,24},{16,0},{24,8},{1,17},{9,25},{17,1},{25,9},{2,18},{10... | collective-permute-start | bytes 393224 | tf_op jit(solution)/shard_map/ppermute | solution.py:307
  42.1 6.9 %collective-permute-start.4 = (bf16[4,2,64,128]{3,2,1,0:T(8,128)(2,1)S(1)}, bf16[4,2,64,128]{3,2,1,0:T(8,128)(2,1)S(1)}, u32[]{:S(2)}, u32[]{:S(2)}) collective-permute-start(bf16[4,2,64,128]{3,2,1,0:T(8,128)(2,1)S(1)} %table_x.1.refs_0_), channel_id=1, source_target_pairs={{0,8},{8,0},{16,24},{24,16},{1,9},{9,1},{17,25},{25,17},{2,10},{10... | collective-permute-start | bytes 393224 | tf_op jit(solution)/shard_map/ppermute | solution.py:307
  71.6 39.8 %all-to-all-start.2 = ((bf16[16,352,128]{2,1,0:T(8,128)(2,1)}), bf16[16,352,128]{2,1,0:T(8,128)(2,1)S(1)}, u32[]{:S(2)}, u32[]{:S(2)}) async-start(bf16[16,352,128]{2,1,0:T(8,128)(2,1)} %placed_grad.1), calls=%async_computation.2 | async-start | bytes 2883584 | tf_op jit(solution)/shard_map/all_to_all | solution.py:300
  75.3 71.1 %copy-start.5 = (s32[128,32]{0,1:T(8,128)S(1)}, s32[128,32]{0,1:T(8,128)}, u32[]{:S(2)}) copy-start(s32[128,32]{0,1:T(8,128)} %param.9) | copy-start | bytes 49156
  75.3 10.4 %collective-permute-start.7 = (bf16[520,128]{1,0:T(8,128)(2,1)S(1)}, bf16[520,128]{1,0:T(8,128)(2,1)S(1)}, u32[]{:S(2)}, u32[]{:S(2)}) collective-permute-start(bf16[520,128]{1,0:T(8,128)(2,1)S(1)} %get-tuple-element.61), channel_id=1, source_target_pairs={{0,8},{8,0},{16,24},{24,16},{1,9},{9,1},{17,25},{25,17},{2,10},{10... | collective-permute-start | bytes 399368 | tf_op jit(solution)/shard_map/ppermute | solution.py:307
  78.2 9.3 %collective-permute-start.8 = (bf16[520,128]{1,0:T(8,128)(2,1)S(1)}, bf16[520,128]{1,0:T(8,128)(2,1)S(1)}, u32[]{:S(2)}, u32[]{:S(2)}) collective-permute-start(bf16[520,128]{1,0:T(8,128)(2,1)S(1)} %get-tuple-element.62), channel_id=1, source_target_pairs={{0,16},{8,24},{16,0},{24,8},{1,17},{9,25},{17,1},{25,9},{2,18},{10... | collective-permute-start | bytes 399368 | tf_op jit(solution)/shard_map/ppermute | solution.py:307
  82.9 8.3 %collective-permute-start.9 = (bf16[520,128]{1,0:T(8,128)(2,1)S(1)}, bf16[520,128]{1,0:T(8,128)(2,1)S(1)}, u32[]{:S(2)}, u32[]{:S(2)}) collective-permute-start(bf16[520,128]{1,0:T(8,128)(2,1)S(1)} %get-tuple-element.63), channel_id=1, source_target_pairs={{0,24},{8,16},{16,8},{24,0},{1,25},{9,17},{17,9},{25,1},{2,26},{10... | collective-permute-start | bytes 399368 | tf_op jit(solution)/shard_map/ppermute | solution.py:307
  91.8 10.4 %collective-permute-start.10 = (bf16[136,128]{1,0:T(8,128)(2,1)S(1)}, bf16[136,128]{1,0:T(8,128)(2,1)S(1)}, u32[]{:S(2)}, u32[]{:S(2)}) collective-permute-start(bf16[136,128]{1,0:T(8,128)(2,1)S(1)} %get-tuple-element.65), channel_id=1, source_target_pairs={{0,2},{1,3},{2,0},{3,1},{4,6},{5,7},{6,4},{7,5},{8,10},{9,11},{10,... | collective-permute-start | bytes 104456 | tf_op jit(solution)/shard_map/ppermute | solution.py:307
  95.4 7.3 %collective-permute-start.11 = (bf16[136,128]{1,0:T(8,128)(2,1)S(1)}, bf16[136,128]{1,0:T(8,128)(2,1)S(1)}, u32[]{:S(2)}, u32[]{:S(2)}) collective-permute-start(bf16[136,128]{1,0:T(8,128)(2,1)S(1)} %get-tuple-element.66), channel_id=1, source_target_pairs={{0,4},{1,5},{2,6},{3,7},{4,0},{5,1},{6,2},{7,3},{8,12},{9,13},{10,... | collective-permute-start | bytes 104456 | tf_op jit(solution)/shard_map/ppermute | solution.py:307
  100.0 7.0 %collective-permute-start.12 = (bf16[136,128]{1,0:T(8,128)(2,1)S(1)}, bf16[136,128]{1,0:T(8,128)(2,1)S(1)}, u32[]{:S(2)}, u32[]{:S(2)}) collective-permute-start(bf16[136,128]{1,0:T(8,128)(2,1)S(1)} %get-tuple-element.67), channel_id=1, source_target_pairs={{0,6},{1,7},{2,4},{3,5},{4,2},{5,3},{6,0},{7,1},{8,14},{9,15},{10,... | collective-permute-start | bytes 104456 | tf_op jit(solution)/shard_map/ppermute | solution.py:307
  107.6 3.2 %collective-permute-start.13 = (bf16[4,72,128]{2,1,0:T(8,128)(2,1)S(1)}, bf16[4,72,128]{2,1,0:T(8,128)(2,1)S(1)}, u32[]{:S(2)}, u32[]{:S(2)}) collective-permute-start(bf16[4,72,128]{2,1,0:T(8,128)(2,1)S(1)} %get-tuple-element.69), channel_id=1, source_target_pairs={{0,1},{1,0},{2,3},{3,2},{4,5},{5,4},{6,7},{7,6},{8,9},{9,8},{10,11... | collective-permute-start | bytes 221192 | tf_op jit(solution)/shard_map/ppermute | solution.py:436
  111.3 54.7 %copy-start.2 = (f32[32,4096]{1,0:T(8,128)S(1)}, f32[32,4096]{1,0:T(8,128)}, u32[]{:S(2)}) copy-start(f32[32,4096]{1,0:T(8,128)} %first_ref.1) | copy-start | bytes 1572868
  111.3 54.7 %copy-start.3 = (f32[32,4096]{1,0:T(8,128)S(1)}, f32[32,4096]{1,0:T(8,128)}, u32[]{:S(2)}) copy-start(f32[32,4096]{1,0:T(8,128)} %second_ref.1) | copy-start | bytes 1572868
  140.3 25.7 %all-to-all-start.4 = ((bf16[16,72,128]{2,1,0:T(8,128)(2,1)}), bf16[16,72,128]{2,1,0:T(8,128)(2,1)S(1)}, u32[]{:S(2)}, u32[]{:S(2)}) async-start(bf16[16,72,128]{2,1,0:T(8,128)(2,1)} %share_sum.1), calls=%async_computation.4 | async-start | bytes 589824 | tf_op jit(solution)/shard_map/all_to_all | solution.py:300

commit v5 on v2

--- a/solution.py
+++ b/solution.py
@@ -36,6 +36,8 @@
 BACK = WIDE + SLOTS
 STEP = 4
 MANY = 4
+PLANE = ("xh", "xl", "yc")
+TEAM = ("xl", "yc")
 VMEM_LIMIT = 32 * 1024 * 1024
 F32 = jnp.float32
 BF16 = jnp.bfloat16
@@ -54,9 +56,8 @@
     return pltpu.HBM(dims_and_type[:-1], dims_and_type[-1])
 
 
-def table_kernel(place_ref, table_ref, out_ref):
-    del place_ref
-    for b in range(RING):
+def table_kernel(table_ref, out_ref):
+    for b in range(GROUP):
         for j in range(TILES):
             at = b * WIDE + j * L
             tile = table_ref[:, at : at + L]
@@ -219,12 +220,11 @@
 
 
 def adam_kernel(grad_ref, table_ref, first_ref, second_ref, new_table_ref, new_first_ref, new_second_ref, gain_ref):
-    for z in range(grad_ref.shape[0]):
-        b = (z % PAIR) * RING + z // PAIR
-        tail = grad_ref[z, GAIN_AT:, :].astype(F32)
+    for b in range(grad_ref.shape[0]):
+        tail = grad_ref[b, GAIN_AT:, :].astype(F32)
         for j in range(TILES):
             at = b * WIDE + j * L
-            grad = grad_ref[z, j * ROWS : (j + 1) * ROWS, :].astype(F32)
+            grad = grad_ref[b, j * ROWS : (j + 1) * ROWS, :].astype(F32)
             first = beta_first * first_ref[:, at : at + L] + (1.0 - beta_first) * grad
             second = beta_second * second_ref[:, at : at + L] + (1.0 - beta_second) * grad * grad
             update = learning_rate * (first / first_bias) / (jnp.sqrt(second / second_bias) + adam_epsilon)
@@ -275,26 +275,19 @@
     second_moment,
     norm_gain,
 ):
-    rows_x = lax.axis_size("x")
+    groups = lax.axis_size("xh")
     steps = GROUP // STEP
-    half = lax.axis_index("dl")
-    block_index = half * RING + lax.axis_index("yc")
+    block_index = lax.axis_index(TEAM)
 
     whole = lambda *dims: pl.BlockSpec(dims, lambda i: (0,) * len(dims))
 
     table_send = pl.pallas_call(
         table_kernel,
-        grid_spec=pltpu.PrefetchScalarGridSpec(
-            num_scalar_prefetch=1,
-            grid=(1,),
-            in_specs=[pl.BlockSpec((ROWS, RING * WIDE), lambda i, place_ref: (0, place_ref[0]))],
-            out_specs=pl.BlockSpec((rows_x, RING, TILES * ROWS, L), lambda i, place_ref: (0, 0, 0, 0)),
-        ),
-        out_shape=in_hbm(rows_x, RING, TILES * ROWS, L, BF16),
+        out_shape=in_hbm(groups, GROUP, TILES * ROWS, L, BF16),
         compiler_params=PARAMS,
         name="table_send",
-    )(half.reshape(1).astype(jnp.int32), value_table)
-    table = exchange(table_send.reshape(OWNERS, TILES * ROWS, L), ("x", "yc"))
+    )(value_table)
+    table = exchange(table_send.reshape(OWNERS, TILES * ROWS, L), PLANE)
 
     batch_send, weights = pl.pallas_call(
         pack_kernel,
@@ -311,7 +304,7 @@
         compiler_params=PARAMS,
         name="pack",
     )(owners.T, pick_index.T, key_scores.T, output_cotangent)
-    batch = exchange(batch_send, ("dl", "yc"))
+    batch = exchange(batch_send, TEAM)
     gain = lax.dynamic_slice(norm_gain, (block_index * WIDE,), (WIDE,)).reshape(WIDE, 1)
 
     batch_spec = pl.BlockSpec((STEP, WIDE + INFO, L), lambda i: (i, 0, 0))
@@ -330,7 +323,7 @@
         compiler_params=PARAMS,
         name="forward",
     )(batch, table, gain)
-    sums = exchange(sums_send, ("dl", "yc"))
+    sums = exchange(sums_send, TEAM)
 
     out_turned, memory_grad, grad_send = pl.pallas_call(
         backward_kernel,
@@ -346,7 +339,7 @@
         compiler_params=PARAMS,
         name="backward",
     )(batch, gain, memory, sums)
-    plane_parts = exchange(grad_send, ("x", "yc"))
+    plane_parts = exchange(grad_send, PLANE)
 
     back_send = pl.pallas_call(
         placed_grad_kernel,
@@ -361,11 +354,11 @@
     plane_parts, back_send = lax.optimization_barrier((plane_parts, back_send))
     shares_send = pl.pallas_call(
         plane_kernel,
-        out_shape=shape(RING, GRAD, L, BF16),
+        out_shape=shape(GROUP, GRAD, L, BF16),
         compiler_params=PARAMS,
         name="plane_sum",
-    )(plane_parts.reshape(rows_x, RING, GRAD, L))
-    shares = exchange(shares_send, "dh")
+    )(plane_parts.reshape(groups, GROUP, GRAD, L))
+    shares = exchange(shares_send, "dp")
     total = pl.pallas_call(
         share_kernel,
         out_shape=shape(GRAD, L, BF16),
@@ -373,9 +366,9 @@
         name="share_sum",
     )(shares)
     total, back_send = lax.optimization_barrier((total, back_send))
-    totals = lax.all_gather(total, ("dh", "dl"), axis=0, tiled=False)
-
-    back = exchange(back_send, ("dl", "yc"))
+    totals = lax.all_gather(total, "dp", axis=0, tiled=False)
+
+    back = exchange(back_send, TEAM)
     memory_out, score_turned = pl.pallas_call(
         out_kernel,
         grid=(GROUP // MANY,),
@@ -403,11 +396,9 @@
 
 def solution(mesh):
     planes, mem_count = mesh.shape["dp"], mesh.shape["mem"]
-    split_mesh = Mesh(
-        mesh.devices.reshape(planes // PAIR, PAIR, mem_count // RING, RING), ("dh", "dl", "x", "yc")
-    )
-    tokens = P(("dh", "dl", "x", "yc"), None)
-    rows = P(("x", "yc"), None)
+    split_mesh = Mesh(mesh.devices.reshape(planes, mem_count // GROUP, PAIR, RING), ("dp",) + PLANE)
+    tokens = P(("dp",) + PLANE, None)
+    rows = P(PLANE, None)
     return jax.shard_map(
         per_device,
         mesh=split_mesh,

time: 163 us -> 156 us (0.957)
  the two profiles are of different devices: /device:TPU:8 before, /device:TPU:6 now
where the time goes in v5:
time: 156 us; the launch traced here: 154 us
  blocking collectives  76.8 us (49%)
  waiting for transfers between devices  30.4 us (19%)
  starting transfers between devices  25.1 us (16%)
  Pallas kernels  16.7 us (11%)
  local copies, waits for them, and re-layouts  4.32 us (3%)
    all_to_all x2, blocking collectives, exchange(): return lax.all_to_all(array, axes, split_axis=0, concat_axis=0, tiled=True)  45.1 us
    all_gather x1, blocking collectives, per_device(): totals = lax.all_gather(total, 'dp', axis=0, tiled=False)  31.7 us
    all_to_all x4, waiting for transfers between devices, exchange(): return lax.all_to_all(array, axes, split_axis=0, concat_axis=0, tiled=True)  30.4 us
    all_to_all x4, starting transfers between devices, exchange(): return lax.all_to_all(array, axes, split_axis=0, concat_axis=0, tiled=True)  25.1 us
    pallas_call x1, Pallas kernels, per_device(): pl.pallas_call(backward_kernel, grid=(steps,), in_specs=[batch_spec, whol...  4.59 us
    unnamed x20, local copies, waits for them, and re-layouts  3.42 us
  transfers between devices with their start and end apart: 4, of which 3 were waited for; matrix products, arithmetic and copies ran while one was open for 1% of the time, Pallas kernels for 4%

profile of v5, /device:TPU:6, one launch (start us, length us, event | category | flops | bytes accessed | tf_op | source)
XLA Modules:
  0.0 154.1 jit_solution(15670164279830786901)
XLA Ops:
  0.6 0.0 copy-start
  0.6 0.9 copy-done
  1.6 0.0 copy-start.2
  1.6 0.0 copy-start.7
  1.6 0.0 copy-start.8
  1.6 0.0 copy-start.9
  1.6 0.9 table_send.1
  2.5 9.6 %all-to-all-start.1 = ((bf16[32,64,128]{2,1,0:T(8,128)(2,1)}), bf16[32,64,128]{2,1,0:T(8,128)(2,1)S(1)}, u32[]{:S(2)}, u32[]{:S(2)}) async-start(bf16[32,64,128]{2,1,0:T(8,128)(2,1)} %bitcast.15), calls=%async_computation.1 | async-start | bytes 1048576 | tf_op jit(solution)/shard_map/all_to_all | solution.py:265
  12.0 0.0 copy-done.2
  12.0 0.0 copy-done.7
  12.0 0.0 copy-done.8
  12.0 0.0 copy-done.9
  12.1 2.2 %pack.1 = (bf16[16,360,128]{2,1,0:T(8,128)(2,1)}, f32[32,128]{1,0:T(8,128)S(1)}) custom-call(s32[3,128]{1,0:T(4,128)S(1)} %bitcast.14, s32[32,128]{1,0:T(8,128)S(1)} %bitcast.11, f32[32,128]{1,0:T(8,128)S(1)} %bitcast.13, bf16[128,4096]{1,0:T(8,128)(2,1)S(1)} %copy-done.2), custom_call_target="tpu_custom_call" | custom-call | tf_op jit(solution)/shard_map/pack/pallas_call | solution.py:292
  14.3 7.1 %all-to-all-done.1.table_ref = bf16[32,64,128]{2,1,0:T(8,128)(2,1)S(1)} async-done(((bf16[32,64,128]{2,1,0:T(8,128)(2,1)}), bf16[32,64,128]{2,1,0:T(8,128)(2,1)S(1)}, u32[]{:S(2)}, u32[]{:S(2)}) %all-to-all-start.1) | async-done | bytes 524320 | tf_op jit(solution)/shard_map/all_to_all | solution.py:265
  21.3 4.5 %all-to-all-start = ((bf16[16,360,128]{2,1,0:T(8,128)(2,1)}), bf16[16,360,128]{2,1,0:T(8,128)(2,1)S(1)}, u32[]{:S(2)}, u32[]{:S(2)}) async-start(bf16[16,360,128]{2,1,0:T(8,128)(2,1)} %get-tuple-element.23), calls=%async_computation | async-start | bytes 2949120 | tf_op jit(solution)/shard_map/all_to_all | solution.py:265
  25.9 0.8 dynamic_slice.3
  26.6 0.1 copy.15.gain_ref
  26.8 18.9 %all-to-all-done.batch_ref = bf16[16,360,128]{2,1,0:T(8,128)(2,1)S(1)} async-done(((bf16[16,360,128]{2,1,0:T(8,128)(2,1)}), bf16[16,360,128]{2,1,0:T(8,128)(2,1)S(1)}, u32[]{:S(2)}, u32[]{:S(2)}) %all-to-all-start) | async-done | bytes 1474592 | tf_op jit(solution)/shard_map/all_to_all | solution.py:265
  45.7 2.5 %forward.1 = (f32[256,2048]{1,0:T(8,128)S(1)}, f32[16,2,2048]{2,1,0:T(2,128)S(1)}) custom-call(bf16[16,360,128]{2,1,0:T(8,128)(2,1)S(1)} %all-to-all-done.batch_ref, bf16[32,64,128]{2,1,0:T(8,128)(2,1)S(1)} %all-to-all-done.1.table_ref, f32[256,1]{1,0:T(8,128)S(1)} %copy.15.gain_ref), custom_call_target="tpu_custom_call" | custom-call | tf_op jit(solution)/shard_map/forward/pallas_call | solution.py:316
  48.2 11.9 %all_to_all.30.sums_ref = f32[16,2,2048]{2,1,0:T(2,128)S(1)} all-to-all(f32[16,2,2048]{2,1,0:T(2,128)S(1)} %get-tuple-element.25), channel_id=1, replica_groups=mesh['dp'=16,'xh'=2,'xl'=2,'yc'=8] {'xl','yc'}, dimensions={0} | all-to-all | bytes 524288 | tf_op jit(solution)/shard_map/all_to_all | solution.py:265
  60.1 4.6 %backward.1 = (bf16[256,2048]{1,0:T(8,128)(2,1)}, bf16[256,2048]{1,0:T(8,128)(2,1)}, bf16[32,72,128]{2,1,0:T(8,128)(2,1)}) custom-call(bf16[16,360,128]{2,1,0:T(8,128)(2,1)S(1)} %all-to-all-done.batch_ref, f32[256,1]{1,0:T(8,128)S(1)} %copy.15.gain_ref, f32[256,2048]{1,0:T(8,128)S(1)} %get-tuple-element.24.memory_ref, f32[16,2,2048]{2,1,0:T(2,128)S(1)} %all_to_all.30.sums_ref), custom_call_target="tpu_custom_call" | custom-call | tf_op jit(solution)/shard_map/backward/pallas_call | solution.py:328
  64.7 6.1 %all-to-all-start.3 = ((bf16[32,72,128]{2,1,0:T(8,128)(2,1)}), bf16[32,72,128]{2,1,0:T(8,128)(2,1)S(1)}, u32[]{:S(2)}, u32[]{:S(2)}) async-start(bf16[32,72,128]{2,1,0:T(8,128)(2,1)} %get-tuple-element.26), calls=%async_computation.3 | async-start | bytes 1179648 | tf_op jit(solution)/shard_map/all_to_all | solution.py:265
  70.9 0.0 copy-start.3
  70.9 1.2 copy-done.3
  72.1 0.0 copy-start.4
  72.1 1.2 copy-done.4
  73.3 3.0 %placed_grad.1 = bf16[16,352,128]{2,1,0:T(8,128)(2,1)} custom-call(bf16[16,360,128]{2,1,0:T(8,128)(2,1)S(1)} %all-to-all-done.batch_ref, bf16[32,64,128]{2,1,0:T(8,128)(2,1)S(1)} %all-to-all-done.1.table_ref, bf16[256,2048]{1,0:T(8,128)(2,1)S(1)} %copy-done.3, bf16[256,2048]{1,0:T(8,128)(2,1)S(1)} %copy-done.4), custom_call_target="tpu_custom_call" | custom-call | tf_op jit(solution)/shard_map/placed_grad/pallas_call | solution.py:344
  76.4 4.4 %all-to-all-done.3 = bf16[32,72,128]{2,1,0:T(8,128)(2,1)S(1)} async-done(((bf16[32,72,128]{2,1,0:T(8,128)(2,1)}), bf16[32,72,128]{2,1,0:T(8,128)(2,1)S(1)}, u32[]{:S(2)}, u32[]{:S(2)}) %all-to-all-start.3) | async-done | bytes 589856 | tf_op jit(solution)/shard_map/all_to_all | solution.py:265
  80.8 0.1 plane_sum.1
  80.9 33.2 %all_to_all.31.parts_ref = bf16[16,72,128]{2,1,0:T(8,128)(2,1)S(1)} all-to-all(bf16[16,72,128]{2,1,0:T(8,128)(2,1)S(1)} %plane_sum.1), channel_id=1, replica_groups=mesh['dp'=16,'xh'=2,'xl'=2,'yc'=8] {'dp'}, dimensions={0} | all-to-all | bytes 589824 | tf_op jit(solution)/shard_map/all_to_all | solution.py:265
  114.1 0.0 copy-start.1
  114.1 0.0 copy-start.5
  114.1 0.0 copy-start.6
  114.1 4.9 %all-to-all-start.5 = ((bf16[16,352,128]{2,1,0:T(8,128)(2,1)}), bf16[16,352,128]{2,1,0:T(8,128)(2,1)S(1)}, u32[]{:S(2)}, u32[]{:S(2)}) async-start(bf16[16,352,128]{2,1,0:T(8,128)(2,1)} %placed_grad.1), calls=%async_computation.5 | async-start | bytes 2883584 | tf_op jit(solution)/shard_map/all_to_all | solution.py:265
  119.1 31.7 %all-gather = bf16[1152,128]{1,0:T(8,128)(2,1)S(1)} all-gather(bf16[72,128]{1,0:T(8,128)(2,1)S(1)} %share_sum.1), channel_id=2, replica_groups=mesh['dp'=16,'xh'=2,'xl'=2,'yc'=8] {'dp'}, dimensions={0}, use_global_device_ids=true | all-gather | bytes 313344 | tf_op jit(solution)/shard_map/all_gather | solution.py:369
  150.8 0.0 copy-done.1
  150.8 0.0 copy-done.5
  150.8 0.0 copy-done.6
  150.8 1.3 adam.1
  152.1 0.0 all-to-all-done.5.parts_ref
  152.1 2.0 %unpack.1 = (bf16[128,4096]{1,0:T(8,128)(2,1)}, f32[32,128]{1,0:T(8,128)}) custom-call(bf16[16,352,128]{2,1,0:T(8,128)(2,1)S(1)} %all-to-all-done.5.parts_ref, s32[32,128]{1,0:T(8,128)S(1)} %bitcast.12, f32[32,128]{1,0:T(8,128)S(1)} %get-tuple-element.32.weights_ref), custom_call_target="tpu_custom_call" | custom-call | tf_op jit(solution)/shard_map/unpack/pallas_call | solution.py:372
  (1 shorter events, 0.0 us)
Async XLA Ops:
  0.6 1.0 copy-start
  1.6 10.4 %copy-start.2 = (bf16[128,4096]{1,0:T(8,128)(2,1)S(1)}, bf16[128,4096]{1,0:T(8,128)(2,1)}, u32[]{:S(2)}) copy-start(bf16[128,4096]{1,0:T(8,128)(2,1)} %cotangent_ref.1) | copy-start | bytes 3145732
  1.6 10.4 %copy-start.7 = (s32[128,32]{0,1:T(8,128)S(1)}, s32[128,32]{0,1:T(8,128)}, u32[]{:S(2)}) copy-start(s32[128,32]{0,1:T(8,128)} %param.9) | copy-start | bytes 49156
  1.6 10.5 %copy-start.8 = (f32[128,32]{0,1:T(8,128)S(1)}, f32[128,32]{0,1:T(8,128)}, u32[]{:S(2)}) copy-start(f32[128,32]{0,1:T(8,128)} %param.10) | copy-start | bytes 49156
  1.6 10.5 %copy-start.9 = (s32[128,3]{0,1:T(4,128)S(1)}, s32[128,3]{0,1:T(4,128)}, u32[]{:S(2)}) copy-start(s32[128,3]{0,1:T(4,128)} %param.8) | copy-start | bytes 4612
  2.5 18.9 %all-to-all-start.1 = ((bf16[32,64,128]{2,1,0:T(8,128)(2,1)}), bf16[32,64,128]{2,1,0:T(8,128)(2,1)S(1)}, u32[]{:S(2)}, u32[]{:S(2)}) async-start(bf16[32,64,128]{2,1,0:T(8,128)(2,1)} %bitcast.15), calls=%async_computation.1 | async-start | bytes 1048576 | tf_op jit(solution)/shard_map/all_to_all | solution.py:265
  21.3 24.4 %all-to-all-start = ((bf16[16,360,128]{2,1,0:T(8,128)(2,1)}), bf16[16,360,128]{2,1,0:T(8,128)(2,1)S(1)}, u32[]{:S(2)}, u32[]{:S(2)}) async-start(bf16[16,360,128]{2,1,0:T(8,128)(2,1)} %get-tuple-element.23), calls=%async_computation | async-start | bytes 2949120 | tf_op jit(solution)/shard_map/all_to_all | solution.py:265
  64.7 16.1 %all-to-all-start.3 = ((bf16[32,72,128]{2,1,0:T(8,128)(2,1)}), bf16[32,72,128]{2,1,0:T(8,128)(2,1)S(1)}, u32[]{:S(2)}, u32[]{:S(2)}) async-start(bf16[32,72,128]{2,1,0:T(8,128)(2,1)} %get-tuple-element.26), calls=%async_computation.3 | async-start | bytes 1179648 | tf_op jit(solution)/shard_map/all_to_all | solution.py:265
  70.9 1.2 copy-start.3
  72.1 1.2 copy-start.4
  114.1 36.7 %copy-start.1 = (bf16[32,4096]{1,0:T(8,128)(2,1)S(1)}, bf16[32,4096]{1,0:T(8,128)(2,1)}, u32[]{:S(2)}) copy-start(bf16[32,4096]{1,0:T(8,128)(2,1)} %table_ref.3) | copy-start | bytes 786436
  114.1 36.7 %copy-start.5 = (f32[32,4096]{1,0:T(8,128)S(1)}, f32[32,4096]{1,0:T(8,128)}, u32[]{:S(2)}) copy-start(f32[32,4096]{1,0:T(8,128)} %first_ref.1) | copy-start | bytes 1572868
  114.1 36.7 %copy-start.6 = (f32[32,4096]{1,0:T(8,128)S(1)}, f32[32,4096]{1,0:T(8,128)}, u32[]{:S(2)}) copy-start(f32[32,4096]{1,0:T(8,128)} %second_ref.1) | copy-start | bytes 1572868
  114.1 38.0 %all-to-all-start.5 = ((bf16[16,352,128]{2,1,0:T(8,128)(2,1)}), bf16[16,352,128]{2,1,0:T(8,128)(2,1)S(1)}, u32[]{:S(2)}, u32[]{:S(2)}) async-start(bf16[16,352,128]{2,1,0:T(8,128)(2,1)} %placed_grad.1), calls=%async_computation.5 | async-start | bytes 2883584 | tf_op jit(solution)/shard_map/all_to_all | solution.py:265

commit v6 on v5

--- a/solution.py
+++ b/solution.py
@@ -60,9 +60,12 @@
     for b in range(GROUP):
         for j in range(TILES):
             at = b * WIDE + j * L
-            tile = table_ref[:, at : at + L]
-            for x in range(out_ref.shape[0]):
-                out_ref[x, b, j * ROWS : (j + 1) * ROWS, :] = tile
+            out_ref[b, j * ROWS : (j + 1) * ROWS, :] = table_ref[:, at : at + L]
+
+
+def join_kernel(place_ref, own_ref, other_ref, out_ref):
+    out_ref[place_ref[0]] = own_ref[...]
+    out_ref[1 - place_ref[0]] = other_ref[...]
 
 
 def pack_kernel(owners_ref, pick_ref, scores_ref, cotangent_ref, send_ref, weights_ref, info_ref):
@@ -261,6 +264,14 @@
         score_ref[...] = weights * (weight_grad - mean)
 
 
+def last_kernel(
+    parts_ref, pick_ref, weights_ref, grad_ref, table_ref, first_ref, second_ref,
+    out_ref, score_ref, new_table_ref, new_first_ref, new_second_ref, gain_ref, placed_grad_ref,
+):
+    adam_kernel(grad_ref, table_ref, first_ref, second_ref, new_table_ref, new_first_ref, new_second_ref, gain_ref)
+    out_kernel(parts_ref, pick_ref, weights_ref, out_ref, score_ref, placed_grad_ref)
+
+
 def exchange(array, axes):
     return lax.all_to_all(array, axes, split_axis=0, concat_axis=0, tiled=True)
 
@@ -283,11 +294,11 @@
 
     table_send = pl.pallas_call(
         table_kernel,
-        out_shape=in_hbm(groups, GROUP, TILES * ROWS, L, BF16),
+        out_shape=in_hbm(GROUP, TILES * ROWS, L, BF16),
         compiler_params=PARAMS,
         name="table_send",
     )(value_table)
-    table = exchange(table_send.reshape(OWNERS, TILES * ROWS, L), PLANE)
+    own_half = exchange(table_send, TEAM)
 
     batch_send, weights = pl.pallas_call(
         pack_kernel,
@@ -304,7 +315,19 @@
         compiler_params=PARAMS,
         name="pack",
     )(owners.T, pick_index.T, key_scores.T, output_cotangent)
+    own_half, batch_send = lax.optimization_barrier((own_half, batch_send))
     batch = exchange(batch_send, TEAM)
+    other_half = lax.ppermute(own_half, "xh", [(i, (i + 1) % groups) for i in range(groups)])
+    vmem = pl.BlockSpec(memory_space=pltpu.VMEM)
+    table = pl.pallas_call(
+        join_kernel,
+        in_specs=[pl.BlockSpec(memory_space=pltpu.SMEM), vmem, vmem],
+        out_specs=vmem,
+        out_shape=shape(groups, GROUP, TILES * ROWS, L, BF16),
+        compiler_params=PARAMS,
+        name="table_join",
+    )(lax.axis_index("xh").reshape(1).astype(jnp.int32), own_half, other_half)
+    table = table.reshape(OWNERS, TILES * ROWS, L)
     gain = lax.dynamic_slice(norm_gain, (block_index * WIDE,), (WIDE,)).reshape(WIDE, 1)
 
     batch_spec = pl.BlockSpec((STEP, WIDE + INFO, L), lambda i: (i, 0, 0))
@@ -369,28 +392,39 @@
     totals = lax.all_gather(total, "dp", axis=0, tiled=False)
 
     back = exchange(back_send, TEAM)
-    memory_out, score_turned = pl.pallas_call(
-        out_kernel,
+    rows_spec = pl.BlockSpec((ROWS, MANY * WIDE), lambda i: (0, i))
+    memory_out, score_turned, new_table, new_first, new_second, gain_gradient = pl.pallas_call(
+        last_kernel,
         grid=(GROUP // MANY,),
-        in_specs=[pl.BlockSpec((MANY, BACK, L), lambda i: (i, 0, 0)), whole(PICKS, TOK), whole(PICKS, TOK)],
-        out_specs=[pl.BlockSpec((TOK, MANY * WIDE), lambda i: (0, i)), whole(PICKS, TOK)],
-        out_shape=(shape(TOK, D, BF16), shape(PICKS, TOK, F32)),
-        scratch_shapes=[pltpu.VMEM((SLOTS, TOK), F32)],
-        compiler_params=PARAMS,
-        name="unpack",
-    )(back, pick_index.T, weights)
-
-    new_table, new_first, new_second, gain_gradient = pl.pallas_call(
-        adam_kernel,
+        in_specs=[
+            pl.BlockSpec((MANY, BACK, L), lambda i: (i, 0, 0)),
+            whole(PICKS, TOK),
+            whole(PICKS, TOK),
+            pl.BlockSpec((MANY, GRAD, L), lambda i: (i, 0, 0)),
+            rows_spec,
+            rows_spec,
+            rows_spec,
+        ],
+        out_specs=[
+            pl.BlockSpec((TOK, MANY * WIDE), lambda i: (0, i)),
+            whole(PICKS, TOK),
+            rows_spec,
+            rows_spec,
+            rows_spec,
+            pl.BlockSpec((1, MANY * WIDE), lambda i: (0, i)),
+        ],
         out_shape=(
+            shape(TOK, D, BF16),
+            shape(PICKS, TOK, F32),
             shape(ROWS, D, BF16),
             shape(ROWS, D, F32),
             shape(ROWS, D, F32),
             shape(1, D, F32),
         ),
-        compiler_params=PARAMS,
-        name="adam",
-    )(totals, value_table, first_moment, second_moment)
+        scratch_shapes=[pltpu.VMEM((SLOTS, TOK), F32)],
+        compiler_params=PARAMS,
+        name="last",
+    )(back, pick_index.T, weights, totals, value_table, first_moment, second_moment)
     return (memory_out, score_turned.T, gain_gradient.reshape(D), new_table, new_first, new_second)
 
 

time: 156 us -> 157 us (level)
  waiting for transfers between devices: 30.4 us -> 26.8 us
  starting transfers between devices: 25.1 us -> 28.3 us
  local copies, waits for them, and re-layouts: 4.32 us -> 6.43 us
    all_to_all x4, waiting for transfers between devices: 30.4 us -> 6.89 us  [exchange(): return lax.all_to_all(array, axes, split_axis=0, concat_axis=0, tiled=True)]
    ppermute x0 -> x1, waiting for transfers between devices: none -> 20 us  [per_device(): lax.ppermute(own_half, 'xh', [(i, (i + 1) % groups) for i in range(groups)])]
    ppermute x0 -> x1, starting transfers between devices: none -> 6.67 us  [per_device(): lax.ppermute(own_half, 'xh', [(i, (i + 1) % groups) for i in range(groups)])]
    all_to_all x4, starting transfers between devices: 25.1 us -> 21.6 us  [exchange(): return lax.all_to_all(array, axes, split_axis=0, concat_axis=0, tiled=True)]
    unnamed x20 -> x22, local copies, waits for them, and re-layouts: 3.42 us -> 5.53 us
  transfers between devices with their start and end apart: 4 -> 5, of which waited for: 3 -> 3; matrix products, arithmetic and copies ran while one was open for 1% -> 1% of each run, Pallas kernels for 4% -> 3%
where the time goes in v6:
time: 157 us; the launch traced here: 155 us
  blocking collectives  76.5 us (49%)
  starting transfers between devices  28.3 us (18%)
  waiting for transfers between devices  26.8 us (17%)
  Pallas kernels  15.8 us (10%)
  local copies, waits for them, and re-layouts  6.43 us (4%)
    all_to_all x2, blocking collectives, exchange(): return lax.all_to_all(array, axes, split_axis=0, concat_axis=0, tiled=True)  44.8 us
    all_gather x1, blocking collectives, per_device(): totals = lax.all_gather(total, 'dp', axis=0, tiled=False)  31.7 us
    all_to_all x4, starting transfers between devices, exchange(): return lax.all_to_all(array, axes, split_axis=0, concat_axis=0, tiled=True)  21.6 us
    ppermute x1, waiting for transfers between devices, per_device(): lax.ppermute(own_half, 'xh', [(i, (i + 1) % groups) for i in range(groups)])  20 us
    all_to_all x4, waiting for transfers between devices, exchange(): return lax.all_to_all(array, axes, split_axis=0, concat_axis=0, tiled=True)  6.89 us
    ppermute x1, starting transfers between devices, per_device(): lax.ppermute(own_half, 'xh', [(i, (i + 1) % groups) for i in range(groups)])  6.67 us
    unnamed x22, local copies, waits for them, and re-layouts  5.53 us
    pallas_call x1, Pallas kernels, per_device(): pl.pallas_call(backward_kernel, grid=(steps,), in_specs=[batch_spec, whol...  4.6 us
  transfers between devices with their start and end apart: 5, of which 3 were waited for; matrix products, arithmetic and copies ran while one was open for 1% of the time, Pallas kernels for 3%

profile of v6, /device:TPU:6, one launch (start us, length us, event | category | flops | bytes accessed | tf_op | source)
XLA Modules:
  0.0 154.7 jit_solution(1476256513853009497)
XLA Ops:
  0.6 0.0 copy-start
  0.6 0.9 copy-done
  1.6 0.0 copy-start.2
  1.6 0.7 table_send.1
  2.3 5.9 %all-to-all-start = ((bf16[16,64,128]{2,1,0:T(8,128)(2,1)}), bf16[16,64,128]{2,1,0:T(8,128)(2,1)S(1)}, u32[]{:S(2)}, u32[]{:S(2)}) async-start(bf16[16,64,128]{2,1,0:T(8,128)(2,1)} %table_send.1), calls=%async_computation | async-start | bytes 524288 | tf_op jit(solution)/shard_map/all_to_all | solution.py:276
  8.3 0.0 copy-done.2
  8.3 0.0 copy-start.7
  8.3 0.7 copy-done.7
  9.0 0.0 copy-start.9
  9.0 0.7 copy-done.9
  9.7 0.0 copy-start.10
  9.7 0.7 copy-done.10
  10.4 2.2 %pack.1 = (bf16[16,360,128]{2,1,0:T(8,128)(2,1)}, f32[32,128]{1,0:T(8,128)S(1)}) custom-call(s32[3,128]{1,0:T(4,128)S(1)} %bitcast.17, s32[32,128]{1,0:T(8,128)S(1)} %bitcast.14, f32[32,128]{1,0:T(8,128)S(1)} %bitcast.16, bf16[128,4096]{1,0:T(8,128)(2,1)S(1)} %copy-done.2), custom_call_target="tpu_custom_call" | custom-call | tf_op jit(solution)/shard_map/pack/pallas_call | solution.py:303
  12.6 2.5 %all-to-all-done.own_ref = bf16[16,64,128]{2,1,0:T(8,128)(2,1)S(1)} async-done(((bf16[16,64,128]{2,1,0:T(8,128)(2,1)}), bf16[16,64,128]{2,1,0:T(8,128)(2,1)S(1)}, u32[]{:S(2)}, u32[]{:S(2)}) %all-to-all-start) | async-done | bytes 262176 | tf_op jit(solution)/shard_map/all_to_all | solution.py:276
  15.1 4.9 %all-to-all-start.1 = ((bf16[16,360,128]{2,1,0:T(8,128)(2,1)}), bf16[16,360,128]{2,1,0:T(8,128)(2,1)S(1)}, u32[]{:S(2)}, u32[]{:S(2)}) async-start(bf16[16,360,128]{2,1,0:T(8,128)(2,1)} %get-tuple-element.26), calls=%async_computation.1 | async-start | bytes 2949120 | tf_op jit(solution)/shard_map/all_to_all | solution.py:276
  20.0 6.7 %collective-permute-start = (bf16[16,64,128]{2,1,0:T(8,128)(2,1)S(1)}, bf16[16,64,128]{2,1,0:T(8,128)(2,1)S(1)}, u32[]{:S(2)}, u32[]{:S(2)}) collective-permute-start(bf16[16,64,128]{2,1,0:T(8,128)(2,1)S(1)} %all-to-all-done.own_ref), channel_id=1, source_target_pairs={{0,16},{16,0},{1,17},{17,1},{2,18},{18,2},{3,19},{19,3},{4,20},{20... | collective-permute-start | bytes 786440 | tf_op jit(solution)/shard_map/ppermute | solution.py:320
  26.7 0.8 dynamic_slice.3
  27.4 0.1 copy.15.gain_ref
  27.6 20.0 %collective-permute-done.other_ref = bf16[16,64,128]{2,1,0:T(8,128)(2,1)S(1)} collective-permute-done((bf16[16,64,128]{2,1,0:T(8,128)(2,1)S(1)}, bf16[16,64,128]{2,1,0:T(8,128)(2,1)S(1)}, u32[]{:S(2)}, u32[]{:S(2)}) %collective-permute-start) | collective-permute-done | bytes 262176 | tf_op jit(solution)/shard_map/ppermute | solution.py:320
  47.6 0.0 all-to-all-done.1.batch_ref
  47.6 2.5 %forward.1 = (f32[256,2048]{1,0:T(8,128)S(1)}, f32[16,2,2048]{2,1,0:T(2,128)S(1)}) custom-call(bf16[16,360,128]{2,1,0:T(8,128)(2,1)S(1)} %all-to-all-done.1.batch_ref, bf16[32,64,128]{2,1,0:T(8,128)(2,1)S(1)} %bitcast.10, f32[256,1]{1,0:T(8,128)S(1)} %copy.15.gain_ref), custom_call_target="tpu_custom_call" | custom-call | tf_op jit(solution)/shard_map/forward/pallas_call | solution.py:339
  50.1 13.0 %all_to_all.30.sums_ref = f32[16,2,2048]{2,1,0:T(2,128)S(1)} all-to-all(f32[16,2,2048]{2,1,0:T(2,128)S(1)} %get-tuple-element.29), channel_id=1, replica_groups=mesh['dp'=16,'xh'=2,'xl'=2,'yc'=8] {'xl','yc'}, dimensions={0} | all-to-all | bytes 524288 | tf_op jit(solution)/shard_map/all_to_all | solution.py:276
  63.1 4.6 %backward.1 = (bf16[256,2048]{1,0:T(8,128)(2,1)}, bf16[256,2048]{1,0:T(8,128)(2,1)}, bf16[32,72,128]{2,1,0:T(8,128)(2,1)}) custom-call(bf16[16,360,128]{2,1,0:T(8,128)(2,1)S(1)} %all-to-all-done.1.batch_ref, f32[256,1]{1,0:T(8,128)S(1)} %copy.15.gain_ref, f32[256,2048]{1,0:T(8,128)S(1)} %get-tuple-element.28.memory_ref, f32[16,2,2048]{2,1,0:T(2,128)S(1)} %all_to_all.30.sums_ref), custom_call_target="tpu_custom_call" | custom-call | tf_op jit(solution)/shard_map/backward/pallas_call | solution.py:351
  67.7 5.9 %all-to-all-start.3 = ((bf16[32,72,128]{2,1,0:T(8,128)(2,1)}), bf16[32,72,128]{2,1,0:T(8,128)(2,1)S(1)}, u32[]{:S(2)}, u32[]{:S(2)}) async-start(bf16[32,72,128]{2,1,0:T(8,128)(2,1)} %get-tuple-element.30), calls=%async_computation.3 | async-start | bytes 1179648 | tf_op jit(solution)/shard_map/all_to_all | solution.py:276
  73.6 0.0 copy-start.3
  73.6 1.2 copy-done.3
  74.8 0.0 copy-start.4
  74.8 1.2 copy-done.4
  76.1 3.0 %placed_grad.1 = bf16[16,352,128]{2,1,0:T(8,128)(2,1)} custom-call(bf16[16,360,128]{2,1,0:T(8,128)(2,1)S(1)} %all-to-all-done.1.batch_ref, bf16[32,64,128]{2,1,0:T(8,128)(2,1)S(1)} %bitcast.11, bf16[256,2048]{1,0:T(8,128)(2,1)S(1)} %copy-done.3, bf16[256,2048]{1,0:T(8,128)(2,1)S(1)} %copy-done.4), custom_call_target="tpu_custom_call" | custom-call | tf_op jit(solution)/shard_map/placed_grad/pallas_call | solution.py:367
  79.1 4.4 %all-to-all-done.3 = bf16[32,72,128]{2,1,0:T(8,128)(2,1)S(1)} async-done(((bf16[32,72,128]{2,1,0:T(8,128)(2,1)}), bf16[32,72,128]{2,1,0:T(8,128)(2,1)S(1)}, u32[]{:S(2)}, u32[]{:S(2)}) %all-to-all-start.3) | async-done | bytes 589856 | tf_op jit(solution)/shard_map/all_to_all | solution.py:276
  83.5 0.1 plane_sum.1
  83.6 31.8 %all_to_all.31.parts_ref = bf16[16,72,128]{2,1,0:T(8,128)(2,1)S(1)} all-to-all(bf16[16,72,128]{2,1,0:T(8,128)(2,1)S(1)} %plane_sum.1), channel_id=1, replica_groups=mesh['dp'=16,'xh'=2,'xl'=2,'yc'=8] {'dp'}, dimensions={0} | all-to-all | bytes 589824 | tf_op jit(solution)/shard_map/all_to_all | solution.py:276
  115.5 0.0 copy-start.1
  115.5 0.0 copy-start.5
  115.5 0.0 copy-start.6
  115.5 0.0 copy-start.8
  115.5 4.8 %all-to-all-start.5 = ((bf16[16,352,128]{2,1,0:T(8,128)(2,1)}), bf16[16,352,128]{2,1,0:T(8,128)(2,1)S(1)}, u32[]{:S(2)}, u32[]{:S(2)}) async-start(bf16[16,352,128]{2,1,0:T(8,128)(2,1)} %placed_grad.1), calls=%async_computation.5 | async-start | bytes 2883584 | tf_op jit(solution)/shard_map/all_to_all | solution.py:276
  120.4 31.7 %all-gather = bf16[1152,128]{1,0:T(8,128)(2,1)S(1)} all-gather(bf16[72,128]{1,0:T(8,128)(2,1)S(1)} %share_sum.1), channel_id=2, replica_groups=mesh['dp'=16,'xh'=2,'xl'=2,'yc'=8] {'dp'}, dimensions={0}, use_global_device_ids=true | all-gather | bytes 313344 | tf_op jit(solution)/shard_map/all_gather | solution.py:392
  152.1 0.0 all-to-all-done.5.parts_ref
  152.1 0.0 copy-done.1
  152.1 0.0 copy-done.5
  152.1 0.0 copy-done.6
  152.2 0.0 copy-done.8
  152.2 2.5 %last.1 = (bf16[128,4096]{1,0:T(8,128)(2,1)}, f32[32,128]{1,0:T(8,128)}, bf16[32,4096]{1,0:T(8,128)(2,1)}, f32[32,4096]{1,0:T(8,128)}, f32[32,4096]{1,0:T(8,128)}, /*index=5*/f32[1,4096]{1,0:T(1,128)}) custom-call(bf16[16,352,128]{2,1,0:T(8,128)(2,1)S(1)} %all-to-all-done.5.parts_ref, s32[32,128]{1,0:T(8,128)S(1)} %bitcast.15, ...), custom_call_target="tpu_custom_call" | custom-call | tf_op jit(solution)/shard_map/last/pallas_call | solution.py:396
  (2 shorter events, 0.1 us)
Async XLA Ops:
  0.6 1.0 copy-start
  1.6 6.7 %copy-start.2 = (bf16[128,4096]{1,0:T(8,128)(2,1)S(1)}, bf16[128,4096]{1,0:T(8,128)(2,1)}, u32[]{:S(2)}) copy-start(bf16[128,4096]{1,0:T(8,128)(2,1)} %cotangent_ref.1) | copy-start | bytes 3145732
  2.3 12.7 %all-to-all-start = ((bf16[16,64,128]{2,1,0:T(8,128)(2,1)}), bf16[16,64,128]{2,1,0:T(8,128)(2,1)S(1)}, u32[]{:S(2)}, u32[]{:S(2)}) async-start(bf16[16,64,128]{2,1,0:T(8,128)(2,1)} %table_send.1), calls=%async_computation | async-start | bytes 524288 | tf_op jit(solution)/shard_map/all_to_all | solution.py:276
  8.3 0.7 copy-start.7
  9.0 0.7 copy-start.9
  9.7 0.7 copy-start.10
  15.1 32.5 %all-to-all-start.1 = ((bf16[16,360,128]{2,1,0:T(8,128)(2,1)}), bf16[16,360,128]{2,1,0:T(8,128)(2,1)S(1)}, u32[]{:S(2)}, u32[]{:S(2)}) async-start(bf16[16,360,128]{2,1,0:T(8,128)(2,1)} %get-tuple-element.26), calls=%async_computation.1 | async-start | bytes 2949120 | tf_op jit(solution)/shard_map/all_to_all | solution.py:276
  20.0 27.5 %collective-permute-start = (bf16[16,64,128]{2,1,0:T(8,128)(2,1)S(1)}, bf16[16,64,128]{2,1,0:T(8,128)(2,1)S(1)}, u32[]{:S(2)}, u32[]{:S(2)}) collective-permute-start(bf16[16,64,128]{2,1,0:T(8,128)(2,1)S(1)} %all-to-all-done.own_ref), channel_id=1, source_target_pairs={{0,16},{16,0},{1,17},{17,1},{2,18},{18,2},{3,19},{19,3},{4,20},{20... | collective-permute-start | bytes 786440 | tf_op jit(solution)/shard_map/ppermute | solution.py:320
  67.7 15.8 %all-to-all-start.3 = ((bf16[32,72,128]{2,1,0:T(8,128)(2,1)}), bf16[32,72,128]{2,1,0:T(8,128)(2,1)S(1)}, u32[]{:S(2)}, u32[]{:S(2)}) async-start(bf16[32,72,128]{2,1,0:T(8,128)(2,1)} %get-tuple-element.30), calls=%async_computation.3 | async-start | bytes 1179648 | tf_op jit(solution)/shard_map/all_to_all | solution.py:276
  73.6 1.2 copy-start.3
  74.8 1.2 copy-start.4
  115.5 36.6 %copy-start.1 = (bf16[32,4096]{1,0:T(8,128)(2,1)S(1)}, bf16[32,4096]{1,0:T(8,128)(2,1)}, u32[]{:S(2)}) copy-start(bf16[32,4096]{1,0:T(8,128)(2,1)} %table_ref.3) | copy-start | bytes 786436
  115.5 36.6 %copy-start.5 = (f32[32,4096]{1,0:T(8,128)S(1)}, f32[32,4096]{1,0:T(8,128)}, u32[]{:S(2)}) copy-start(f32[32,4096]{1,0:T(8,128)} %first_ref.1) | copy-start | bytes 1572868
  115.5 36.6 %copy-start.6 = (f32[32,4096]{1,0:T(8,128)S(1)}, f32[32,4096]{1,0:T(8,128)}, u32[]{:S(2)}) copy-start(f32[32,4096]{1,0:T(8,128)} %second_ref.1) | copy-start | bytes 1572868
  115.5 36.6 %copy-start.8 = (s32[128,32]{0,1:T(8,128)S(1)}, s32[128,32]{0,1:T(8,128)}, u32[]{:S(2)}) copy-start(s32[128,32]{0,1:T(8,128)} %param.9) | copy-start | bytes 49156
  115.5 36.6 %all-to-all-start.5 = ((bf16[16,352,128]{2,1,0:T(8,128)(2,1)}), bf16[16,352,128]{2,1,0:T(8,128)(2,1)S(1)}, u32[]{:S(2)}, u32[]{:S(2)}) async-start(bf16[16,352,128]{2,1,0:T(8,128)(2,1)} %placed_grad.1), calls=%async_computation.5 | async-start | bytes 2883584 | tf_op jit(solution)/shard_map/all_to_all | solution.py:276

commit v7 on v6

--- a/solution.py
+++ b/solution.py
@@ -60,12 +60,9 @@
     for b in range(GROUP):
         for j in range(TILES):
             at = b * WIDE + j * L
-            out_ref[b, j * ROWS : (j + 1) * ROWS, :] = table_ref[:, at : at + L]
-
-
-def join_kernel(place_ref, own_ref, other_ref, out_ref):
-    out_ref[place_ref[0]] = own_ref[...]
-    out_ref[1 - place_ref[0]] = other_ref[...]
+            tile = table_ref[:, at : at + L]
+            for x in range(out_ref.shape[0]):
+                out_ref[x, b, j * ROWS : (j + 1) * ROWS, :] = tile
 
 
 def pack_kernel(owners_ref, pick_ref, scores_ref, cotangent_ref, send_ref, weights_ref, info_ref):
@@ -94,8 +91,8 @@
         send_ref[b, WIDE:, :] = info_ref[...]
 
 
-def load_info(batch_ref):
-    info = jnp.concatenate([batch_ref[i, WIDE:, :] for i in range(STEP)], axis=1).astype(F32)
+def load_info(batch_ref, first=0):
+    info = jnp.concatenate([batch_ref[first + i, WIDE:, :] for i in range(STEP)], axis=1).astype(F32)
     placed = [info[c * ROWS : (c + 1) * ROWS] for c in range(CANDS)]
     named = [
         jnp.broadcast_to(info[SLOTS + c : SLOTS + c + 1], (ROWS, STEP * TOK)) for c in range(CANDS)
@@ -119,23 +116,25 @@
     )
 
 
-def load_cotangent(batch_ref):
-    return jnp.concatenate([batch_ref[i, :WIDE, :] for i in range(STEP)], axis=1).astype(F32)
-
-
-def forward_kernel(batch_ref, table_ref, gain_ref, memory_ref, sums_ref, turned_ref):
-    @pl.when(pl.program_id(0) == 0)
-    def _():
-        turned_ref[...] = jnp.transpose(load_table(table_ref))
-
-    memory = dot(turned_ref[...], place(*load_info(batch_ref)), ((1,), (0,)))
-    memory_ref[...] = memory
-    scaled = load_cotangent(batch_ref) * gain_ref[...]
-    square = jnp.sum(memory * memory, axis=0, keepdims=True)
-    cross = jnp.sum(scaled * memory, axis=0, keepdims=True)
-    both = jnp.concatenate([square, cross], axis=0)
-    for g in range(sums_ref.shape[0]):
-        sums_ref[g] = both
+def load_cotangent(batch_ref, first):
+    return jnp.concatenate([batch_ref[first + i, :WIDE, :] for i in range(STEP)], axis=1).astype(F32)
+
+
+def forward_kernel(batch_ref, table_ref, gain_ref, memory_ref, sums_ref, placed_ref):
+    turned = jnp.transpose(load_table(table_ref))
+    gain = gain_ref[...]
+    for first in range(0, GROUP, STEP):
+        at = slice(first * TOK, (first + STEP) * TOK)
+        placed = place(*load_info(batch_ref, first))
+        placed_ref[:, at] = placed
+        memory = dot(turned, placed, ((1,), (0,)))
+        memory_ref[:, at] = memory
+        scaled = load_cotangent(batch_ref, first) * gain
+        square = jnp.sum(memory * memory, axis=0, keepdims=True)
+        cross = jnp.sum(scaled * memory, axis=0, keepdims=True)
+        both = jnp.concatenate([square, cross], axis=0)
+        for g in range(sums_ref.shape[0]):
+            sums_ref[g, :, at] = both
 
 
 def split(value):
@@ -148,43 +147,37 @@
     return jnp.concatenate([high, low, jnp.zeros((8 - 2 * TILES, L), F32)], axis=0).astype(BF16)
 
 
-def backward_kernel(batch_ref, gain_ref, memory_ref, sums_ref, out_ref, grad_ref, send_ref, total_ref, gain_sum_ref):
-    step = pl.program_id(0)
-    sums = jnp.sum(sums_ref[...], axis=0)
-    inverse = lax.rsqrt(sums[0:1] / D + norm_epsilon)
-    factor = inverse * inverse * inverse * (sums[1:2] / D)
-    memory = memory_ref[...]
-    cotangent = load_cotangent(batch_ref)
+def backward_kernel(
+    batch_ref, gain_ref, memory_ref, sums_ref, placed_ref, out_ref, grad_ref, send_ref, out_held, grad_held, sems
+):
     gain = gain_ref[...]
-    normed = memory * inverse
-    out_ref[...] = (normed * gain).astype(BF16)
-    grad = (inverse * (cotangent * gain) - memory * factor).astype(BF16)
-    grad_ref[...] = grad
-    gain_part = cotangent * normed
-    folded = sum(gain_part[:, i * L : (i + 1) * L] for i in range(STEP))
-    table_part = dot(place(*load_info(batch_ref)), grad, ((1,), (1,)))
-
-    @pl.when(step == 0)
-    def _():
-        total_ref[...] = table_part
-        gain_sum_ref[...] = folded
-
-    @pl.when(step > 0)
-    def _():
-        total_ref[...] += table_part
-        gain_sum_ref[...] += folded
-
-    @pl.when(step == pl.num_programs(0) - 1)
-    def _():
-        for j in range(TILES):
-            send_ref[:, j * ROWS : (j + 1) * ROWS, :] = (
-                total_ref[:, j * L : (j + 1) * L].astype(BF16).reshape(OWNERS, ROWS, L)
-            )
-        turned = jnp.transpose(gain_sum_ref[...])
-        rows = [jnp.sum(turned[:, j * L : (j + 1) * L], axis=0, keepdims=True) for j in range(TILES)]
-        tail = gain_rows(jnp.concatenate(rows, axis=0))
-        for o in range(OWNERS):
-            send_ref[o, GAIN_AT:, :] = tail
+    gain_sum = jnp.zeros((WIDE, L), F32)
+    for first in range(0, GROUP, STEP):
+        at = slice(first * TOK, (first + STEP) * TOK)
+        sums = jnp.sum(sums_ref[:, :, at], axis=0)
+        inverse = lax.rsqrt(sums[0:1] / D + norm_epsilon)
+        factor = inverse * inverse * inverse * (sums[1:2] / D)
+        memory = memory_ref[:, at]
+        cotangent = load_cotangent(batch_ref, first)
+        normed = memory * inverse
+        out_held[:, at] = (normed * gain).astype(BF16)
+        grad_held[:, at] = (inverse * (cotangent * gain) - memory * factor).astype(BF16)
+        gain_part = cotangent * normed
+        gain_sum += sum(gain_part[:, i * L : (i + 1) * L] for i in range(STEP))
+    out_copy = pltpu.make_async_copy(out_held, out_ref, sems.at[0])
+    grad_copy = pltpu.make_async_copy(grad_held, grad_ref, sems.at[1])
+    out_copy.start()
+    grad_copy.start()
+    total = dot(placed_ref[...], grad_held[...], ((1,), (1,))).astype(BF16)
+    for j in range(TILES):
+        send_ref[:, j * ROWS : (j + 1) * ROWS, :] = total[:, j * L : (j + 1) * L].reshape(OWNERS, ROWS, L)
+    turned = jnp.transpose(gain_sum)
+    rows = [jnp.sum(turned[:, j * L : (j + 1) * L], axis=0, keepdims=True) for j in range(TILES)]
+    tail = gain_rows(jnp.concatenate(rows, axis=0))
+    for o in range(OWNERS):
+        send_ref[o, GAIN_AT:, :] = tail
+    out_copy.wait()
+    grad_copy.wait()
 
 
 def placed_grad_kernel(batch_ref, table_ref, out_ref, grad_ref, send_ref):
@@ -294,11 +287,11 @@
 
     table_send = pl.pallas_call(
         table_kernel,
-        out_shape=in_hbm(GROUP, TILES * ROWS, L, BF16),
+        out_shape=in_hbm(groups, GROUP, TILES * ROWS, L, BF16),
         compiler_params=PARAMS,
         name="table_send",
     )(value_table)
-    own_half = exchange(table_send, TEAM)
+    table = exchange(table_send.reshape(OWNERS, TILES * ROWS, L), PLANE)
 
     batch_send, weights = pl.pallas_call(
         pack_kernel,
@@ -315,19 +308,7 @@
         compiler_params=PARAMS,
         name="pack",
     )(owners.T, pick_index.T, key_scores.T, output_cotangent)
-    own_half, batch_send = lax.optimization_barrier((own_half, batch_send))
     batch = exchange(batch_send, TEAM)
-    other_half = lax.ppermute(own_half, "xh", [(i, (i + 1) % groups) for i in range(groups)])
-    vmem = pl.BlockSpec(memory_space=pltpu.VMEM)
-    table = pl.pallas_call(
-        join_kernel,
-        in_specs=[pl.BlockSpec(memory_space=pltpu.SMEM), vmem, vmem],
-        out_specs=vmem,
-        out_shape=shape(groups, GROUP, TILES * ROWS, L, BF16),
-        compiler_params=PARAMS,
-        name="table_join",
-    )(lax.axis_index("xh").reshape(1).astype(jnp.int32), own_half, other_half)
-    table = table.reshape(OWNERS, TILES * ROWS, L)
     gain = lax.dynamic_slice(norm_gain, (block_index * WIDE,), (WIDE,)).reshape(WIDE, 1)
 
     batch_spec = pl.BlockSpec((STEP, WIDE + INFO, L), lambda i: (i, 0, 0))
@@ -336,13 +317,17 @@
     sums_spec = pl.BlockSpec((GROUP, 2, STEP * TOK), lambda i: (0, 0, i))
     tokens = GROUP * TOK
 
-    memory, sums_send = pl.pallas_call(
+    vmem = pl.BlockSpec(memory_space=pltpu.VMEM)
+    hbm = pl.BlockSpec(memory_space=pl.ANY)
+    memory, sums_send, placed = pl.pallas_call(
         forward_kernel,
-        grid=(steps,),
-        in_specs=[batch_spec, table_spec, whole(WIDE, 1)],
-        out_specs=[wide_spec, sums_spec],
-        out_shape=(shape(WIDE, tokens, F32), shape(GROUP, 2, tokens, F32)),
-        scratch_shapes=[pltpu.VMEM((WIDE, TABLE), BF16)],
+        in_specs=[vmem] * 3,
+        out_specs=[vmem] * 3,
+        out_shape=(
+            shape(WIDE, tokens, F32),
+            shape(GROUP, 2, tokens, F32),
+            shape(TABLE, tokens, BF16),
+        ),
         compiler_params=PARAMS,
         name="forward",
     )(batch, table, gain)
@@ -350,18 +335,21 @@
 
     out_turned, memory_grad, grad_send = pl.pallas_call(
         backward_kernel,
-        grid=(steps,),
-        in_specs=[batch_spec, whole(WIDE, 1), wide_spec, sums_spec],
-        out_specs=[wide_spec, wide_spec, whole(OWNERS, GRAD, L)],
+        in_specs=[vmem] * 5,
+        out_specs=[hbm, hbm, pl.BlockSpec()],
         out_shape=(
             in_hbm(WIDE, tokens, BF16),
             in_hbm(WIDE, tokens, BF16),
             in_hbm(OWNERS, GRAD, L, BF16),
         ),
-        scratch_shapes=[pltpu.VMEM((TABLE, WIDE), F32), pltpu.VMEM((WIDE, L), F32)],
+        scratch_shapes=[
+            pltpu.VMEM((WIDE, tokens), BF16),
+            pltpu.VMEM((WIDE, tokens), BF16),
+            pltpu.SemaphoreType.DMA((2,)),
+        ],
         compiler_params=PARAMS,
         name="backward",
-    )(batch, gain, memory, sums)
+    )(batch, gain, memory, sums, placed)
     plane_parts = exchange(grad_send, PLANE)
 
     back_send = pl.pallas_call(

time: 157 us -> 154 us (0.981)
  waiting for transfers between devices: 26.8 us -> 30.4 us
  starting transfers between devices: 28.3 us -> 25.2 us
  local copies, waits for them, and re-layouts: 6.43 us -> 4.32 us
    all_to_all x4, waiting for transfers between devices: 6.89 us -> 30.4 us  [exchange(): return lax.all_to_all(array, axes, split_axis=0, concat_axis=0, tiled=True)]
    ppermute x1 -> x0, waiting for transfers between devices: 20 us -> none  [per_device(): lax.ppermute(own_half, 'xh', [(i, (i + 1) % groups) for i in range(groups)])]
    ppermute x1 -> x0, starting transfers between devices: 6.67 us -> none  [per_device(): lax.ppermute(own_half, 'xh', [(i, (i + 1) % groups) for i in range(groups)])]
    all_to_all x4, starting transfers between devices: 21.6 us -> 25.2 us  [exchange(): return lax.all_to_all(array, axes, split_axis=0, concat_axis=0, tiled=True)]
    unnamed x22 -> x20, local copies, waits for them, and re-layouts: 5.53 us -> 3.42 us
    pallas_call x4 -> x3, Pallas kernels: 7.92 us -> 6.77 us  [the longest x1 3.71 us: per_device(): pl.pallas_call(backward_kernel, in_specs=[vmem] * 5, out_specs=[hbm, hbm,...]
  transfers between devices with their start and end apart: 5 -> 4, of which waited for: 3 -> 3; matrix products, arithmetic and copies ran while one was open for 1% -> 1% of each run, Pallas kernels for 3% -> 3%
where the time goes in v7:
time: 154 us; the launch traced here: 152 us
  blocking collectives  76.8 us (50%)
  waiting for transfers between devices  30.4 us (20%)
  starting transfers between devices  25.2 us (16%)
  Pallas kernels  14.7 us (10%)
  local copies, waits for them, and re-layouts  4.32 us (3%)
    all_to_all x2, blocking collectives, exchange(): return lax.all_to_all(array, axes, split_axis=0, concat_axis=0, tiled=True)  45.1 us
    all_gather x1, blocking collectives, per_device(): totals = lax.all_gather(total, 'dp', axis=0, tiled=False)  31.7 us
    all_to_all x4, waiting for transfers between devices, exchange(): return lax.all_to_all(array, axes, split_axis=0, concat_axis=0, tiled=True)  30.4 us
    all_to_all x4, starting transfers between devices, exchange(): return lax.all_to_all(array, axes, split_axis=0, concat_axis=0, tiled=True)  25.2 us
    pallas_call x1, Pallas kernels, per_device(): pl.pallas_call(backward_kernel, in_specs=[vmem] * 5, out_specs=[hbm, hbm,...  3.71 us
    unnamed x20, local copies, waits for them, and re-layouts  3.42 us
  transfers between devices with their start and end apart: 4, of which 3 were waited for; matrix products, arithmetic and copies ran while one was open for 1% of the time, Pallas kernels for 3%

profile of v7, /device:TPU:6, one launch (start us, length us, event | category | flops | bytes accessed | tf_op | source)
XLA Modules:
  0.0 152.2 jit_solution(18356354348694606305)
XLA Ops:
  0.6 0.0 copy-start
  0.6 0.9 copy-done
  1.6 0.0 copy-start.2
  1.6 0.0 copy-start.7
  1.6 0.0 copy-start.8
  1.6 0.0 copy-start.9
  1.6 0.9 table_send.1
  2.5 9.6 %all-to-all-start.1 = ((bf16[32,64,128]{2,1,0:T(8,128)(2,1)}), bf16[32,64,128]{2,1,0:T(8,128)(2,1)S(1)}, u32[]{:S(2)}, u32[]{:S(2)}) async-start(bf16[32,64,128]{2,1,0:T(8,128)(2,1)} %bitcast.15), calls=%async_computation.1 | async-start | bytes 1048576 | tf_op jit(solution)/shard_map/all_to_all | solution.py:269
  12.0 0.0 copy-done.2
  12.0 0.0 copy-done.7
  12.0 0.0 copy-done.8
  12.1 0.0 copy-done.9
  12.1 2.2 %pack.1 = (bf16[16,360,128]{2,1,0:T(8,128)(2,1)}, f32[32,128]{1,0:T(8,128)S(1)}) custom-call(s32[3,128]{1,0:T(4,128)S(1)} %bitcast.14, s32[32,128]{1,0:T(8,128)S(1)} %bitcast.11, f32[32,128]{1,0:T(8,128)S(1)} %bitcast.13, bf16[128,4096]{1,0:T(8,128)(2,1)S(1)} %copy-done.2), custom_call_target="tpu_custom_call" | custom-call | tf_op jit(solution)/shard_map/pack/pallas_call | solution.py:296
  14.3 7.1 %all-to-all-done.1.table_ref = bf16[32,64,128]{2,1,0:T(8,128)(2,1)S(1)} async-done(((bf16[32,64,128]{2,1,0:T(8,128)(2,1)}), bf16[32,64,128]{2,1,0:T(8,128)(2,1)S(1)}, u32[]{:S(2)}, u32[]{:S(2)}) %all-to-all-start.1) | async-done | bytes 524320 | tf_op jit(solution)/shard_map/all_to_all | solution.py:269
  21.3 4.5 %all-to-all-start = ((bf16[16,360,128]{2,1,0:T(8,128)(2,1)}), bf16[16,360,128]{2,1,0:T(8,128)(2,1)S(1)}, u32[]{:S(2)}, u32[]{:S(2)}) async-start(bf16[16,360,128]{2,1,0:T(8,128)(2,1)} %get-tuple-element.24), calls=%async_computation | async-start | bytes 2949120 | tf_op jit(solution)/shard_map/all_to_all | solution.py:269
  25.9 0.8 dynamic_slice.3
  26.6 0.1 copy.15.gain_ref
  26.8 18.9 %all-to-all-done.batch_ref = bf16[16,360,128]{2,1,0:T(8,128)(2,1)S(1)} async-done(((bf16[16,360,128]{2,1,0:T(8,128)(2,1)}), bf16[16,360,128]{2,1,0:T(8,128)(2,1)S(1)}, u32[]{:S(2)}, u32[]{:S(2)}) %all-to-all-start) | async-done | bytes 1474592 | tf_op jit(solution)/shard_map/all_to_all | solution.py:269
  45.7 2.2 %forward.1 = (f32[256,2048]{1,0:T(8,128)S(1)}, f32[16,2,2048]{2,1,0:T(2,128)S(1)}, bf16[1024,2048]{1,0:T(8,128)(2,1)S(1)}) custom-call(bf16[16,360,128]{2,1,0:T(8,128)(2,1)S(1)} %all-to-all-done.batch_ref, bf16[32,64,128]{2,1,0:T(8,128)(2,1)S(1)} %all-to-all-done.1.table_ref, f32[256,1]{1,0:T(8,128)S(1)} %copy.15.gain_ref), custom_call_target="tpu_custom_call" | custom-call | tf_op jit(solution)/shard_map/forward/pallas_call | solution.py:322
  47.9 11.9 %all_to_all.30.sums_ref = f32[16,2,2048]{2,1,0:T(2,128)S(1)} all-to-all(f32[16,2,2048]{2,1,0:T(2,128)S(1)} %get-tuple-element.26), channel_id=1, replica_groups=mesh['dp'=16,'xh'=2,'xl'=2,'yc'=8] {'xl','yc'}, dimensions={0} | all-to-all | bytes 524288 | tf_op jit(solution)/shard_map/all_to_all | solution.py:269
  59.8 3.7 %backward.1 = (bf16[256,2048]{1,0:T(8,128)(2,1)}, bf16[256,2048]{1,0:T(8,128)(2,1)}, bf16[32,72,128]{2,1,0:T(8,128)(2,1)}) custom-call(bf16[16,360,128]{2,1,0:T(8,128)(2,1)S(1)} %all-to-all-done.batch_ref, f32[256,1]{1,0:T(8,128)S(1)} %copy.15.gain_ref, f32[256,2048]{1,0:T(8,128)S(1)} %get-tuple-element.25.memory_ref, ...), custom_call_target="tpu_custom_call" | custom-call | tf_op jit(solution)/shard_map/backward/pallas_call | solution.py:336
  63.5 6.2 %all-to-all-start.3 = ((bf16[32,72,128]{2,1,0:T(8,128)(2,1)}), bf16[32,72,128]{2,1,0:T(8,128)(2,1)S(1)}, u32[]{:S(2)}, u32[]{:S(2)}) async-start(bf16[32,72,128]{2,1,0:T(8,128)(2,1)} %get-tuple-element.28), calls=%async_computation.3 | async-start | bytes 1179648 | tf_op jit(solution)/shard_map/all_to_all | solution.py:269
  69.7 0.0 copy-start.3
  69.7 1.2 copy-done.3
  70.9 0.0 copy-start.4
  70.9 1.2 copy-done.4
  72.1 3.0 %placed_grad.1 = bf16[16,352,128]{2,1,0:T(8,128)(2,1)} custom-call(bf16[16,360,128]{2,1,0:T(8,128)(2,1)S(1)} %all-to-all-done.batch_ref, bf16[32,64,128]{2,1,0:T(8,128)(2,1)S(1)} %all-to-all-done.1.table_ref, bf16[256,2048]{1,0:T(8,128)(2,1)S(1)} %copy-done.3, bf16[256,2048]{1,0:T(8,128)(2,1)S(1)} %copy-done.4), custom_call_target="tpu_custom_call" | custom-call | tf_op jit(solution)/shard_map/placed_grad/pallas_call | solution.py:355
  75.2 4.5 %all-to-all-done.3 = bf16[32,72,128]{2,1,0:T(8,128)(2,1)S(1)} async-done(((bf16[32,72,128]{2,1,0:T(8,128)(2,1)}), bf16[32,72,128]{2,1,0:T(8,128)(2,1)S(1)}, u32[]{:S(2)}, u32[]{:S(2)}) %all-to-all-start.3) | async-done | bytes 589856 | tf_op jit(solution)/shard_map/all_to_all | solution.py:269
  79.6 0.1 plane_sum.1
  79.7 33.2 %all_to_all.31.parts_ref = bf16[16,72,128]{2,1,0:T(8,128)(2,1)S(1)} all-to-all(bf16[16,72,128]{2,1,0:T(8,128)(2,1)S(1)} %plane_sum.1), channel_id=1, replica_groups=mesh['dp'=16,'xh'=2,'xl'=2,'yc'=8] {'dp'}, dimensions={0} | all-to-all | bytes 589824 | tf_op jit(solution)/shard_map/all_to_all | solution.py:269
  112.9 0.0 copy-start.1
  112.9 0.0 copy-start.5
  112.9 0.0 copy-start.6
  113.0 4.9 %all-to-all-start.5 = ((bf16[16,352,128]{2,1,0:T(8,128)(2,1)}), bf16[16,352,128]{2,1,0:T(8,128)(2,1)S(1)}, u32[]{:S(2)}, u32[]{:S(2)}) async-start(bf16[16,352,128]{2,1,0:T(8,128)(2,1)} %placed_grad.1), calls=%async_computation.5 | async-start | bytes 2883584 | tf_op jit(solution)/shard_map/all_to_all | solution.py:269
  117.9 31.7 %all-gather = bf16[1152,128]{1,0:T(8,128)(2,1)S(1)} all-gather(bf16[72,128]{1,0:T(8,128)(2,1)S(1)} %share_sum.1), channel_id=2, replica_groups=mesh['dp'=16,'xh'=2,'xl'=2,'yc'=8] {'dp'}, dimensions={0}, use_global_device_ids=true | all-gather | bytes 313344 | tf_op jit(solution)/shard_map/all_gather | solution.py:380
  149.6 0.0 all-to-all-done.5.parts_ref
  149.6 0.0 copy-done.1
  149.6 0.0 copy-done.5
  149.6 0.0 copy-done.6
  149.6 2.5 %last.1 = (bf16[128,4096]{1,0:T(8,128)(2,1)}, f32[32,128]{1,0:T(8,128)}, bf16[32,4096]{1,0:T(8,128)(2,1)}, f32[32,4096]{1,0:T(8,128)}, f32[32,4096]{1,0:T(8,128)}, /*index=5*/f32[1,4096]{1,0:T(1,128)}) custom-call(bf16[16,352,128]{2,1,0:T(8,128)(2,1)S(1)} %all-to-all-done.5.parts_ref, s32[32,128]{1,0:T(8,128)S(1)} %bitcast.12, ...), custom_call_target="tpu_custom_call" | custom-call | tf_op jit(solution)/shard_map/last/pallas_call | solution.py:384
  (1 shorter events, 0.0 us)
Async XLA Ops:
  0.6 1.0 copy-start
  1.6 10.4 %copy-start.2 = (bf16[128,4096]{1,0:T(8,128)(2,1)S(1)}, bf16[128,4096]{1,0:T(8,128)(2,1)}, u32[]{:S(2)}) copy-start(bf16[128,4096]{1,0:T(8,128)(2,1)} %cotangent_ref.1) | copy-start | bytes 3145732
  1.6 10.4 %copy-start.7 = (s32[128,32]{0,1:T(8,128)S(1)}, s32[128,32]{0,1:T(8,128)}, u32[]{:S(2)}) copy-start(s32[128,32]{0,1:T(8,128)} %param.9) | copy-start | bytes 49156
  1.6 10.5 %copy-start.8 = (f32[128,32]{0,1:T(8,128)S(1)}, f32[128,32]{0,1:T(8,128)}, u32[]{:S(2)}) copy-start(f32[128,32]{0,1:T(8,128)} %param.10) | copy-start | bytes 49156
  1.6 10.5 %copy-start.9 = (s32[128,3]{0,1:T(4,128)S(1)}, s32[128,3]{0,1:T(4,128)}, u32[]{:S(2)}) copy-start(s32[128,3]{0,1:T(4,128)} %param.8) | copy-start | bytes 4612
  2.5 18.9 %all-to-all-start.1 = ((bf16[32,64,128]{2,1,0:T(8,128)(2,1)}), bf16[32,64,128]{2,1,0:T(8,128)(2,1)S(1)}, u32[]{:S(2)}, u32[]{:S(2)}) async-start(bf16[32,64,128]{2,1,0:T(8,128)(2,1)} %bitcast.15), calls=%async_computation.1 | async-start | bytes 1048576 | tf_op jit(solution)/shard_map/all_to_all | solution.py:269
  21.3 24.4 %all-to-all-start = ((bf16[16,360,128]{2,1,0:T(8,128)(2,1)}), bf16[16,360,128]{2,1,0:T(8,128)(2,1)S(1)}, u32[]{:S(2)}, u32[]{:S(2)}) async-start(bf16[16,360,128]{2,1,0:T(8,128)(2,1)} %get-tuple-element.24), calls=%async_computation | async-start | bytes 2949120 | tf_op jit(solution)/shard_map/all_to_all | solution.py:269
  63.5 16.1 %all-to-all-start.3 = ((bf16[32,72,128]{2,1,0:T(8,128)(2,1)}), bf16[32,72,128]{2,1,0:T(8,128)(2,1)S(1)}, u32[]{:S(2)}, u32[]{:S(2)}) async-start(bf16[32,72,128]{2,1,0:T(8,128)(2,1)} %get-tuple-element.28), calls=%async_computation.3 | async-start | bytes 1179648 | tf_op jit(solution)/shard_map/all_to_all | solution.py:269
  69.7 1.2 copy-start.3
  70.9 1.2 copy-start.4
  112.9 36.7 %copy-start.1 = (bf16[32,4096]{1,0:T(8,128)(2,1)S(1)}, bf16[32,4096]{1,0:T(8,128)(2,1)}, u32[]{:S(2)}) copy-start(bf16[32,4096]{1,0:T(8,128)(2,1)} %table_ref.3) | copy-start | bytes 786436
  112.9 36.7 %copy-start.5 = (f32[32,4096]{1,0:T(8,128)S(1)}, f32[32,4096]{1,0:T(8,128)}, u32[]{:S(2)}) copy-start(f32[32,4096]{1,0:T(8,128)} %first_ref.1) | copy-start | bytes 1572868
  112.9 36.7 %copy-start.6 = (f32[32,4096]{1,0:T(8,128)S(1)}, f32[32,4096]{1,0:T(8,128)}, u32[]{:S(2)}) copy-start(f32[32,4096]{1,0:T(8,128)} %second_ref.1) | copy-start | bytes 1572868
  113.0 36.6 %all-to-all-start.5 = ((bf16[16,352,128]{2,1,0:T(8,128)(2,1)}), bf16[16,352,128]{2,1,0:T(8,128)(2,1)S(1)}, u32[]{:S(2)}, u32[]{:S(2)}) async-start(bf16[16,352,128]{2,1,0:T(8,128)(2,1)} %placed_grad.1), calls=%async_computation.5 | async-start | bytes 2883584 | tf_op jit(solution)/shard_map/all_to_all | solution.py:269

commit v8 on v7

--- a/solution.py
+++ b/solution.py
@@ -36,6 +36,7 @@
 BACK = WIDE + SLOTS
 STEP = 4
 MANY = 4
+LAST = 8
 PLANE = ("xh", "xl", "yc")
 TEAM = ("xl", "yc")
 VMEM_LIMIT = 32 * 1024 * 1024
@@ -56,13 +57,22 @@
     return pltpu.HBM(dims_and_type[:-1], dims_and_type[-1])
 
 
-def table_kernel(table_ref, out_ref):
-    for b in range(GROUP):
-        for j in range(TILES):
-            at = b * WIDE + j * L
-            tile = table_ref[:, at : at + L]
-            for x in range(out_ref.shape[0]):
-                out_ref[x, b, j * ROWS : (j + 1) * ROWS, :] = tile
+def table_kernel(table_ref, out_ref, sems):
+    copies = []
+    for x in range(out_ref.shape[0]):
+        for b in range(GROUP):
+            for j in range(TILES):
+                source = table_ref.at[:, pl.ds(b * WIDE + j * L, L)]
+                target = out_ref.at[x, b, pl.ds(j * ROWS, ROWS), :]
+                copies.append(pltpu.make_async_copy(source, target, sems.at[len(copies)]))
+    for copy in copies:
+        copy.start()
+    for copy in copies:
+        copy.wait()
+
+
+def turn_kernel(table_ref, out_ref):
+    out_ref[...] = jnp.transpose(load_table(table_ref))
 
 
 def pack_kernel(owners_ref, pick_ref, scores_ref, cotangent_ref, send_ref, weights_ref, info_ref):
@@ -120,8 +130,8 @@
     return jnp.concatenate([batch_ref[first + i, :WIDE, :] for i in range(STEP)], axis=1).astype(F32)
 
 
-def forward_kernel(batch_ref, table_ref, gain_ref, memory_ref, sums_ref, placed_ref):
-    turned = jnp.transpose(load_table(table_ref))
+def forward_kernel(batch_ref, turned_ref, gain_ref, memory_ref, sums_ref, placed_ref):
+    turned = turned_ref[...]
     gain = gain_ref[...]
     for first in range(0, GROUP, STEP):
         at = slice(first * TOK, (first + STEP) * TOK)
@@ -232,11 +242,11 @@
 
 def out_kernel(parts_ref, pick_ref, weights_ref, out_ref, score_ref, placed_grad_ref):
     step = pl.program_id(0)
-    for b in range(MANY):
+    for b in range(LAST):
         for j in range(TILES):
             at = b * WIDE + j * L
             out_ref[:, at : at + L] = jnp.transpose(parts_ref[b, j * L : (j + 1) * L, :])
-    part = sum(parts_ref[b, WIDE:, :].astype(F32) for b in range(MANY))
+    part = sum(parts_ref[b, WIDE:, :].astype(F32) for b in range(LAST))
 
     @pl.when(step == 0)
     def _():
@@ -287,10 +297,13 @@
 
     table_send = pl.pallas_call(
         table_kernel,
+        in_specs=[pl.BlockSpec(memory_space=pltpu.HBM)],
+        out_specs=pl.BlockSpec(memory_space=pltpu.HBM),
         out_shape=in_hbm(groups, GROUP, TILES * ROWS, L, BF16),
+        scratch_shapes=[pltpu.SemaphoreType.DMA((groups * GROUP * TILES,))],
         compiler_params=PARAMS,
         name="table_send",
-    )(value_table)
+    )(pltpu.with_memory_space_constraint(value_table, pltpu.HBM))
     table = exchange(table_send.reshape(OWNERS, TILES * ROWS, L), PLANE)
 
     batch_send, weights = pl.pallas_call(
@@ -319,6 +332,14 @@
 
     vmem = pl.BlockSpec(memory_space=pltpu.VMEM)
     hbm = pl.BlockSpec(memory_space=pl.ANY)
+    turned = pl.pallas_call(
+        turn_kernel,
+        in_specs=[vmem],
+        out_specs=vmem,
+        out_shape=shape(WIDE, TABLE, BF16),
+        compiler_params=PARAMS,
+        name="turn",
+    )(table)
     memory, sums_send, placed = pl.pallas_call(
         forward_kernel,
         in_specs=[vmem] * 3,
@@ -330,7 +351,7 @@
         ),
         compiler_params=PARAMS,
         name="forward",
-    )(batch, table, gain)
+    )(batch, turned, gain)
     sums = exchange(sums_send, TEAM)
 
     out_turned, memory_grad, grad_send = pl.pallas_call(
@@ -380,26 +401,26 @@
     totals = lax.all_gather(total, "dp", axis=0, tiled=False)
 
     back = exchange(back_send, TEAM)
-    rows_spec = pl.BlockSpec((ROWS, MANY * WIDE), lambda i: (0, i))
+    rows_spec = pl.BlockSpec((ROWS, LAST * WIDE), lambda i: (0, i))
     memory_out, score_turned, new_table, new_first, new_second, gain_gradient = pl.pallas_call(
         last_kernel,
-        grid=(GROUP // MANY,),
+        grid=(GROUP // LAST,),
         in_specs=[
-            pl.BlockSpec((MANY, BACK, L), lambda i: (i, 0, 0)),
+            pl.BlockSpec((LAST, BACK, L), lambda i: (i, 0, 0)),
             whole(PICKS, TOK),
             whole(PICKS, TOK),
-            pl.BlockSpec((MANY, GRAD, L), lambda i: (i, 0, 0)),
+            pl.BlockSpec((LAST, GRAD, L), lambda i: (i, 0, 0)),
             rows_spec,
             rows_spec,
             rows_spec,
         ],
         out_specs=[
-            pl.BlockSpec((TOK, MANY * WIDE), lambda i: (0, i)),
+            pl.BlockSpec((TOK, LAST * WIDE), lambda i: (0, i)),
             whole(PICKS, TOK),
             rows_spec,
             rows_spec,
             rows_spec,
-            pl.BlockSpec((1, MANY * WIDE), lambda i: (0, i)),
+            pl.BlockSpec((1, LAST * WIDE), lambda i: (0, i)),
         ],
         out_shape=(
             shape(TOK, D, BF16),

time: 154 us -> 169 us (1.097)
  Pallas kernels: 14.7 us -> 31.2 us
    pallas_call x2 -> x3, Pallas kernels: 3.41 us -> 19.9 us  [the longest x1 17.6 us: per_device(): pl.pallas_call(table_kernel, in_specs=[pl.BlockSpec(memory_space=pltpu.HB...]
    unnamed x20 -> x18, local copies, waits for them, and re-layouts: 3.42 us -> 2.48 us
where the time goes in v8:
time: 169 us; the launch traced here: 168 us
  blocking collectives  76.8 us (45%)
  Pallas kernels  31.2 us (18%)
  waiting for transfers between devices  30.2 us (18%)
  starting transfers between devices  25.2 us (15%)
  local copies, waits for them, and re-layouts  3.37 us (2%)
    all_to_all x2, blocking collectives, exchange(): return lax.all_to_all(array, axes, split_axis=0, concat_axis=0, tiled=True)  45 us
    all_gather x1, blocking collectives, per_device(): totals = lax.all_gather(total, 'dp', axis=0, tiled=False)  31.7 us
    all_to_all x4, waiting for transfers between devices, exchange(): return lax.all_to_all(array, axes, split_axis=0, concat_axis=0, tiled=True)  30.2 us
    all_to_all x4, starting transfers between devices, exchange(): return lax.all_to_all(array, axes, split_axis=0, concat_axis=0, tiled=True)  25.2 us
    pallas_call x1, Pallas kernels, per_device(): pl.pallas_call(table_kernel, in_specs=[pl.BlockSpec(memory_space=pltpu.HB...  17.6 us
    pallas_call x1, Pallas kernels, per_device(): pl.pallas_call(backward_kernel, in_specs=[vmem] * 5, out_specs=[hbm, hbm,...  3.73 us
  transfers between devices with their start and end apart: 4, of which 3 were waited for; matrix products, arithmetic and copies ran while one was open for 1% of the time, Pallas kernels for 3%

profile of v8, /device:TPU:6, one launch (start us, length us, event | category | flops | bytes accessed | tf_op | source)
XLA Modules:
  0.0 167.5 jit_solution(11498415911947346739)
XLA Ops:
  0.6 0.0 copy-start.1
  0.6 0.0 copy-start.7
  0.7 0.0 copy-start.6
  0.7 0.0 copy-start.8
  0.7 17.6 %table_send.1 = bf16[2,16,64,128]{3,2,1,0:T(8,128)(2,1)} custom-call(bf16[32,4096]{1,0:T(8,128)(2,1)} %table_ref.3), custom_call_target="tpu_custom_call" | custom-call | tf_op jit(solution)/shard_map/table_send/pallas_call | solution.py:298
  18.3 9.6 %all-to-all-start.1 = ((bf16[32,64,128]{2,1,0:T(8,128)(2,1)}), bf16[32,64,128]{2,1,0:T(8,128)(2,1)S(1)}, u32[]{:S(2)}, u32[]{:S(2)}) async-start(bf16[32,64,128]{2,1,0:T(8,128)(2,1)} %bitcast.15), calls=%async_computation.1 | async-start | bytes 1048576 | tf_op jit(solution)/shard_map/all_to_all | solution.py:279
  27.8 0.0 copy-done.1
  27.8 0.0 copy-done.7
  27.8 0.0 copy-done.6
  27.9 0.0 copy-done.8
  27.9 2.2 %pack.1 = (bf16[16,360,128]{2,1,0:T(8,128)(2,1)}, f32[32,128]{1,0:T(8,128)S(1)}) custom-call(s32[3,128]{1,0:T(4,128)S(1)} %bitcast.14, s32[32,128]{1,0:T(8,128)S(1)} %bitcast.11, f32[32,128]{1,0:T(8,128)S(1)} %bitcast.13, bf16[128,4096]{1,0:T(8,128)(2,1)S(1)} %copy-done.1), custom_call_target="tpu_custom_call" | custom-call | tf_op jit(solution)/shard_map/pack/pallas_call | solution.py:309
  30.1 7.1 %all-to-all-done.1.table_ref = bf16[32,64,128]{2,1,0:T(8,128)(2,1)S(1)} async-done(((bf16[32,64,128]{2,1,0:T(8,128)(2,1)}), bf16[32,64,128]{2,1,0:T(8,128)(2,1)S(1)}, u32[]{:S(2)}, u32[]{:S(2)}) %all-to-all-start.1) | async-done | bytes 524320 | tf_op jit(solution)/shard_map/all_to_all | solution.py:279
  37.1 4.5 %all-to-all-start = ((bf16[16,360,128]{2,1,0:T(8,128)(2,1)}), bf16[16,360,128]{2,1,0:T(8,128)(2,1)S(1)}, u32[]{:S(2)}, u32[]{:S(2)}) async-start(bf16[16,360,128]{2,1,0:T(8,128)(2,1)} %get-tuple-element.24), calls=%async_computation | async-start | bytes 2949120 | tf_op jit(solution)/shard_map/all_to_all | solution.py:279
  41.7 0.8 dynamic_slice.3
  42.4 0.1 copy.15.gain_ref
  42.6 0.2 turn.1.turned_ref
  42.8 18.7 %all-to-all-done.batch_ref = bf16[16,360,128]{2,1,0:T(8,128)(2,1)S(1)} async-done(((bf16[16,360,128]{2,1,0:T(8,128)(2,1)}), bf16[16,360,128]{2,1,0:T(8,128)(2,1)S(1)}, u32[]{:S(2)}, u32[]{:S(2)}) %all-to-all-start) | async-done | bytes 1474592 | tf_op jit(solution)/shard_map/all_to_all | solution.py:279
  61.5 2.1 %forward.1 = (f32[256,2048]{1,0:T(8,128)S(1)}, f32[16,2,2048]{2,1,0:T(2,128)S(1)}, bf16[1024,2048]{1,0:T(8,128)(2,1)S(1)}) custom-call(bf16[16,360,128]{2,1,0:T(8,128)(2,1)S(1)} %all-to-all-done.batch_ref, bf16[256,1024]{1,0:T(8,128)(2,1)S(1)} %turn.1.turned_ref, f32[256,1]{1,0:T(8,128)S(1)} %copy.15.gain_ref), custom_call_target="tpu_custom_call" | custom-call | tf_op jit(solution)/shard_map/forward/pallas_call | solution.py:343
  63.7 11.9 %all_to_all.30.sums_ref = f32[16,2,2048]{2,1,0:T(2,128)S(1)} all-to-all(f32[16,2,2048]{2,1,0:T(2,128)S(1)} %get-tuple-element.26), channel_id=1, replica_groups=mesh['dp'=16,'xh'=2,'xl'=2,'yc'=8] {'xl','yc'}, dimensions={0} | all-to-all | bytes 524288 | tf_op jit(solution)/shard_map/all_to_all | solution.py:279
  75.5 3.7 %backward.1 = (bf16[256,2048]{1,0:T(8,128)(2,1)}, bf16[256,2048]{1,0:T(8,128)(2,1)}, bf16[32,72,128]{2,1,0:T(8,128)(2,1)}) custom-call(bf16[16,360,128]{2,1,0:T(8,128)(2,1)S(1)} %all-to-all-done.batch_ref, f32[256,1]{1,0:T(8,128)S(1)} %copy.15.gain_ref, f32[256,2048]{1,0:T(8,128)S(1)} %get-tuple-element.25.memory_ref, ...), custom_call_target="tpu_custom_call" | custom-call | tf_op jit(solution)/shard_map/backward/pallas_call | solution.py:357
  79.3 6.1 %all-to-all-start.3 = ((bf16[32,72,128]{2,1,0:T(8,128)(2,1)}), bf16[32,72,128]{2,1,0:T(8,128)(2,1)S(1)}, u32[]{:S(2)}, u32[]{:S(2)}) async-start(bf16[32,72,128]{2,1,0:T(8,128)(2,1)} %get-tuple-element.28), calls=%async_computation.3 | async-start | bytes 1179648 | tf_op jit(solution)/shard_map/all_to_all | solution.py:279
  85.4 0.0 copy-start.2
  85.4 1.2 copy-done.2
  86.7 0.0 copy-start.3
  86.7 1.2 copy-done.3
  87.9 3.0 %placed_grad.1 = bf16[16,352,128]{2,1,0:T(8,128)(2,1)} custom-call(bf16[16,360,128]{2,1,0:T(8,128)(2,1)S(1)} %all-to-all-done.batch_ref, bf16[32,64,128]{2,1,0:T(8,128)(2,1)S(1)} %all-to-all-done.1.table_ref, bf16[256,2048]{1,0:T(8,128)(2,1)S(1)} %copy-done.2, bf16[256,2048]{1,0:T(8,128)(2,1)S(1)} %copy-done.3), custom_call_target="tpu_custom_call" | custom-call | tf_op jit(solution)/shard_map/placed_grad/pallas_call | solution.py:376
  90.9 4.4 %all-to-all-done.3 = bf16[32,72,128]{2,1,0:T(8,128)(2,1)S(1)} async-done(((bf16[32,72,128]{2,1,0:T(8,128)(2,1)}), bf16[32,72,128]{2,1,0:T(8,128)(2,1)S(1)}, u32[]{:S(2)}, u32[]{:S(2)}) %all-to-all-start.3) | async-done | bytes 589856 | tf_op jit(solution)/shard_map/all_to_all | solution.py:279
  95.4 0.1 plane_sum.1
  95.5 33.2 %all_to_all.31.parts_ref = bf16[16,72,128]{2,1,0:T(8,128)(2,1)S(1)} all-to-all(bf16[16,72,128]{2,1,0:T(8,128)(2,1)S(1)} %plane_sum.1), channel_id=1, replica_groups=mesh['dp'=16,'xh'=2,'xl'=2,'yc'=8] {'dp'}, dimensions={0} | all-to-all | bytes 589824 | tf_op jit(solution)/shard_map/all_to_all | solution.py:279
  128.7 0.0 copy-start
  128.7 0.0 copy-start.4
  128.7 0.0 copy-start.5
  128.7 4.9 %all-to-all-start.5 = ((bf16[16,352,128]{2,1,0:T(8,128)(2,1)}), bf16[16,352,128]{2,1,0:T(8,128)(2,1)S(1)}, u32[]{:S(2)}, u32[]{:S(2)}) async-start(bf16[16,352,128]{2,1,0:T(8,128)(2,1)} %placed_grad.1), calls=%async_computation.5 | async-start | bytes 2883584 | tf_op jit(solution)/shard_map/all_to_all | solution.py:279
  133.6 31.7 %all-gather = bf16[1152,128]{1,0:T(8,128)(2,1)S(1)} all-gather(bf16[72,128]{1,0:T(8,128)(2,1)S(1)} %share_sum.1), channel_id=2, replica_groups=mesh['dp'=16,'xh'=2,'xl'=2,'yc'=8] {'dp'}, dimensions={0}, use_global_device_ids=true | all-gather | bytes 313344 | tf_op jit(solution)/shard_map/all_gather | solution.py:401
  165.3 0.0 all-to-all-done.5.parts_ref
  165.4 0.0 copy-done
  165.4 0.0 copy-done.4
  165.4 0.0 copy-done.5
  165.4 2.1 %last.1 = (bf16[128,4096]{1,0:T(8,128)(2,1)}, f32[32,128]{1,0:T(8,128)}, bf16[32,4096]{1,0:T(8,128)(2,1)}, f32[32,4096]{1,0:T(8,128)}, f32[32,4096]{1,0:T(8,128)}, /*index=5*/f32[1,4096]{1,0:T(1,128)}) custom-call(bf16[16,352,128]{2,1,0:T(8,128)(2,1)S(1)} %all-to-all-done.5.parts_ref, s32[32,128]{1,0:T(8,128)S(1)} %bitcast.12, ...), custom_call_target="tpu_custom_call" | custom-call | tf_op jit(solution)/shard_map/last/pallas_call | solution.py:405
  (1 shorter events, 0.0 us)
Async XLA Ops:
  0.6 27.2 %copy-start.1 = (bf16[128,4096]{1,0:T(8,128)(2,1)S(1)}, bf16[128,4096]{1,0:T(8,128)(2,1)}, u32[]{:S(2)}) copy-start(bf16[128,4096]{1,0:T(8,128)(2,1)} %cotangent_ref.1) | copy-start | bytes 3145732
  0.6 27.2 %copy-start.7 = (f32[128,32]{0,1:T(8,128)S(1)}, f32[128,32]{0,1:T(8,128)}, u32[]{:S(2)}) copy-start(f32[128,32]{0,1:T(8,128)} %param.10) | copy-start | bytes 49156
  0.7 27.2 %copy-start.6 = (s32[128,32]{0,1:T(8,128)S(1)}, s32[128,32]{0,1:T(8,128)}, u32[]{:S(2)}) copy-start(s32[128,32]{0,1:T(8,128)} %param.9) | copy-start | bytes 49156
  0.7 27.2 %copy-start.8 = (s32[128,3]{0,1:T(4,128)S(1)}, s32[128,3]{0,1:T(4,128)}, u32[]{:S(2)}) copy-start(s32[128,3]{0,1:T(4,128)} %param.8) | copy-start | bytes 4612
  18.3 18.9 %all-to-all-start.1 = ((bf16[32,64,128]{2,1,0:T(8,128)(2,1)}), bf16[32,64,128]{2,1,0:T(8,128)(2,1)S(1)}, u32[]{:S(2)}, u32[]{:S(2)}) async-start(bf16[32,64,128]{2,1,0:T(8,128)(2,1)} %bitcast.15), calls=%async_computation.1 | async-start | bytes 1048576 | tf_op jit(solution)/shard_map/all_to_all | solution.py:279
  37.1 24.4 %all-to-all-start = ((bf16[16,360,128]{2,1,0:T(8,128)(2,1)}), bf16[16,360,128]{2,1,0:T(8,128)(2,1)S(1)}, u32[]{:S(2)}, u32[]{:S(2)}) async-start(bf16[16,360,128]{2,1,0:T(8,128)(2,1)} %get-tuple-element.24), calls=%async_computation | async-start | bytes 2949120 | tf_op jit(solution)/shard_map/all_to_all | solution.py:279
  79.3 16.1 %all-to-all-start.3 = ((bf16[32,72,128]{2,1,0:T(8,128)(2,1)}), bf16[32,72,128]{2,1,0:T(8,128)(2,1)S(1)}, u32[]{:S(2)}, u32[]{:S(2)}) async-start(bf16[32,72,128]{2,1,0:T(8,128)(2,1)} %get-tuple-element.28), calls=%async_computation.3 | async-start | bytes 1179648 | tf_op jit(solution)/shard_map/all_to_all | solution.py:279
  85.4 1.2 copy-start.2
  86.7 1.2 copy-start.3
  128.7 36.7 %copy-start = (bf16[32,4096]{1,0:T(8,128)(2,1)S(1)}, bf16[32,4096]{1,0:T(8,128)(2,1)}, u32[]{:S(2)}) copy-start(bf16[32,4096]{1,0:T(8,128)(2,1)} %table_ref.3) | copy-start | bytes 786436
  128.7 36.7 %copy-start.4 = (f32[32,4096]{1,0:T(8,128)S(1)}, f32[32,4096]{1,0:T(8,128)}, u32[]{:S(2)}) copy-start(f32[32,4096]{1,0:T(8,128)} %first_ref.1) | copy-start | bytes 1572868
  128.7 36.7 %copy-start.5 = (f32[32,4096]{1,0:T(8,128)S(1)}, f32[32,4096]{1,0:T(8,128)}, u32[]{:S(2)}) copy-start(f32[32,4096]{1,0:T(8,128)} %second_ref.1) | copy-start | bytes 1572868
  128.7 36.6 %all-to-all-start.5 = ((bf16[16,352,128]{2,1,0:T(8,128)(2,1)}), bf16[16,352,128]{2,1,0:T(8,128)(2,1)S(1)}, u32[]{:S(2)}, u32[]{:S(2)}) async-start(bf16[16,352,128]{2,1,0:T(8,128)(2,1)} %placed_grad.1), calls=%async_computation.5 | async-start | bytes 2883584 | tf_op jit(solution)/shard_map/all_to_all | solution.py:279

commit v9 on v8

--- a/solution.py
+++ b/solution.py
@@ -57,18 +57,13 @@
     return pltpu.HBM(dims_and_type[:-1], dims_and_type[-1])
 
 
-def table_kernel(table_ref, out_ref, sems):
-    copies = []
-    for x in range(out_ref.shape[0]):
-        for b in range(GROUP):
-            for j in range(TILES):
-                source = table_ref.at[:, pl.ds(b * WIDE + j * L, L)]
-                target = out_ref.at[x, b, pl.ds(j * ROWS, ROWS), :]
-                copies.append(pltpu.make_async_copy(source, target, sems.at[len(copies)]))
-    for copy in copies:
-        copy.start()
-    for copy in copies:
-        copy.wait()
+def table_kernel(table_ref, out_ref):
+    for b in range(GROUP):
+        for j in range(TILES):
+            at = b * WIDE + j * L
+            tile = table_ref[:, at : at + L]
+            for x in range(out_ref.shape[0]):
+                out_ref[x, b, j * ROWS : (j + 1) * ROWS, :] = tile
 
 
 def turn_kernel(table_ref, out_ref):
@@ -297,13 +292,10 @@
 
     table_send = pl.pallas_call(
         table_kernel,
-        in_specs=[pl.BlockSpec(memory_space=pltpu.HBM)],
-        out_specs=pl.BlockSpec(memory_space=pltpu.HBM),
         out_shape=in_hbm(groups, GROUP, TILES * ROWS, L, BF16),
-        scratch_shapes=[pltpu.SemaphoreType.DMA((groups * GROUP * TILES,))],
         compiler_params=PARAMS,
         name="table_send",
-    )(pltpu.with_memory_space_constraint(value_table, pltpu.HBM))
+    )(value_table)
     table = exchange(table_send.reshape(OWNERS, TILES * ROWS, L), PLANE)
 
     batch_send, weights = pl.pallas_call(

time: 169 us -> 154 us (0.911)
  Pallas kernels: 31.2 us -> 14.4 us
    pallas_call x1, Pallas kernels: 17.6 us -> 0.86 us  [per_device(): pl.pallas_call(table_kernel, out_shape=in_hbm(groups, GROUP, TILES * ROWS...]
    unnamed x18 -> x20, local copies, waits for them, and re-layouts: 2.48 us -> 3.42 us
  transfers between devices with their start and end apart: 4 -> 4, of which waited for: 3 -> 3; matrix products, arithmetic and copies ran while one was open for 1% -> 1% of each run, Pallas kernels for 3% -> 4%
where the time goes in v9:
time: 154 us; the launch traced here: 152 us
  blocking collectives  76.8 us (50%)
  waiting for transfers between devices  30.2 us (20%)
  starting transfers between devices  25.1 us (16%)
  Pallas kernels  14.4 us (9%)
  local copies, waits for them, and re-layouts  4.32 us (3%)
    all_to_all x2, blocking collectives, exchange(): return lax.all_to_all(array, axes, split_axis=0, concat_axis=0, tiled=True)  45.1 us
    all_gather x1, blocking collectives, per_device(): totals = lax.all_gather(total, 'dp', axis=0, tiled=False)  31.7 us
    all_to_all x4, waiting for transfers between devices, exchange(): return lax.all_to_all(array, axes, split_axis=0, concat_axis=0, tiled=True)  30.2 us
    all_to_all x4, starting transfers between devices, exchange(): return lax.all_to_all(array, axes, split_axis=0, concat_axis=0, tiled=True)  25.1 us
    pallas_call x1, Pallas kernels, per_device(): pl.pallas_call(backward_kernel, in_specs=[vmem] * 5, out_specs=[hbm, hbm,...  3.72 us
    unnamed x20, local copies, waits for them, and re-layouts  3.42 us
  transfers between devices with their start and end apart: 4, of which 3 were waited for; matrix products, arithmetic and copies ran while one was open for 1% of the time, Pallas kernels for 4%

profile of v9, /device:TPU:6, one launch (start us, length us, event | category | flops | bytes accessed | tf_op | source)
XLA Modules:
  0.0 151.7 jit_solution(5055620281102805621)
XLA Ops:
  0.6 0.0 copy-start
  0.6 0.9 copy-done
  1.6 0.0 copy-start.2
  1.6 0.0 copy-start.7
  1.6 0.0 copy-start.8
  1.6 0.0 copy-start.9
  1.6 0.9 table_send.1
  2.5 9.6 %all-to-all-start.1 = ((bf16[32,64,128]{2,1,0:T(8,128)(2,1)}), bf16[32,64,128]{2,1,0:T(8,128)(2,1)S(1)}, u32[]{:S(2)}, u32[]{:S(2)}) async-start(bf16[32,64,128]{2,1,0:T(8,128)(2,1)} %bitcast.15), calls=%async_computation.1 | async-start | bytes 1048576 | tf_op jit(solution)/shard_map/all_to_all | solution.py:274
  12.0 0.0 copy-done.2
  12.0 0.0 copy-done.7
  12.0 0.0 copy-done.8
  12.1 0.0 copy-done.9
  12.1 2.2 %pack.1 = (bf16[16,360,128]{2,1,0:T(8,128)(2,1)}, f32[32,128]{1,0:T(8,128)S(1)}) custom-call(s32[3,128]{1,0:T(4,128)S(1)} %bitcast.14, s32[32,128]{1,0:T(8,128)S(1)} %bitcast.11, f32[32,128]{1,0:T(8,128)S(1)} %bitcast.13, bf16[128,4096]{1,0:T(8,128)(2,1)S(1)} %copy-done.2), custom_call_target="tpu_custom_call" | custom-call | tf_op jit(solution)/shard_map/pack/pallas_call | solution.py:301
  14.3 7.1 %all-to-all-done.1.table_ref = bf16[32,64,128]{2,1,0:T(8,128)(2,1)S(1)} async-done(((bf16[32,64,128]{2,1,0:T(8,128)(2,1)}), bf16[32,64,128]{2,1,0:T(8,128)(2,1)S(1)}, u32[]{:S(2)}, u32[]{:S(2)}) %all-to-all-start.1) | async-done | bytes 524320 | tf_op jit(solution)/shard_map/all_to_all | solution.py:274
  21.3 4.5 %all-to-all-start = ((bf16[16,360,128]{2,1,0:T(8,128)(2,1)}), bf16[16,360,128]{2,1,0:T(8,128)(2,1)S(1)}, u32[]{:S(2)}, u32[]{:S(2)}) async-start(bf16[16,360,128]{2,1,0:T(8,128)(2,1)} %get-tuple-element.24), calls=%async_computation | async-start | bytes 2949120 | tf_op jit(solution)/shard_map/all_to_all | solution.py:274
  25.9 0.8 dynamic_slice.3
  26.6 0.1 copy.15.gain_ref
  26.8 0.2 turn.1.turned_ref
  27.0 18.7 %all-to-all-done.batch_ref = bf16[16,360,128]{2,1,0:T(8,128)(2,1)S(1)} async-done(((bf16[16,360,128]{2,1,0:T(8,128)(2,1)}), bf16[16,360,128]{2,1,0:T(8,128)(2,1)S(1)}, u32[]{:S(2)}, u32[]{:S(2)}) %all-to-all-start) | async-done | bytes 1474592 | tf_op jit(solution)/shard_map/all_to_all | solution.py:274
  45.7 2.1 %forward.1 = (f32[256,2048]{1,0:T(8,128)S(1)}, f32[16,2,2048]{2,1,0:T(2,128)S(1)}, bf16[1024,2048]{1,0:T(8,128)(2,1)S(1)}) custom-call(bf16[16,360,128]{2,1,0:T(8,128)(2,1)S(1)} %all-to-all-done.batch_ref, bf16[256,1024]{1,0:T(8,128)(2,1)S(1)} %turn.1.turned_ref, f32[256,1]{1,0:T(8,128)S(1)} %copy.15.gain_ref), custom_call_target="tpu_custom_call" | custom-call | tf_op jit(solution)/shard_map/forward/pallas_call | solution.py:335
  47.8 11.9 %all_to_all.30.sums_ref = f32[16,2,2048]{2,1,0:T(2,128)S(1)} all-to-all(f32[16,2,2048]{2,1,0:T(2,128)S(1)} %get-tuple-element.26), channel_id=1, replica_groups=mesh['dp'=16,'xh'=2,'xl'=2,'yc'=8] {'xl','yc'}, dimensions={0} | all-to-all | bytes 524288 | tf_op jit(solution)/shard_map/all_to_all | solution.py:274
  59.7 3.7 %backward.1 = (bf16[256,2048]{1,0:T(8,128)(2,1)}, bf16[256,2048]{1,0:T(8,128)(2,1)}, bf16[32,72,128]{2,1,0:T(8,128)(2,1)}) custom-call(bf16[16,360,128]{2,1,0:T(8,128)(2,1)S(1)} %all-to-all-done.batch_ref, f32[256,1]{1,0:T(8,128)S(1)} %copy.15.gain_ref, f32[256,2048]{1,0:T(8,128)S(1)} %get-tuple-element.25.memory_ref, ...), custom_call_target="tpu_custom_call" | custom-call | tf_op jit(solution)/shard_map/backward/pallas_call | solution.py:349
  63.5 6.1 %all-to-all-start.3 = ((bf16[32,72,128]{2,1,0:T(8,128)(2,1)}), bf16[32,72,128]{2,1,0:T(8,128)(2,1)S(1)}, u32[]{:S(2)}, u32[]{:S(2)}) async-start(bf16[32,72,128]{2,1,0:T(8,128)(2,1)} %get-tuple-element.28), calls=%async_computation.3 | async-start | bytes 1179648 | tf_op jit(solution)/shard_map/all_to_all | solution.py:274
  69.6 0.0 copy-start.3
  69.6 1.2 copy-done.3
  70.8 0.0 copy-start.4
  70.9 1.2 copy-done.4
  72.1 3.0 %placed_grad.1 = bf16[16,352,128]{2,1,0:T(8,128)(2,1)} custom-call(bf16[16,360,128]{2,1,0:T(8,128)(2,1)S(1)} %all-to-all-done.batch_ref, bf16[32,64,128]{2,1,0:T(8,128)(2,1)S(1)} %all-to-all-done.1.table_ref, bf16[256,2048]{1,0:T(8,128)(2,1)S(1)} %copy-done.3, bf16[256,2048]{1,0:T(8,128)(2,1)S(1)} %copy-done.4), custom_call_target="tpu_custom_call" | custom-call | tf_op jit(solution)/shard_map/placed_grad/pallas_call | solution.py:368
  75.1 4.5 %all-to-all-done.3 = bf16[32,72,128]{2,1,0:T(8,128)(2,1)S(1)} async-done(((bf16[32,72,128]{2,1,0:T(8,128)(2,1)}), bf16[32,72,128]{2,1,0:T(8,128)(2,1)S(1)}, u32[]{:S(2)}, u32[]{:S(2)}) %all-to-all-start.3) | async-done | bytes 589856 | tf_op jit(solution)/shard_map/all_to_all | solution.py:274
  79.6 0.1 plane_sum.1
  79.6 33.2 %all_to_all.31.parts_ref = bf16[16,72,128]{2,1,0:T(8,128)(2,1)S(1)} all-to-all(bf16[16,72,128]{2,1,0:T(8,128)(2,1)S(1)} %plane_sum.1), channel_id=1, replica_groups=mesh['dp'=16,'xh'=2,'xl'=2,'yc'=8] {'dp'}, dimensions={0} | all-to-all | bytes 589824 | tf_op jit(solution)/shard_map/all_to_all | solution.py:274
  112.9 0.0 copy-start.1
  112.9 0.0 copy-start.5
  112.9 0.0 copy-start.6
  112.9 4.9 %all-to-all-start.5 = ((bf16[16,352,128]{2,1,0:T(8,128)(2,1)}), bf16[16,352,128]{2,1,0:T(8,128)(2,1)S(1)}, u32[]{:S(2)}, u32[]{:S(2)}) async-start(bf16[16,352,128]{2,1,0:T(8,128)(2,1)} %placed_grad.1), calls=%async_computation.5 | async-start | bytes 2883584 | tf_op jit(solution)/shard_map/all_to_all | solution.py:274
  117.8 31.7 %all-gather = bf16[1152,128]{1,0:T(8,128)(2,1)S(1)} all-gather(bf16[72,128]{1,0:T(8,128)(2,1)S(1)} %share_sum.1), channel_id=2, replica_groups=mesh['dp'=16,'xh'=2,'xl'=2,'yc'=8] {'dp'}, dimensions={0}, use_global_device_ids=true | all-gather | bytes 313344 | tf_op jit(solution)/shard_map/all_gather | solution.py:393
  149.5 0.0 all-to-all-done.5.parts_ref
  149.5 0.0 copy-done.1
  149.5 0.0 copy-done.5
  149.5 0.0 copy-done.6
  149.6 2.1 %last.1 = (bf16[128,4096]{1,0:T(8,128)(2,1)}, f32[32,128]{1,0:T(8,128)}, bf16[32,4096]{1,0:T(8,128)(2,1)}, f32[32,4096]{1,0:T(8,128)}, f32[32,4096]{1,0:T(8,128)}, /*index=5*/f32[1,4096]{1,0:T(1,128)}) custom-call(bf16[16,352,128]{2,1,0:T(8,128)(2,1)S(1)} %all-to-all-done.5.parts_ref, s32[32,128]{1,0:T(8,128)S(1)} %bitcast.12, ...), custom_call_target="tpu_custom_call" | custom-call | tf_op jit(solution)/shard_map/last/pallas_call | solution.py:397
  (1 shorter events, 0.0 us)
Async XLA Ops:
  0.6 1.0 copy-start
  1.6 10.4 %copy-start.2 = (bf16[128,4096]{1,0:T(8,128)(2,1)S(1)}, bf16[128,4096]{1,0:T(8,128)(2,1)}, u32[]{:S(2)}) copy-start(bf16[128,4096]{1,0:T(8,128)(2,1)} %cotangent_ref.1) | copy-start | bytes 3145732
  1.6 10.4 %copy-start.7 = (s32[128,32]{0,1:T(8,128)S(1)}, s32[128,32]{0,1:T(8,128)}, u32[]{:S(2)}) copy-start(s32[128,32]{0,1:T(8,128)} %param.9) | copy-start | bytes 49156
  1.6 10.5 %copy-start.8 = (f32[128,32]{0,1:T(8,128)S(1)}, f32[128,32]{0,1:T(8,128)}, u32[]{:S(2)}) copy-start(f32[128,32]{0,1:T(8,128)} %param.10) | copy-start | bytes 49156
  1.6 10.5 %copy-start.9 = (s32[128,3]{0,1:T(4,128)S(1)}, s32[128,3]{0,1:T(4,128)}, u32[]{:S(2)}) copy-start(s32[128,3]{0,1:T(4,128)} %param.8) | copy-start | bytes 4612
  2.5 18.9 %all-to-all-start.1 = ((bf16[32,64,128]{2,1,0:T(8,128)(2,1)}), bf16[32,64,128]{2,1,0:T(8,128)(2,1)S(1)}, u32[]{:S(2)}, u32[]{:S(2)}) async-start(bf16[32,64,128]{2,1,0:T(8,128)(2,1)} %bitcast.15), calls=%async_computation.1 | async-start | bytes 1048576 | tf_op jit(solution)/shard_map/all_to_all | solution.py:274
  21.3 24.4 %all-to-all-start = ((bf16[16,360,128]{2,1,0:T(8,128)(2,1)}), bf16[16,360,128]{2,1,0:T(8,128)(2,1)S(1)}, u32[]{:S(2)}, u32[]{:S(2)}) async-start(bf16[16,360,128]{2,1,0:T(8,128)(2,1)} %get-tuple-element.24), calls=%async_computation | async-start | bytes 2949120 | tf_op jit(solution)/shard_map/all_to_all | solution.py:274
  63.5 16.1 %all-to-all-start.3 = ((bf16[32,72,128]{2,1,0:T(8,128)(2,1)}), bf16[32,72,128]{2,1,0:T(8,128)(2,1)S(1)}, u32[]{:S(2)}, u32[]{:S(2)}) async-start(bf16[32,72,128]{2,1,0:T(8,128)(2,1)} %get-tuple-element.28), calls=%async_computation.3 | async-start | bytes 1179648 | tf_op jit(solution)/shard_map/all_to_all | solution.py:274
  69.6 1.2 copy-start.3
  70.8 1.2 copy-start.4
  112.9 36.7 %copy-start.1 = (bf16[32,4096]{1,0:T(8,128)(2,1)S(1)}, bf16[32,4096]{1,0:T(8,128)(2,1)}, u32[]{:S(2)}) copy-start(bf16[32,4096]{1,0:T(8,128)(2,1)} %table_ref.3) | copy-start | bytes 786436
  112.9 36.7 %copy-start.5 = (f32[32,4096]{1,0:T(8,128)S(1)}, f32[32,4096]{1,0:T(8,128)}, u32[]{:S(2)}) copy-start(f32[32,4096]{1,0:T(8,128)} %first_ref.1) | copy-start | bytes 1572868
  112.9 36.7 %copy-start.6 = (f32[32,4096]{1,0:T(8,128)S(1)}, f32[32,4096]{1,0:T(8,128)}, u32[]{:S(2)}) copy-start(f32[32,4096]{1,0:T(8,128)} %second_ref.1) | copy-start | bytes 1572868
  112.9 36.6 %all-to-all-start.5 = ((bf16[16,352,128]{2,1,0:T(8,128)(2,1)}), bf16[16,352,128]{2,1,0:T(8,128)(2,1)S(1)}, u32[]{:S(2)}, u32[]{:S(2)}) async-start(bf16[16,352,128]{2,1,0:T(8,128)(2,1)} %placed_grad.1), calls=%async_computation.5 | async-start | bytes 2883584 | tf_op jit(solution)/shard_map/all_to_all | solution.py:274
